TPU v7x, 512 devices: a whole 4x8x8 slice. The times are simulated.
512 devices in a mesh: dp: 4 (over x), ctx: 32 (over y_lo, z), tp: 4 (over y_hi, core).
Axes of the slice: x: 4, y: 8 (y_hi: 2, y_lo: 4; y = y_hi * 4 + y_lo), z: 8, core: 2. Of those that a mesh axis runs over, the one named last changes fastest.
Arguments:
- queries: bfloat16 [4, 4096, 4096], P('dp', 'ctx', 'tp'), may hold values from -156 to 156
- keys: bfloat16 [4, 4096, 512], P('dp', 'ctx', 'tp'), may hold values from -6 to 6
- values: bfloat16 [4, 4096, 512], P('dp', 'ctx', 'tp'), may hold values from -6 to 6
- out_grad: bfloat16 [4, 4096, 4096], P('dp', 'ctx', 'tp'), may hold values from -6 to 6
- normed_input: bfloat16 [4, 4096, 8192], P('dp', 'ctx', 'tp'), may hold values from -6 to 6
- doc_lengths: int32 [4, 8], P('dp'), may hold values from 1 to 2048, 4096 in all within a row
- span_order: int32 [32], replicated, may hold values from 0 to 31, each once
Outputs:
- query_grad: bfloat16 [4, 4096, 4096], P('dp', 'ctx', 'tp')
- key_grad: bfloat16 [4, 4096, 512], P('dp', 'ctx', 'tp')
- value_grad: bfloat16 [4, 4096, 512], P('dp', 'ctx', 'tp')
- key_weight_grad: float32 [8192, 512], P('ctx', 'tp')
- value_weight_grad: float32 [8192, 512], P('ctx', 'tp')
Inputs may be any that keep to these rules, and one draw needn't show every extreme that they name: `doc_lengths`: each row sums to 4096; the longest document of each row has exactly 2048 positions. `span_order`: each value once.
All inputs are finite; a program needn't handle non-finite values.
Results may differ from a plain program's by a relative error of at most 0.0095.
Values may be sent and summed in bfloat16 or wider, within the bound.
No kernel may reach another device: no remote copies, remote signals or barrier semaphores. Data moves between devices by JAX's collectives and lax.ppermute only.
A program may use at most 64 MiB of HBM per device.

v0:
```python
import jax
import jax.numpy as jnp
from jax import lax
from jax.sharding import PartitionSpec as P

HEAD_WIDTH = 128


def shifted(array, axis, by):
    devices = lax.axis_size(axis)
    return lax.ppermute(array, axis, [(i, (i + by) % devices) for i in range(devices)])


def stored_positions(order, owners, height):
    count = order.shape[0]
    half_rows = height // 2
    within = jnp.arange(height, dtype=jnp.int32)
    matches = owners[:, None] == jnp.arange(count, dtype=jnp.int32)[None, :]
    first = jnp.sum(jnp.where(matches, order[None, :], 0), axis=1)[:, None]
    blocks = jnp.where(within[None, :] < half_rows, first, 2 * count - 1 - first)
    return (blocks * half_rows + within[None, :] % half_rows).reshape(-1)


def document_ids(positions, boundary):
    return jnp.sum((boundary[None, :] <= positions[:, None]).astype(jnp.int32), axis=1)


def contract_last(left, right):
    return lax.dot_general(
        left, right, (((1,), (1,)), ((), ())), preferred_element_type=jnp.float32
    )


def contract_first(left, right):
    return lax.dot_general(
        left, right, (((0,), (0,)), ((), ())), preferred_element_type=jnp.float32
    )


def rotate_keys(key_pair):
    return shifted(key_pair, "ctx", 1)


def rotate_grads(grad_pair):
    return shifted(grad_pair, "ctx", 1)


def collect_grads(own_rounded):
    return lax.all_gather(own_rounded, "ctx", axis=0, tiled=True)


def shards(queries, keys, values, out_grad, normed_input, doc_lengths, span_order):
    height = queries.shape[1]
    group_size = queries.shape[2] // HEAD_WIDTH
    factor = HEAD_WIDTH ** (-0.5)
    context = lax.axis_size("ctx")
    my_index = jnp.reshape(lax.axis_index("ctx"), (1,))
    query_rows = queries[0].reshape(height * group_size, HEAD_WIDTH)
    grad_rows = out_grad[0].reshape(height * group_size, HEAD_WIDTH)
    boundary = jnp.cumsum(doc_lengths[0])
    my_positions = stored_positions(span_order, my_index, height)
    my_documents = document_ids(my_positions, boundary)
    row_positions = jnp.repeat(my_positions, group_size)
    row_documents = jnp.repeat(my_documents, group_size)
    local_pair = jnp.concatenate([keys[0], values[0]], axis=1)

    def allowed(key_positions, key_documents):
        return (key_positions[None, :] <= row_positions[:, None]) & (
            key_documents[None, :] == row_documents[:, None]
        )

    def is_live(key_positions):
        return jnp.min(key_positions) <= jnp.max(my_positions)

    def stats_tile(state, key_pair, key_positions, key_documents):

        def stats_compute(carry):
            row_max, summed, weighted = carry
            mask = allowed(key_positions, key_documents)
            scores = jnp.where(
                mask, contract_last(query_rows, key_pair[:, :HEAD_WIDTH]) * factor, -1e30
            )
            new_max = jnp.maximum(row_max, jnp.max(scores, axis=1))
            probabilities = jnp.where(mask, jnp.exp(scores - new_max[:, None]), 0.0)
            prob_grad = contract_last(grad_rows, key_pair[:, HEAD_WIDTH:])
            retain = jnp.exp(row_max - new_max)
            return (
                new_max,
                retain * summed + jnp.sum(probabilities, axis=1),
                retain * weighted + jnp.sum(probabilities * prob_grad, axis=1),
            )

        return lax.cond(is_live(key_positions), stats_compute, lambda carry: carry, state)

    def grad_tile(query_total, key_pair, key_positions, key_documents, log_norm, row_drift):

        def grad_compute(running):
            mask = allowed(key_positions, key_documents)
            scores = contract_last(query_rows, key_pair[:, :HEAD_WIDTH]) * factor
            probabilities = jnp.where(mask, jnp.exp(scores - log_norm[:, None]), 0.0)
            prob_grad = contract_last(grad_rows, key_pair[:, HEAD_WIDTH:])
            score_grad = (probabilities * (prob_grad - row_drift[:, None])).astype(jnp.bfloat16)
            prob_rounded = probabilities.astype(jnp.bfloat16)
            running = running + jnp.dot(
                score_grad, key_pair[:, :HEAD_WIDTH], preferred_element_type=jnp.float32
            )
            key_part = contract_first(score_grad, query_rows) * factor
            value_part = contract_first(prob_rounded, grad_rows)
            return (running, jnp.concatenate([key_part, value_part], axis=1))

        def leave(running):
            return (running, jnp.zeros((key_pair.shape[0], 2 * HEAD_WIDTH), jnp.float32))

        return lax.cond(is_live(key_positions), grad_compute, leave, query_total)

    width_rows = height * group_size
    start_stats = (
        jnp.full((width_rows,), -1e30, jnp.float32),
        jnp.zeros((width_rows,), jnp.float32),
        jnp.zeros((width_rows,), jnp.float32),
    )
    query_start = jnp.zeros((width_rows, HEAD_WIDTH), jnp.float32)

    def key_info(step_number):
        owner = jnp.reshape((my_index[0] - step_number) % context, (1,))
        key_positions = stored_positions(span_order, owner, height)
        return (key_positions, document_ids(key_positions, boundary))

    first_stats = stats_tile(start_stats, local_pair, my_positions, my_documents)
    kept_start = jnp.zeros((context, height, 2 * HEAD_WIDTH), jnp.bfloat16)
    kept_start = lax.dynamic_update_index_in_dim(kept_start, local_pair, 0, 0)

    def stats_step(step_number, carry):
        key_pair = rotate_keys(carry[0])
        key_positions, key_documents = key_info(step_number)
        kept = lax.dynamic_update_index_in_dim(carry[2], key_pair, step_number, 0)
        return (key_pair, stats_tile(carry[1], key_pair, key_positions, key_documents), kept)

    stats_state = lax.fori_loop(1, context, stats_step, (local_pair, first_stats, kept_start))
    final_stats = stats_state[1]
    kept_pairs = stats_state[2]
    log_norm = final_stats[0] + jnp.log(final_stats[1])
    row_drift = final_stats[2] / final_stats[1]
    query_total, travelling = grad_tile(
        query_start, local_pair, my_positions, my_documents, log_norm, row_drift
    )

    def grad_step(step_number, carry):
        key_pair = lax.dynamic_index_in_dim(kept_pairs, step_number, 0, keepdims=False)
        moved_grads = rotate_grads(carry[0])
        key_positions, key_documents = key_info(step_number)
        new_total, terms = grad_tile(
            carry[1], key_pair, key_positions, key_documents, log_norm, row_drift
        )
        return (moved_grads + terms, new_total)

    loop_state = lax.fori_loop(1, context, grad_step, (travelling, query_total))
    query_total = loop_state[1]
    own_grads = rotate_grads(loop_state[0])
    own_rounded = own_grads.astype(jnp.bfloat16)
    all_grads = collect_grads(own_rounded)
    features = lax.all_gather(normed_input[0], "tp", axis=1, tiled=True)
    columns = lax.all_to_all(features, "ctx", split_axis=1, concat_axis=0, tiled=True)
    weight_part = contract_first(columns, all_grads)
    weight_total = lax.psum(weight_part, "dp")
    query_grad = (
        (query_total * factor).astype(jnp.bfloat16).reshape(1, height, group_size * HEAD_WIDTH)
    )
    key_grad = own_rounded[:, :HEAD_WIDTH].reshape(1, height, HEAD_WIDTH)
    value_grad = own_rounded[:, HEAD_WIDTH:].reshape(1, height, HEAD_WIDTH)
    return (
        query_grad,
        key_grad,
        value_grad,
        weight_total[:, :HEAD_WIDTH],
        weight_total[:, HEAD_WIDTH:],
    )


def solution(mesh):
    in_specs = (
        P("dp", "ctx", "tp"),
        P("dp", "ctx", "tp"),
        P("dp", "ctx", "tp"),
        P("dp", "ctx", "tp"),
        P("dp", "ctx", "tp"),
        P("dp", None),
        P(),
    )
    out_specs = (
        P("dp", "ctx", "tp"),
        P("dp", "ctx", "tp"),
        P("dp", "ctx", "tp"),
        P("ctx", "tp"),
        P("ctx", "tp"),
    )
    return jax.shard_map(shards, mesh=mesh, in_specs=in_specs, out_specs=out_specs, check_vma=False)
```

profile of v0, /device:TPU:1, one launch (start us, length us, event | category | flops | bytes accessed | tf_op | source)
XLA Modules:
  0.0 1086.1 jit_solution(4451572780697770838)
XLA Ops:
  20.9 405.3 %while.48 = (s32[]{:T(128)}, bf16[128,256]{1,0:T(8,128)(2,1)S(1)}, f32[1024]{0:T(1024)}, f32[1024]{0:T(1024)S(1)}, f32[1024]{0:T(1024)S(1)}, /*index=5*/bf16[32,...) while((s32[]{:T(128)}, bf16[128,256]{1,0:T(8,128)(2,1)S(1)}, ...), condition=%wide.region_19.20_spmd.clone, body=%wide.region_10.19_spmd.clone.sunk | while | flops 69608688 | bytes 2826494 | solution.py:139
  20.9 4.8 collective-permute-start
  30.3 6.9 collective-permute-done
  47.3 5.1 collective-permute-done
  52.4 3.7 conditional.10
  91.5 3.7 conditional.10
  104.2 3.7 conditional.10
  116.9 3.7 conditional.10
  142.2 3.7 conditional.10
  154.9 3.7 conditional.10
  167.6 3.7 conditional.10
  180.4 3.7 conditional.10
  218.9 3.7 conditional.10
  231.5 3.7 conditional.10
  244.2 3.7 conditional.10
  269.6 3.7 conditional.10
  430.0 368.3 %while.49 = (s32[]{:T(128)}, f32[128,256]{0,1:T(8,128)S(1)}, f32[1024,128]{1,0:T(8,128)S(1)}, s32[]{:T(128)}, s32[32]{0:T(128)}, /*index=5*/s32[]{:T(128)}, s32[...) while((s32[]{:T(128)}, f32[128,256]{0,1:T(8,128)S(1)}, ...), condition=%wide.region_28.29_spmd.clone, body=%wide.region_22.28_spmd.clone.sunk | while | flops 169302256 | bytes 6052046 | solution.py:157
  437.1 3.8 conditional.11
  448.1 3.8 conditional.11
  459.0 3.8 conditional.11
  470.0 3.8 conditional.11
  481.0 3.8 conditional.11
  492.0 3.8 conditional.11
  502.9 3.8 conditional.11
  513.9 3.8 conditional.11
  524.9 3.8 conditional.11
  535.9 3.8 conditional.11
  546.8 3.8 conditional.11
  557.8 3.8 conditional.11
  568.8 3.8 conditional.11
  579.7 3.8 conditional.11
  590.7 3.8 conditional.11
  601.7 3.8 conditional.11
  612.7 3.8 conditional.11
  623.6 3.8 conditional.11
  634.6 3.8 conditional.11
  645.8 3.8 conditional.11
  649.7 4.4 collective-permute-start.1
  659.2 3.8 conditional.11
  663.1 4.4 collective-permute-start.1
  672.7 3.8 conditional.11
  676.6 4.4 collective-permute-start.1
  686.1 3.8 conditional.11
  690.0 4.4 collective-permute-start.1
  699.6 3.8 conditional.11
  703.4 4.4 collective-permute-start.1
  713.0 3.8 conditional.11
  716.9 5.2 collective-permute-start.1
  727.2 3.8 conditional.11
  731.1 4.4 collective-permute-start.1
  740.7 3.8 conditional.11
  744.5 4.4 collective-permute-start.1
  754.1 3.8 conditional.11
  758.0 4.4 collective-permute-start.1
  767.6 3.8 conditional.11
  771.4 4.4 collective-permute-start.1
  781.0 3.8 conditional.11
  784.9 4.4 collective-permute-start.1
  794.4 3.8 conditional.11
  798.4 4.4 collective-permute-start.2
  802.8 4.6 all-to-all-start
  808.9 31.1 %all-to-all-done = bf16[128,32,256]{0,2,1:T(8,128)(2,1)S(1)} async-done(((bf16[128,32,256]{0,2,1:T(8,128)(2,1)}), bf16[128,32,256]{0,2,1:T(8,128)(2,1)S(1)}, u32[]{:S(2)}, u32[]{:S(2)}) %all-to-all-start) | async-done | bytes 2097184 | tf_op jit(solution)/shard_map/all_to_all | solution.py:163
  843.0 162.3 %all-gather.4.cloned.1.call-done = bf16[4096,256]{1,0:T(8,128)(2,1)} async-done(((bf16[128,256]{1,0:T(8,128)(2,1)}), bf16[4096,256]{1,0:T(8,128)(2,1)}) %all-gather.4.cloned.1.call-update) | async-done | bytes 2097168 | tf_op jit(solution)/shard_map/all_gather | solution.py:49
  1010.5 65.6 %all-reduce.3.cloned.1.call-done = f32[256,256]{0,1:T(8,128)} async-done(((f32[256,256]{0,1:T(8,128)}), f32[256,256]{0,1:T(8,128)}) %all-reduce.3.cloned.1.call-update) | async-done | bytes 262160 | tf_op jit(solution)/shard_map/psum | solution.py:165
  (1302 shorter events, 687.1 us)
Async XLA Ops:
  8.0 794.8 %all-gather.6.cloned.1.call-start = ((), (), s32[]{:S(2)}) async-start(), calls=%async_computation.3 | async-start | bytes 2621440 | tf_op jit(solution)/shard_map/all_gather | solution.py:162
  20.9 16.2 %collective-permute-start = (bf16[128,256]{1,0:T(8,128)(2,1)S(1)}, bf16[128,256]{1,0:T(8,128)(2,1)S(1)}, u32[]{:S(2)}, u32[]{:S(2)}) collective-permute-start(bf16[128,256]{1,0:T(8,128)(2,1)S(1)} %get-tuple-element.1657), channel_id=1, source_target_pairs={{0,4},{4,8},{8,12},{12,16},{16,20},{20,24},{24,28},{28,32},{32,36}... | collective-permute-start | bytes 196616 | tf_op jit(solution)/shard_map/while/body/eval_jaxpr/ppermute | solution.py:11
  40.9 11.5 %collective-permute-start = (bf16[128,256]{1,0:T(8,128)(2,1)S(1)}, bf16[128,256]{1,0:T(8,128)(2,1)S(1)}, u32[]{:S(2)}, u32[]{:S(2)}) collective-permute-start(bf16[128,256]{1,0:T(8,128)(2,1)S(1)} %get-tuple-element.1657), channel_id=1, source_target_pairs={{0,4},{4,8},{8,12},{12,16},{16,20},{20,24},{24,28},{28,32},{32,36}... | collective-permute-start | bytes 196616 | tf_op jit(solution)/shard_map/while/body/eval_jaxpr/ppermute | solution.py:11
  56.1 10.0 collective-permute-start
  69.9 8.9 collective-permute-start
  82.6 8.9 collective-permute-start
  95.3 8.9 collective-permute-start
  107.9 8.9 collective-permute-start
  120.6 8.9 collective-permute-start
  133.3 8.9 collective-permute-start
  146.0 8.9 collective-permute-start
  158.7 8.9 collective-permute-start
  171.4 9.0 collective-permute-start
  184.2 9.3 collective-permute-start
  197.3 8.9 collective-permute-start
  209.9 8.9 collective-permute-start
  222.6 8.9 collective-permute-start
  235.3 8.9 collective-permute-start
  248.0 8.9 collective-permute-start
  260.7 8.9 collective-permute-start
  273.3 8.9 collective-permute-start
  286.0 8.9 collective-permute-start
  298.7 8.9 collective-permute-start
  311.4 8.9 collective-permute-start
  324.1 8.9 collective-permute-start
  336.7 9.7 collective-permute-start
  350.2 8.9 collective-permute-start
  362.9 8.9 collective-permute-start
  375.6 8.9 collective-permute-start
  430.0 10.9 %collective-permute-start.1 = (f32[128,256]{0,1:T(8,128)S(1)}, f32[128,256]{0,1:T(8,128)S(1)}, u32[]{:S(2)}, u32[]{:S(2)}) collective-permute-start(f32[128,256]{0,1:T(8,128)S(1)} %get-tuple-element.1720), channel_id=1, source_target_pairs={{0,4},{4,8},{8,12},{12,16},{16,20},{20,24},{24,28},{28,32},{32,36}... | collective-permute-start | bytes 393224 | tf_op jit(solution)/shard_map/while/body/eval_jaxpr/ppermute | solution.py:11
  441.0 10.9 %collective-permute-start.1 = (f32[128,256]{0,1:T(8,128)S(1)}, f32[128,256]{0,1:T(8,128)S(1)}, u32[]{:S(2)}, u32[]{:S(2)}) collective-permute-start(f32[128,256]{0,1:T(8,128)S(1)} %get-tuple-element.1720), channel_id=1, source_target_pairs={{0,4},{4,8},{8,12},{12,16},{16,20},{20,24},{24,28},{28,32},{32,36}... | collective-permute-start | bytes 393224 | tf_op jit(solution)/shard_map/while/body/eval_jaxpr/ppermute | solution.py:11
  451.9 10.9 %collective-permute-start.1 = (f32[128,256]{0,1:T(8,128)S(1)}, f32[128,256]{0,1:T(8,128)S(1)}, u32[]{:S(2)}, u32[]{:S(2)}) collective-permute-start(f32[128,256]{0,1:T(8,128)S(1)} %get-tuple-element.1720), channel_id=1, source_target_pairs={{0,4},{4,8},{8,12},{12,16},{16,20},{20,24},{24,28},{28,32},{32,36}... | collective-permute-start | bytes 393224 | tf_op jit(solution)/shard_map/while/body/eval_jaxpr/ppermute | solution.py:11
  462.9 10.9 %collective-permute-start.1 = (f32[128,256]{0,1:T(8,128)S(1)}, f32[128,256]{0,1:T(8,128)S(1)}, u32[]{:S(2)}, u32[]{:S(2)}) collective-permute-start(f32[128,256]{0,1:T(8,128)S(1)} %get-tuple-element.1720), channel_id=1, source_target_pairs={{0,4},{4,8},{8,12},{12,16},{16,20},{20,24},{24,28},{28,32},{32,36}... | collective-permute-start | bytes 393224 | tf_op jit(solution)/shard_map/while/body/eval_jaxpr/ppermute | solution.py:11
  473.9 10.9 %collective-permute-start.1 = (f32[128,256]{0,1:T(8,128)S(1)}, f32[128,256]{0,1:T(8,128)S(1)}, u32[]{:S(2)}, u32[]{:S(2)}) collective-permute-start(f32[128,256]{0,1:T(8,128)S(1)} %get-tuple-element.1720), channel_id=1, source_target_pairs={{0,4},{4,8},{8,12},{12,16},{16,20},{20,24},{24,28},{28,32},{32,36}... | collective-permute-start | bytes 393224 | tf_op jit(solution)/shard_map/while/body/eval_jaxpr/ppermute | solution.py:11
  484.9 10.9 %collective-permute-start.1 = (f32[128,256]{0,1:T(8,128)S(1)}, f32[128,256]{0,1:T(8,128)S(1)}, u32[]{:S(2)}, u32[]{:S(2)}) collective-permute-start(f32[128,256]{0,1:T(8,128)S(1)} %get-tuple-element.1720), channel_id=1, source_target_pairs={{0,4},{4,8},{8,12},{12,16},{16,20},{20,24},{24,28},{28,32},{32,36}... | collective-permute-start | bytes 393224 | tf_op jit(solution)/shard_map/while/body/eval_jaxpr/ppermute | solution.py:11
  495.8 10.9 %collective-permute-start.1 = (f32[128,256]{0,1:T(8,128)S(1)}, f32[128,256]{0,1:T(8,128)S(1)}, u32[]{:S(2)}, u32[]{:S(2)}) collective-permute-start(f32[128,256]{0,1:T(8,128)S(1)} %get-tuple-element.1720), channel_id=1, source_target_pairs={{0,4},{4,8},{8,12},{12,16},{16,20},{20,24},{24,28},{28,32},{32,36}... | collective-permute-start | bytes 393224 | tf_op jit(solution)/shard_map/while/body/eval_jaxpr/ppermute | solution.py:11
  506.8 10.9 %collective-permute-start.1 = (f32[128,256]{0,1:T(8,128)S(1)}, f32[128,256]{0,1:T(8,128)S(1)}, u32[]{:S(2)}, u32[]{:S(2)}) collective-permute-start(f32[128,256]{0,1:T(8,128)S(1)} %get-tuple-element.1720), channel_id=1, source_target_pairs={{0,4},{4,8},{8,12},{12,16},{16,20},{20,24},{24,28},{28,32},{32,36}... | collective-permute-start | bytes 393224 | tf_op jit(solution)/shard_map/while/body/eval_jaxpr/ppermute | solution.py:11
  517.8 10.9 %collective-permute-start.1 = (f32[128,256]{0,1:T(8,128)S(1)}, f32[128,256]{0,1:T(8,128)S(1)}, u32[]{:S(2)}, u32[]{:S(2)}) collective-permute-start(f32[128,256]{0,1:T(8,128)S(1)} %get-tuple-element.1720), channel_id=1, source_target_pairs={{0,4},{4,8},{8,12},{12,16},{16,20},{20,24},{24,28},{28,32},{32,36}... | collective-permute-start | bytes 393224 | tf_op jit(solution)/shard_map/while/body/eval_jaxpr/ppermute | solution.py:11
  528.7 10.9 %collective-permute-start.1 = (f32[128,256]{0,1:T(8,128)S(1)}, f32[128,256]{0,1:T(8,128)S(1)}, u32[]{:S(2)}, u32[]{:S(2)}) collective-permute-start(f32[128,256]{0,1:T(8,128)S(1)} %get-tuple-element.1720), channel_id=1, source_target_pairs={{0,4},{4,8},{8,12},{12,16},{16,20},{20,24},{24,28},{28,32},{32,36}... | collective-permute-start | bytes 393224 | tf_op jit(solution)/shard_map/while/body/eval_jaxpr/ppermute | solution.py:11
  539.7 10.9 %collective-permute-start.1 = (f32[128,256]{0,1:T(8,128)S(1)}, f32[128,256]{0,1:T(8,128)S(1)}, u32[]{:S(2)}, u32[]{:S(2)}) collective-permute-start(f32[128,256]{0,1:T(8,128)S(1)} %get-tuple-element.1720), channel_id=1, source_target_pairs={{0,4},{4,8},{8,12},{12,16},{16,20},{20,24},{24,28},{28,32},{32,36}... | collective-permute-start | bytes 393224 | tf_op jit(solution)/shard_map/while/body/eval_jaxpr/ppermute | solution.py:11
  550.7 10.9 %collective-permute-start.1 = (f32[128,256]{0,1:T(8,128)S(1)}, f32[128,256]{0,1:T(8,128)S(1)}, u32[]{:S(2)}, u32[]{:S(2)}) collective-permute-start(f32[128,256]{0,1:T(8,128)S(1)} %get-tuple-element.1720), channel_id=1, source_target_pairs={{0,4},{4,8},{8,12},{12,16},{16,20},{20,24},{24,28},{28,32},{32,36}... | collective-permute-start | bytes 393224 | tf_op jit(solution)/shard_map/while/body/eval_jaxpr/ppermute | solution.py:11
  561.7 10.9 %collective-permute-start.1 = (f32[128,256]{0,1:T(8,128)S(1)}, f32[128,256]{0,1:T(8,128)S(1)}, u32[]{:S(2)}, u32[]{:S(2)}) collective-permute-start(f32[128,256]{0,1:T(8,128)S(1)} %get-tuple-element.1720), channel_id=1, source_target_pairs={{0,4},{4,8},{8,12},{12,16},{16,20},{20,24},{24,28},{28,32},{32,36}... | collective-permute-start | bytes 393224 | tf_op jit(solution)/shard_map/while/body/eval_jaxpr/ppermute | solution.py:11
  572.6 10.9 %collective-permute-start.1 = (f32[128,256]{0,1:T(8,128)S(1)}, f32[128,256]{0,1:T(8,128)S(1)}, u32[]{:S(2)}, u32[]{:S(2)}) collective-permute-start(f32[128,256]{0,1:T(8,128)S(1)} %get-tuple-element.1720), channel_id=1, source_target_pairs={{0,4},{4,8},{8,12},{12,16},{16,20},{20,24},{24,28},{28,32},{32,36}... | collective-permute-start | bytes 393224 | tf_op jit(solution)/shard_map/while/body/eval_jaxpr/ppermute | solution.py:11
  583.6 10.9 %collective-permute-start.1 = (f32[128,256]{0,1:T(8,128)S(1)}, f32[128,256]{0,1:T(8,128)S(1)}, u32[]{:S(2)}, u32[]{:S(2)}) collective-permute-start(f32[128,256]{0,1:T(8,128)S(1)} %get-tuple-element.1720), channel_id=1, source_target_pairs={{0,4},{4,8},{8,12},{12,16},{16,20},{20,24},{24,28},{28,32},{32,36}... | collective-permute-start | bytes 393224 | tf_op jit(solution)/shard_map/while/body/eval_jaxpr/ppermute | solution.py:11
  594.6 10.9 %collective-permute-start.1 = (f32[128,256]{0,1:T(8,128)S(1)}, f32[128,256]{0,1:T(8,128)S(1)}, u32[]{:S(2)}, u32[]{:S(2)}) collective-permute-start(f32[128,256]{0,1:T(8,128)S(1)} %get-tuple-element.1720), channel_id=1, source_target_pairs={{0,4},{4,8},{8,12},{12,16},{16,20},{20,24},{24,28},{28,32},{32,36}... | collective-permute-start | bytes 393224 | tf_op jit(solution)/shard_map/while/body/eval_jaxpr/ppermute | solution.py:11
  605.6 10.9 %collective-permute-start.1 = (f32[128,256]{0,1:T(8,128)S(1)}, f32[128,256]{0,1:T(8,128)S(1)}, u32[]{:S(2)}, u32[]{:S(2)}) collective-permute-start(f32[128,256]{0,1:T(8,128)S(1)} %get-tuple-element.1720), channel_id=1, source_target_pairs={{0,4},{4,8},{8,12},{12,16},{16,20},{20,24},{24,28},{28,32},{32,36}... | collective-permute-start | bytes 393224 | tf_op jit(solution)/shard_map/while/body/eval_jaxpr/ppermute | solution.py:11
  616.5 10.9 %collective-permute-start.1 = (f32[128,256]{0,1:T(8,128)S(1)}, f32[128,256]{0,1:T(8,128)S(1)}, u32[]{:S(2)}, u32[]{:S(2)}) collective-permute-start(f32[128,256]{0,1:T(8,128)S(1)} %get-tuple-element.1720), channel_id=1, source_target_pairs={{0,4},{4,8},{8,12},{12,16},{16,20},{20,24},{24,28},{28,32},{32,36}... | collective-permute-start | bytes 393224 | tf_op jit(solution)/shard_map/while/body/eval_jaxpr/ppermute | solution.py:11
  627.5 10.9 %collective-permute-start.1 = (f32[128,256]{0,1:T(8,128)S(1)}, f32[128,256]{0,1:T(8,128)S(1)}, u32[]{:S(2)}, u32[]{:S(2)}) collective-permute-start(f32[128,256]{0,1:T(8,128)S(1)} %get-tuple-element.1720), channel_id=1, source_target_pairs={{0,4},{4,8},{8,12},{12,16},{16,20},{20,24},{24,28},{28,32},{32,36}... | collective-permute-start | bytes 393224 | tf_op jit(solution)/shard_map/while/body/eval_jaxpr/ppermute | solution.py:11
  638.5 11.1 %collective-permute-start.1 = (f32[128,256]{0,1:T(8,128)S(1)}, f32[128,256]{0,1:T(8,128)S(1)}, u32[]{:S(2)}, u32[]{:S(2)}) collective-permute-start(f32[128,256]{0,1:T(8,128)S(1)} %get-tuple-element.1720), channel_id=1, source_target_pairs={{0,4},{4,8},{8,12},{12,16},{16,20},{20,24},{24,28},{28,32},{32,36}... | collective-permute-start | bytes 393224 | tf_op jit(solution)/shard_map/while/body/eval_jaxpr/ppermute | solution.py:11
  649.7 13.4 %collective-permute-start.1 = (f32[128,256]{0,1:T(8,128)S(1)}, f32[128,256]{0,1:T(8,128)S(1)}, u32[]{:S(2)}, u32[]{:S(2)}) collective-permute-start(f32[128,256]{0,1:T(8,128)S(1)} %get-tuple-element.1720), channel_id=1, source_target_pairs={{0,4},{4,8},{8,12},{12,16},{16,20},{20,24},{24,28},{28,32},{32,36}... | collective-permute-start | bytes 393224 | tf_op jit(solution)/shard_map/while/body/eval_jaxpr/ppermute | solution.py:11
  663.1 13.4 %collective-permute-start.1 = (f32[128,256]{0,1:T(8,128)S(1)}, f32[128,256]{0,1:T(8,128)S(1)}, u32[]{:S(2)}, u32[]{:S(2)}) collective-permute-start(f32[128,256]{0,1:T(8,128)S(1)} %get-tuple-element.1720), channel_id=1, source_target_pairs={{0,4},{4,8},{8,12},{12,16},{16,20},{20,24},{24,28},{28,32},{32,36}... | collective-permute-start | bytes 393224 | tf_op jit(solution)/shard_map/while/body/eval_jaxpr/ppermute | solution.py:11
  676.6 13.4 %collective-permute-start.1 = (f32[128,256]{0,1:T(8,128)S(1)}, f32[128,256]{0,1:T(8,128)S(1)}, u32[]{:S(2)}, u32[]{:S(2)}) collective-permute-start(f32[128,256]{0,1:T(8,128)S(1)} %get-tuple-element.1720), channel_id=1, source_target_pairs={{0,4},{4,8},{8,12},{12,16},{16,20},{20,24},{24,28},{28,32},{32,36}... | collective-permute-start | bytes 393224 | tf_op jit(solution)/shard_map/while/body/eval_jaxpr/ppermute | solution.py:11
  690.0 13.4 %collective-permute-start.1 = (f32[128,256]{0,1:T(8,128)S(1)}, f32[128,256]{0,1:T(8,128)S(1)}, u32[]{:S(2)}, u32[]{:S(2)}) collective-permute-start(f32[128,256]{0,1:T(8,128)S(1)} %get-tuple-element.1720), channel_id=1, source_target_pairs={{0,4},{4,8},{8,12},{12,16},{16,20},{20,24},{24,28},{28,32},{32,36}... | collective-permute-start | bytes 393224 | tf_op jit(solution)/shard_map/while/body/eval_jaxpr/ppermute | solution.py:11
  703.4 13.4 %collective-permute-start.1 = (f32[128,256]{0,1:T(8,128)S(1)}, f32[128,256]{0,1:T(8,128)S(1)}, u32[]{:S(2)}, u32[]{:S(2)}) collective-permute-start(f32[128,256]{0,1:T(8,128)S(1)} %get-tuple-element.1720), channel_id=1, source_target_pairs={{0,4},{4,8},{8,12},{12,16},{16,20},{20,24},{24,28},{28,32},{32,36}... | collective-permute-start | bytes 393224 | tf_op jit(solution)/shard_map/while/body/eval_jaxpr/ppermute | solution.py:11
  716.9 14.2 %collective-permute-start.1 = (f32[128,256]{0,1:T(8,128)S(1)}, f32[128,256]{0,1:T(8,128)S(1)}, u32[]{:S(2)}, u32[]{:S(2)}) collective-permute-start(f32[128,256]{0,1:T(8,128)S(1)} %get-tuple-element.1720), channel_id=1, source_target_pairs={{0,4},{4,8},{8,12},{12,16},{16,20},{20,24},{24,28},{28,32},{32,36}... | collective-permute-start | bytes 393224 | tf_op jit(solution)/shard_map/while/body/eval_jaxpr/ppermute | solution.py:11
  731.1 13.4 %collective-permute-start.1 = (f32[128,256]{0,1:T(8,128)S(1)}, f32[128,256]{0,1:T(8,128)S(1)}, u32[]{:S(2)}, u32[]{:S(2)}) collective-permute-start(f32[128,256]{0,1:T(8,128)S(1)} %get-tuple-element.1720), channel_id=1, source_target_pairs={{0,4},{4,8},{8,12},{12,16},{16,20},{20,24},{24,28},{28,32},{32,36}... | collective-permute-start | bytes 393224 | tf_op jit(solution)/shard_map/while/body/eval_jaxpr/ppermute | solution.py:11
  744.5 13.4 %collective-permute-start.1 = (f32[128,256]{0,1:T(8,128)S(1)}, f32[128,256]{0,1:T(8,128)S(1)}, u32[]{:S(2)}, u32[]{:S(2)}) collective-permute-start(f32[128,256]{0,1:T(8,128)S(1)} %get-tuple-element.1720), channel_id=1, source_target_pairs={{0,4},{4,8},{8,12},{12,16},{16,20},{20,24},{24,28},{28,32},{32,36}... | collective-permute-start | bytes 393224 | tf_op jit(solution)/shard_map/while/body/eval_jaxpr/ppermute | solution.py:11
  758.0 13.4 %collective-permute-start.1 = (f32[128,256]{0,1:T(8,128)S(1)}, f32[128,256]{0,1:T(8,128)S(1)}, u32[]{:S(2)}, u32[]{:S(2)}) collective-permute-start(f32[128,256]{0,1:T(8,128)S(1)} %get-tuple-element.1720), channel_id=1, source_target_pairs={{0,4},{4,8},{8,12},{12,16},{16,20},{20,24},{24,28},{28,32},{32,36}... | collective-permute-start | bytes 393224 | tf_op jit(solution)/shard_map/while/body/eval_jaxpr/ppermute | solution.py:11
  771.4 13.4 %collective-permute-start.1 = (f32[128,256]{0,1:T(8,128)S(1)}, f32[128,256]{0,1:T(8,128)S(1)}, u32[]{:S(2)}, u32[]{:S(2)}) collective-permute-start(f32[128,256]{0,1:T(8,128)S(1)} %get-tuple-element.1720), channel_id=1, source_target_pairs={{0,4},{4,8},{8,12},{12,16},{16,20},{20,24},{24,28},{28,32},{32,36}... | collective-permute-start | bytes 393224 | tf_op jit(solution)/shard_map/while/body/eval_jaxpr/ppermute | solution.py:11
  784.9 13.4 %collective-permute-start.1 = (f32[128,256]{0,1:T(8,128)S(1)}, f32[128,256]{0,1:T(8,128)S(1)}, u32[]{:S(2)}, u32[]{:S(2)}) collective-permute-start(f32[128,256]{0,1:T(8,128)S(1)} %get-tuple-element.1720), channel_id=1, source_target_pairs={{0,4},{4,8},{8,12},{12,16},{16,20},{20,24},{24,28},{28,32},{32,36}... | collective-permute-start | bytes 393224 | tf_op jit(solution)/shard_map/while/body/eval_jaxpr/ppermute | solution.py:11
  798.4 9.8 collective-permute-start.2
  802.8 37.3 %all-to-all-start = ((bf16[128,32,256]{0,2,1:T(8,128)(2,1)}), bf16[128,32,256]{0,2,1:T(8,128)(2,1)S(1)}, u32[]{:S(2)}, u32[]{:S(2)}) async-start(bf16[128,32,256]{0,2,1:T(8,128)(2,1)} %bitcast.61), calls=%async_computation | async-start | bytes 4194304 | tf_op jit(solution)/shard_map/all_to_all | solution.py:163
  807.4 197.9 %all-gather.4.cloned.1.call-start = ((), (), s32[]{:S(2)}) async-start(), calls=%async_computation.1 | async-start | bytes 2162688 | tf_op jit(solution)/shard_map/all_gather | solution.py:49
  808.9 267.2 %all-reduce.3.cloned.1.call-start = ((), (), s32[]{:S(2)}) async-start(), calls=%async_computation.2 | async-start | bytes 524288 | tf_op jit(solution)/shard_map/psum | solution.py:165
  (8 other events, 60.4 us)
Sparse Core Ops, SparseCore 0:
  11.0 51.6 all-gather.5
  1009.1 66.9 all-reduce.2
Sparse Core Ops, SparseCore 1:
  810.5 194.7 all-gather.3
where the time goes:
time: 1100 us; the launch traced here: 1090 us
  waiting for transfers between devices  347 us (32%)
  other arithmetic  283 us (26%)
  starting transfers between devices  159 us (14%)
  loops' own time  124 us (11%)
  matrix products  87.6 us (8%)
  local copies, waits for them, and re-layouts  67.8 us (6%)
  between operations  17.6 us (2%)
    all_gather x1, waiting for transfers between devices, collect_grads(): return lax.all_gather(own_rounded, 'ctx', axis=0, tiled=True)  162 us
    ppermute x63, starting transfers between devices, shifted(): lax.ppermute(array, axis, [(i, (i + by) % devices) for i in range(devices)])  154 us
    ppermute x63, waiting for transfers between devices, shifted(): lax.ppermute(array, axis, [(i, (i + by) % devices) for i in range(devices)])  87.8 us
    reduce_sum x63, other arithmetic, stored_positions(): first = jnp.sum(jnp.where(matches, order[None, :], 0), axis=1)[:, None]  81.8 us
    reduce_min x62, other arithmetic, is_live(): return jnp.min(key_positions) <= jnp.max(my_positions)  80.3 us
    psum x1, waiting for transfers between devices, shards(): weight_total = lax.psum(weight_part, 'dp')  65.6 us
    another operation x1, loops' own time, shards(): loop_state = lax.fori_loop(1, context, grad_step, (travelling, query_total))  62.2 us
    le x62, other arithmetic, allowed(): key_positions[None, :] <= row_positions[:, None]  60.6 us
  transfers between devices with their start and end apart: 67, of which 35 were waited for; matrix products, arithmetic and copies ran while one was open for 40% of the time, Pallas kernels for 0%

commit v1 on v0

v1 whole, which is shorter than its diff:
```python
import functools

import jax
import jax.numpy as jnp
from jax import lax
from jax.experimental import pallas as pl
from jax.experimental.pallas import tpu as pltpu
from jax.sharding import Mesh, PartitionSpec as P

HEAD = 128
SPAN = 64
TILE = 256
SPANS_PER_TILE = TILE // SPAN
NEG = -1e30
SCALE = HEAD ** (-0.5)
VMEM_LIMIT = 40 * 1024 * 1024


def nt(left, right):
    return lax.dot_general(left, right, (((1,), (1,)), ((), ())), preferred_element_type=jnp.float32)


def nn(left, right):
    return lax.dot_general(left, right, (((1,), (0,)), ((), ())), preferred_element_type=jnp.float32)


def load_operands(meta, own, other, kv, q_s, g_s, k_s, v_s, pos_s):
    heads = own.shape[2] // HEAD
    rows = heads * SPAN
    for source, block in enumerate((own, other)):
        for half in range(2):
            base = (source * 2 + half) * rows
            for head in range(heads):
                here = pl.ds(base + head * SPAN, SPAN)
                q_s[here, :] = block[0, half * SPAN:(half + 1) * SPAN, head * HEAD:(head + 1) * HEAD]
                g_s[here, :] = block[1, half * SPAN:(half + 1) * SPAN, head * HEAD:(head + 1) * HEAD]
    lane_rows = lax.broadcasted_iota(jnp.int32, (SPAN, 128), 0)

    def place(block, carry):
        for half in range(2):
            span = 2 * block + half
            start = pl.multiple_of(meta[0, span] * SPAN, SPAN)
            piece = kv[block, half * SPAN:(half + 1) * SPAN, :]
            k_s[pl.ds(start, SPAN), :] = piece[:, :HEAD]
            v_s[pl.ds(start, SPAN), :] = piece[:, HEAD:]
            pos_s[pl.ds(start, SPAN), :] = lane_rows + meta[1, span] * SPAN
        return carry

    lax.fori_loop(0, kv.shape[0], place, 0)


def masked_scores(k_tile, q_rows, pos_tile, q_pos, q_start):
    copies = q_rows.shape[0] // 128
    key_pos = jnp.concatenate([pos_tile] * copies, axis=1)
    mask = (key_pos <= q_pos) & (key_pos >= q_start)
    return jnp.where(mask, nt(k_tile, q_rows) * SCALE, NEG)


def stats_kernel(meta, qmeta, own, other, kv, out, q_s, g_s, k_s, v_s, pos_s):
    load_operands(meta, own, other, kv, q_s, g_s, k_s, v_s, pos_s)
    rows = q_s.shape[0] // 4

    def span_step(u, carry):
        q_rows = q_s[pl.ds(u * rows, rows), :]
        g_rows = g_s[pl.ds(u * rows, rows), :]
        q_pos = qmeta[pl.ds(u, 1), :]
        q_start = qmeta[pl.ds(4 + u, 1), :]

        def tile_step(t, state):
            top, total, weighted = state
            here = pl.ds(pl.multiple_of(t * TILE, TILE), TILE)
            scores = masked_scores(k_s[here, :], q_rows, pos_s[here, :], q_pos, q_start)
            new_top = jnp.maximum(top, jnp.max(scores, axis=0, keepdims=True))
            probs = jnp.exp(scores - new_top)
            keep = jnp.exp(top - new_top)
            grad = nt(v_s[here, :], g_rows)
            return (
                new_top,
                keep * total + jnp.sum(probs, axis=0, keepdims=True),
                keep * weighted + jnp.sum(probs * grad, axis=0, keepdims=True),
            )

        zero = jnp.zeros((1, rows), jnp.float32)
        top, total, weighted = lax.fori_loop(
            meta[2, u], meta[2, 4 + u], tile_step, (jnp.full((1, rows), NEG, jnp.float32), zero, zero)
        )
        out[pl.ds(u, 1), :] = top
        out[pl.ds(4 + u, 1), :] = total
        out[pl.ds(8 + u, 1), :] = weighted
        return carry

    lax.fori_loop(0, 4, span_step, 0)
    out[12:16, :] = jnp.zeros((4, rows), jnp.float32)


def grad_kernel(
    meta, qmeta, own, other, kv, stats, far, dq_own, dq_other, dkv,
    q_s, g_s, k_s, v_s, pos_s, kt_s, dk_s, dv_s, dq_s, fin_s,
):
    load_operands(meta, own, other, kv, q_s, g_s, k_s, v_s, pos_s)
    rows = q_s.shape[0] // 4
    heads = rows // SPAN
    tiles = k_s.shape[0] // TILE
    for t in range(tiles):
        kt_s[t] = k_s[t * TILE:(t + 1) * TILE, :].T
    dk_s[...] = jnp.zeros_like(dk_s)
    dv_s[...] = jnp.zeros_like(dv_s)
    for u in range(4):
        v = (u + 2) % 4
        top_a, top_b = stats[u:u + 1, :], far[v:v + 1, :]
        top = jnp.maximum(top_a, top_b)
        scale_a, scale_b = jnp.exp(top_a - top), jnp.exp(top_b - top)
        total = scale_a * stats[4 + u:5 + u, :] + scale_b * far[4 + v:5 + v, :]
        weighted = scale_a * stats[8 + u:9 + u, :] + scale_b * far[8 + v:9 + v, :]
        fin_s[u:u + 1, :] = top + jnp.log(total)
        fin_s[4 + u:5 + u, :] = weighted / total

    def span_step(u, carry):
        q_rows = q_s[pl.ds(u * rows, rows), :]
        g_rows = g_s[pl.ds(u * rows, rows), :]
        q_pos = qmeta[pl.ds(u, 1), :]
        q_start = qmeta[pl.ds(4 + u, 1), :]
        log_norm = fin_s[pl.ds(u, 1), :]
        drift = fin_s[pl.ds(4 + u, 1), :]
        dq_s[...] = jnp.zeros_like(dq_s)

        def tile_step(t, inner):
            here = pl.ds(pl.multiple_of(t * TILE, TILE), TILE)
            scores = masked_scores(k_s[here, :], q_rows, pos_s[here, :], q_pos, q_start)
            probs = jnp.exp(scores - log_norm)
            grad = nt(v_s[here, :], g_rows)
            score_grad = (probs * (grad - drift)).astype(jnp.bfloat16)
            dv_s[here, :] += nn(probs.astype(jnp.bfloat16), g_rows)
            dk_s[here, :] += nn(score_grad, q_rows)
            dq_s[...] += nn(kt_s[t], score_grad)
            return inner

        lax.fori_loop(meta[2, u], meta[2, 4 + u], tile_step, 0)
        flat = (dq_s[...] * SCALE).T
        half = pl.multiple_of(lax.rem(u, 2) * SPAN, SPAN)

        @pl.when(u < 2)
        def _():
            for head in range(heads):
                dq_own[pl.ds(half, SPAN), head * HEAD:(head + 1) * HEAD] = flat[head * SPAN:(head + 1) * SPAN, :]

        @pl.when(u >= 2)
        def _():
            for head in range(heads):
                dq_other[pl.ds(half, SPAN), head * HEAD:(head + 1) * HEAD] = flat[
                    head * SPAN:(head + 1) * SPAN, :
                ].astype(jnp.bfloat16)

        return carry

    lax.fori_loop(0, 4, span_step, 0)

    def unplace(block, carry):
        for half in range(2):
            start = pl.multiple_of(meta[0, 2 * block + half] * SPAN, SPAN)
            here = pl.ds(start, SPAN)
            dkv[block, half * SPAN:(half + 1) * SPAN, :HEAD] = (dk_s[here, :] * SCALE).astype(jnp.bfloat16)
            dkv[block, half * SPAN:(half + 1) * SPAN, HEAD:] = dv_s[here, :].astype(jnp.bfloat16)
        return carry

    lax.fori_loop(0, dkv.shape[0], unplace, 0)


def operand_scratch(rows, keys):
    return [
        pltpu.VMEM((4 * rows, HEAD), jnp.bfloat16),
        pltpu.VMEM((4 * rows, HEAD), jnp.bfloat16),
        pltpu.VMEM((keys, HEAD), jnp.bfloat16),
        pltpu.VMEM((keys, HEAD), jnp.bfloat16),
        pltpu.VMEM((keys, 128), jnp.int32),
    ]


def in_vmem(count):
    return [pl.BlockSpec(memory_space=pltpu.SMEM)] + [pl.BlockSpec(memory_space=pltpu.VMEM)] * count


def stats_call(meta, qmeta, own, other, kv):
    rows = own.shape[2] // HEAD * SPAN
    keys = kv.shape[0] * kv.shape[1]
    return pl.pallas_call(
        stats_kernel,
        out_shape=jax.ShapeDtypeStruct((16, rows), jnp.float32),
        in_specs=in_vmem(4),
        out_specs=pl.BlockSpec(memory_space=pltpu.VMEM),
        scratch_shapes=operand_scratch(rows, keys),
        compiler_params=pltpu.CompilerParams(vmem_limit_bytes=VMEM_LIMIT),
        cost_estimate=pl.CostEstimate(flops=2 * 10**9, bytes_accessed=4 * 10**6, transcendentals=10**6),
        name="stats",
    )(meta, qmeta, own, other, kv)


def grad_call(meta, qmeta, own, other, kv, stats, far):
    rows = own.shape[2] // HEAD * SPAN
    keys = kv.shape[0] * kv.shape[1]
    height, width = own.shape[1:]
    return pl.pallas_call(
        grad_kernel,
        out_shape=(
            jax.ShapeDtypeStruct((height, width), jnp.float32),
            jax.ShapeDtypeStruct((height, width), jnp.bfloat16),
            jax.ShapeDtypeStruct(kv.shape, jnp.bfloat16),
        ),
        in_specs=in_vmem(6),
        out_specs=[pl.BlockSpec(memory_space=pltpu.VMEM)] * 3,
        scratch_shapes=operand_scratch(rows, keys) + [
            pltpu.VMEM((keys // TILE, HEAD, TILE), jnp.bfloat16),
            pltpu.VMEM((keys, HEAD), jnp.float32),
            pltpu.VMEM((keys, HEAD), jnp.float32),
            pltpu.VMEM((HEAD, rows), jnp.float32),
            pltpu.VMEM((8, rows), jnp.float32),
        ],
        compiler_params=pltpu.CompilerParams(vmem_limit_bytes=VMEM_LIMIT),
        cost_estimate=pl.CostEstimate(flops=5 * 10**9, bytes_accessed=6 * 10**6, transcendentals=10**6),
        name="grads",
    )(meta, qmeta, own, other, kv, stats, far)


def swapped(array, axis):
    return lax.ppermute(array, axis, [(0, 1), (1, 0)])


def tables(doc_lengths, span_order):
    count = span_order.shape[0]
    outer, inner = lax.axis_size("ya"), lax.axis_size("z")
    side = lax.axis_index("yb")
    boundary = jnp.cumsum(doc_lengths[0])
    order = span_order.reshape(outer, 2, inner)
    mine = jnp.where(side == 0, order[:, 0], order[:, 1]).reshape(-1)
    spans = jnp.stack([mine, 2 * count - 1 - mine], axis=1).reshape(-1)
    rank = jnp.sum((spans[None, :] < spans[:, None]).astype(jnp.int32), axis=1)
    ctx = lax.axis_index(("ya", "yb", "z"))
    ids = jnp.arange(count, dtype=jnp.int32)
    first = jnp.sum(jnp.where(ids == ctx, span_order, 0))
    partner = ctx + (1 - 2 * side) * inner
    second = jnp.sum(jnp.where(ids == partner, span_order, 0))
    q_spans = jnp.stack([first, 2 * count - 1 - first, second, 2 * count - 1 - second])

    def doc_start(positions):
        reached = boundary <= positions[..., None]
        return jnp.max(jnp.where(reached, boundary, 0), axis=-1)

    low = doc_start(q_spans * SPAN) // SPAN
    lower = jnp.sum((spans[None, :] < low[:, None]).astype(jnp.int32), axis=1) // SPANS_PER_TILE
    upper = jnp.sum((spans[None, :] <= q_spans[:, None]).astype(jnp.int32), axis=1)
    upper = (upper + SPANS_PER_TILE - 1) // SPANS_PER_TILE
    bounds = jnp.concatenate([lower, upper, jnp.zeros((spans.shape[0] - 8,), jnp.int32)])
    meta = jnp.stack([rank, spans, bounds])
    return meta, q_spans, doc_start


def shards(queries, keys, values, out_grad, normed_input, doc_lengths, span_order):
    height = queries.shape[1]
    heads = queries.shape[2] // HEAD
    group = ("ya", "z")
    group_size = lax.axis_size("ya") * lax.axis_size("z")
    depth = lax.axis_size("z")

    own = jnp.concatenate([queries, out_grad], axis=0)
    other = swapped(own, "yb")
    pair = jnp.concatenate([keys[0], values[0]], axis=1)
    kv = lax.all_to_all(
        jnp.broadcast_to(pair[None], (group_size,) + pair.shape), group, 0, 0, tiled=True
    )

    meta, q_spans, doc_start = tables(doc_lengths, span_order)
    q_pos = q_spans[:, None] * SPAN + jnp.arange(SPAN, dtype=jnp.int32)[None, :]
    q_start = doc_start(q_pos)
    qmeta = jnp.tile(jnp.concatenate([q_pos, q_start], axis=0), (1, heads))

    stats = stats_call(meta, qmeta, own, other, kv)
    far = swapped(stats, "yb")

    width = normed_input.shape[2] // depth
    columns = lax.all_to_all(
        normed_input[0].reshape(height, depth, width), "z", split_axis=1, concat_axis=0, tiled=True
    ).reshape(depth * height, width)
    beside = swapped(columns, "yh")
    both = jnp.stack([columns, beside])
    across = swapped(both, "core")

    dq_own, dq_other, dkv = grad_call(meta, qmeta, own, other, kv, stats, far)
    dq_far = swapped(dq_other, "yb")
    parts = lax.all_to_all(dkv, group, 0, 0, tiled=True)
    own_grads = jnp.sum(parts.astype(jnp.float32), axis=0).astype(jnp.bfloat16)
    query_grad = (dq_own + dq_far.astype(jnp.float32)).astype(jnp.bfloat16)[None]

    all_grads = lax.all_to_all(
        jnp.broadcast_to(own_grads[None], (depth,) + own_grads.shape), "z", 0, 0, tiled=True
    ).reshape(depth * height, 2 * HEAD)

    def weights(features):
        return lax.dot_general(
            features, all_grads, (((1,), (0,)), ((), ())), preferred_element_type=jnp.float32
        )

    near = weights(both)
    far_weights = weights(across)
    core, high = lax.axis_index("core"), lax.axis_index("yh")
    by_core = jnp.where(
        core == 0, jnp.stack([near, far_weights], axis=1), jnp.stack([far_weights, near], axis=1)
    )
    by_high = jnp.where(high == 0, by_core, by_core[::-1]).astype(jnp.bfloat16)
    blocks = by_high.reshape((4,) + by_high.shape[2:])
    pieces = lax.all_to_all(blocks, ("ya", "yb"), 0, 0, tiled=True)
    partial = jnp.sum(pieces.astype(jnp.float32), axis=0).astype(jnp.bfloat16)
    spread = lax.all_to_all(
        jnp.broadcast_to(partial[None], (lax.axis_size("dp"),) + partial.shape), "dp", 0, 0, tiled=True
    )
    weight_total = jnp.sum(spread.astype(jnp.float32), axis=0)
    return (
        query_grad,
        own_grads[None, :, :HEAD],
        own_grads[None, :, HEAD:],
        weight_total[:, :HEAD],
        weight_total[:, HEAD:],
    )


def solution(mesh):
    sizes = dict(mesh.shape)
    deep = sizes["ctx"] // 4
    fine = Mesh(
        mesh.devices.reshape(sizes["dp"], 2, 2, deep, 2, sizes["tp"] // 2),
        ("dp", "ya", "yb", "z", "yh", "core"),
    )
    context, model = ("ya", "yb", "z"), ("yh", "core")
    in_specs = (
        P("dp", context, model),
        P("dp", context, model),
        P("dp", context, model),
        P("dp", context, model),
        P("dp", context, model),
        P("dp", None),
        P(),
    )
    out_specs = (
        P("dp", context, model),
        P("dp", context, model),
        P("dp", context, model),
        P(context, model),
        P(context, model),
    )
    return jax.shard_map(shards, mesh=fine, in_specs=in_specs, out_specs=out_specs, check_vma=False)
```

time: 1100 us -> 195 us (0.18); the launches traced: 1090 us -> 193 us
  other arithmetic: 283 us -> 6.25 us
  waiting for transfers between devices: 347 us -> 94.7 us
  loops' own time: 124 us -> 0 us
  starting transfers between devices: 159 us -> 64.5 us
  matrix products: 87.6 us -> 3.14 us
  local copies, waits for them, and re-layouts: 67.8 us -> 8.47 us
  between operations: 17.6 us -> 2.21 us
  Pallas kernels: 0 us -> 14 us
    all_gather x2 -> x0, waiting for transfers between devices: 162 us -> none  [the longest x1 162 us: collect_grads(): return lax.all_gather(own_rounded, 'ctx', axis=0, tiled=True)]
    ppermute x63 -> x5, starting transfers between devices: 154 us -> 15.2 us  [swapped(): return lax.ppermute(array, axis, [(0, 1), (1, 0)])]
    another operation x66 -> x0, loops' own time: 124 us -> none  [the longest x1 62.2 us: shards(): loop_state = lax.fori_loop(1, context, grad_step, (travelling, query_total))]
    reduce_sum x158 -> x6, other arithmetic: 89.3 us -> 1.32 us  [the longest x1 0.63 us: tables(): first = jnp.sum(jnp.where(ids == ctx, span_order, 0))]
    ppermute x63 -> x5, waiting for transfers between devices: 87.8 us -> 3.04 us  [swapped(): return lax.ppermute(array, axis, [(0, 1), (1, 0)])]
    dot_general x225 -> x2, matrix products: 87.6 us -> 3.14 us  [weights(): lax.dot_general(features, all_grads, (((1,), (0,)), ((), ())), preferred_...]
    reduce_min x62 -> x0, other arithmetic: 80.3 us -> none  [is_live(): return jnp.min(key_positions) <= jnp.max(my_positions)]
    psum x1 -> x0, waiting for transfers between devices: 65.6 us -> none  [shards(): weight_total = lax.psum(weight_part, 'dp')]
  transfers between devices with their start and end apart: 67 -> 11, of which waited for: 35 -> 6; matrix products, arithmetic and copies ran while one was open for 40% -> 6% of each run, Pallas kernels for 0% -> 7%
where the time goes in v1:
time: 195 us; the launch traced here: 193 us
  waiting for transfers between devices  94.7 us (49%)
  starting transfers between devices  64.5 us (33%)
  Pallas kernels  14 us (7%)
  local copies, waits for them, and re-layouts  8.47 us (4%)
  other arithmetic  6.25 us (3%)
  matrix products  3.14 us (2%)
  between operations  2.21 us (1%)
    all_to_all x1, waiting for transfers between devices, shards(): parts = lax.all_to_all(dkv, group, 0, 0, tiled=True)  48.3 us
    all_to_all x1, waiting for transfers between devices, shards(): lax.all_to_all(jnp.broadcast_to(pair[None], (group_size,) + pair.shape),...  18.2 us
    ppermute x5, starting transfers between devices, swapped(): return lax.ppermute(array, axis, [(0, 1), (1, 0)])  15.2 us
    all_to_all x1, starting transfers between devices, shards(): parts = lax.all_to_all(dkv, group, 0, 0, tiled=True)  14.6 us
    all_to_all x1, starting transfers between devices, shards(): lax.all_to_all(jnp.broadcast_to(pair[None], (group_size,) + pair.shape),...  13.1 us
    all_to_all x1, waiting for transfers between devices, shards(): pieces = lax.all_to_all(blocks, ('ya', 'yb'), 0, 0, tiled=True)  10.2 us
    all_to_all x1, starting transfers between devices, shards(): pieces = lax.all_to_all(blocks, ('ya', 'yb'), 0, 0, tiled=True)  9.48 us
    all_to_all x1, waiting for transfers between devices, shards(): lax.all_to_all(jnp.broadcast_to(own_grads[None], (depth,) + own_grads.sha...  9.17 us
  transfers between devices with their start and end apart: 11, of which 6 were waited for; matrix products, arithmetic and copies ran while one was open for 6% of the time, Pallas kernels for 7%

profile of v1, /device:TPU:1, one launch (start us, length us, event | category | flops | bytes accessed | tf_op | source)
XLA Modules:
  0.0 193.3 jit_solution(226807795309808875)
XLA Ops:
  0.6 0.8 pad_maximum_fusion.1
  1.4 1.1 broadcast_in_dim.32
  2.5 13.1 %all-to-all-start = ((bf16[16,128,256]{2,1,0:T(8,128)(2,1)}), bf16[16,128,256]{2,1,0:T(8,128)(2,1)S(1)}, u32[]{:S(2)}, u32[]{:S(2)}) async-start(bf16[16,128,256]{2,1,0:T(8,128)(2,1)} %broadcast_in_dim.32), calls=%async_computation | async-start | bytes 2097152 | tf_op jit(solution)/shard_map/all_to_all | solution.py:267
  15.7 0.0 copy-start
  15.7 3.3 %collective-permute-start = (bf16[2,128,1024]{2,1,0:T(8,128)(2,1)S(1)}, bf16[2,128,1024]{2,1,0:T(8,128)(2,1)S(1)}, u32[]{:S(2)}, u32[]{:S(2)}) collective-permute-start(bf16[2,128,1024]{2,1,0:T(8,128)(2,1)S(1)} %constant_dynamic-update-slice_fusion.own), channel_id=1, source_target_pairs={{0,32},{32,0},{1,33},{33,1},{2,34},{34,2},{3,35},{35,3},{4,36},{36... | collective-permute-start | bytes 1572872 | tf_op jit(solution)/shard_map/ppermute | solution.py:225
  19.1 0.0 copy-start.3
  19.1 0.6 copy-done.3
  19.7 0.1 reshape.172
  19.8 0.1 select_n.69
  20.0 0.1 copy.25
  20.0 0.1 lt.28
  20.1 0.0 copy-start.4
  20.1 0.6 copy-done.4
  20.8 0.2 reduce-window.8
  21.0 0.6 fusion.3
  22.9 1.0 copy.27
  23.9 1.4 broadcast_multiply_fusion
  25.3 0.1 iota_add_fusion
  25.4 0.1 select_reduce_fusion
  25.5 0.2 select_reduce_fusion.1
  25.7 0.2 convert_reduce_fusion.3
  25.9 18.2 %all-to-all-done.kv = bf16[16,128,256]{2,1,0:T(8,128)(2,1)S(1)} async-done(((bf16[16,128,256]{2,1,0:T(8,128)(2,1)}), bf16[16,128,256]{2,1,0:T(8,128)(2,1)S(1)}, u32[]{:S(2)}, u32[]{:S(2)}) %all-to-all-start) | async-done | bytes 1048608 | tf_op jit(solution)/shard_map/all_to_all | solution.py:267
  44.1 4.2 %all-to-all-start.2 = ((bf16[128,8,256]{0,2,1:T(8,128)(2,1)}), bf16[128,8,256]{0,2,1:T(8,128)(2,1)S(1)}, u32[]{:S(2)}, u32[]{:S(2)}) async-start(bf16[128,8,256]{0,2,1:T(8,128)(2,1)} %bitcast.13), calls=%async_computation.2 | async-start | bytes 1048576 | tf_op jit(solution)/shard_map/all_to_all | solution.py:280
  48.3 0.1 add_bitcast_fusion
  48.4 0.1 broadcast_in_dim_reshape.2
  48.5 0.1 tile.10.qmeta
  48.6 0.2 convert_reduce_fusion.1
  48.7 0.0 collective-permute-done.other
  48.8 5.1 %stats.1 = f32[16,512]{1,0:T(8,128)S(1)} custom-call(s32[3,32]{1,0:T(4,128)S(1)} %pad_add_fusion.1.meta, s32[8,512]{1,0:T(8,128)S(1)} %tile.10.qmeta, bf16[2,128,1024]{2,1,0:T(8,128)(2,1)S(1)} %constant_dynamic-update-slice_fusion.own, bf16[2,128,1024]{2,1,0:T(8,128)(2,1)S(1)} %collective-permute-done.other, bf16[16,128,256]{2,1,0:T(8,128)(2,1)S(1)} %all-to-all-done.kv), custom_call_target="tpu_custom_call" | custom-call | flops 2000000000 | bytes 4000000 | tf_op jit(solution)/shard_map/stats/pallas_call | solution.py:186
  53.8 1.9 collective-permute-start.1
  55.8 3.0 %collective-permute-done.1.far = f32[16,512]{1,0:T(8,128)S(1)} collective-permute-done((f32[16,512]{1,0:T(8,128)S(1)}, f32[16,512]{1,0:T(8,128)S(1)}, u32[]{:S(2)}, u32[]{:S(2)}) %collective-permute-start.1) | collective-permute-done | bytes 32800 | tf_op jit(solution)/shard_map/ppermute | solution.py:225
  58.8 8.9 %grads.1 = (f32[128,1024]{1,0:T(8,128)S(1)}, bf16[128,1024]{1,0:T(8,128)(2,1)S(1)}, bf16[16,128,256]{2,1,0:T(8,128)(2,1)}) custom-call(s32[3,32]{1,0:T(4,128)S(1)} %pad_add_fusion.1.meta, s32[8,512]{1,0:T(8,128)S(1)} %tile.10.qmeta, bf16[2,128,1024]{2,1,0:T(8,128)(2,1)S(1)} %constant_dynamic-update-slice_fusion.own, ...), custom_call_target="tpu_custom_call" | custom-call | flops 5000000000 | bytes 6000000 | tf_op jit(solution)/shard_map/grads/pallas_call | solution.py:202
  67.7 0.0 all-to-all-done.2
  67.7 14.6 %all-to-all-start.1 = ((bf16[16,128,256]{2,1,0:T(8,128)(2,1)}), bf16[16,128,256]{2,1,0:T(8,128)(2,1)S(1)}, u32[]{:S(2)}, u32[]{:S(2)}) async-start(bf16[16,128,256]{2,1,0:T(8,128)(2,1)} %get-tuple-element.10), calls=%async_computation.1 | async-start | bytes 2097152 | tf_op jit(solution)/shard_map/all_to_all | solution.py:289
  82.3 0.3 copy.28
  82.6 0.1 copy.33
  82.7 2.1 %collective-permute-start.3 = (bf16[1024,256]{0,1:T(8,128)(2,1)S(1)}, bf16[1024,256]{0,1:T(8,128)(2,1)}, u32[]{:S(2)}, u32[]{:S(2)}) collective-permute-start(bf16[1024,256]{0,1:T(8,128)(2,1)S(1)} %bitcast.48), channel_id=1, source_target_pairs={{0,2},{2,0},{1,3},{3,1},{4,6},{6,4},{5,7},{7,5},{8,10},{10,8},{9,1... | collective-permute-start | bytes 1572872 | tf_op jit(solution)/shard_map/ppermute | solution.py:225
  84.8 0.2 stack_reshape.2
  85.1 48.3 %all-to-all-done.1 = bf16[16,128,256]{2,1,0:T(8,128)(2,1)S(1)} async-done(((bf16[16,128,256]{2,1,0:T(8,128)(2,1)}), bf16[16,128,256]{2,1,0:T(8,128)(2,1)S(1)}, u32[]{:S(2)}, u32[]{:S(2)}) %all-to-all-start.1) | async-done | bytes 1048608 | tf_op jit(solution)/shard_map/all_to_all | solution.py:289
  133.4 0.1 reduce_sum.83
  133.5 0.8 broadcast_in_dim.59
  134.4 4.5 %all-to-all-start.3 = ((bf16[8,128,256]{2,1,0:T(8,128)(2,1)}), bf16[8,128,256]{2,1,0:T(8,128)(2,1)S(1)}, u32[]{:S(2)}, u32[]{:S(2)}) async-start(bf16[8,128,256]{2,1,0:T(8,128)(2,1)} %broadcast_in_dim.59), calls=%async_computation.3 | async-start | bytes 1048576 | tf_op jit(solution)/shard_map/all_to_all | solution.py:293
  138.8 0.0 collective-permute-done.3
  138.8 1.1 pad_maximum_fusion
  140.0 4.5 %collective-permute-start.4 = (bf16[2,1024,256]{1,2,0:T(8,128)(2,1)S(1)}, bf16[2,1024,256]{1,2,0:T(8,128)(2,1)}, u32[]{:S(2)}, u32[]{:S(2)}) collective-permute-start(bf16[2,1024,256]{1,2,0:T(8,128)(2,1)S(1)} %pad_maximum_fusion), channel_id=1, source_target_pairs={{0,1},{1,0},{2,3},{3,2},{4,5},{5,4},{6,7},{7,6},{8,9},{9,8},{10,11... | collective-permute-start | bytes 3145736 | tf_op jit(solution)/shard_map/ppermute | solution.py:225
  144.5 9.2 %all-to-all-done.3 = bf16[8,128,256]{2,1,0:T(8,128)(2,1)S(1)} async-done(((bf16[8,128,256]{2,1,0:T(8,128)(2,1)}), bf16[8,128,256]{2,1,0:T(8,128)(2,1)S(1)}, u32[]{:S(2)}, u32[]{:S(2)}) %all-to-all-start.3) | async-done | bytes 524320 | tf_op jit(solution)/shard_map/all_to_all | solution.py:293
  153.7 1.5 convolution_bitcast_fusion.1
  155.2 0.0 collective-permute-done.4
  155.2 1.7 convolution_bitcast_fusion
  156.8 0.1 maximum_select_fusion
  156.9 0.1 fusion
  157.0 0.8 copy.30
  157.9 9.5 %all-to-all-start.4 = ((bf16[4,256,256]{2,1,0:T(8,128)(2,1)}), bf16[4,256,256]{2,1,0:T(8,128)(2,1)S(1)}, u32[]{:S(2)}, u32[]{:S(2)}) async-start(bf16[4,256,256]{2,1,0:T(8,128)(2,1)} %bitcast.23), calls=%async_computation.4 | async-start | bytes 1048576 | tf_op jit(solution)/shard_map/all_to_all | solution.py:310
  167.3 3.4 %collective-permute-start.2 = (bf16[128,1024]{1,0:T(8,128)(2,1)S(1)}, bf16[128,1024]{1,0:T(8,128)(2,1)S(1)}, u32[]{:S(2)}, u32[]{:S(2)}) collective-permute-start(bf16[128,1024]{1,0:T(8,128)(2,1)S(1)} %get-tuple-element.9), channel_id=1, source_target_pairs={{0,32},{32,0},{1,33},{33,1},{2,34},{34,2},{3,35},{35,3},{4,36},{36... | collective-permute-start | bytes 786440 | tf_op jit(solution)/shard_map/ppermute | solution.py:225
  170.7 10.2 %all-to-all-done.4 = bf16[4,256,256]{2,1,0:T(8,128)(2,1)S(1)} async-done(((bf16[4,256,256]{2,1,0:T(8,128)(2,1)}), bf16[4,256,256]{2,1,0:T(8,128)(2,1)S(1)}, u32[]{:S(2)}, u32[]{:S(2)}) %all-to-all-start.4) | async-done | bytes 524320 | tf_op jit(solution)/shard_map/all_to_all | solution.py:310
  180.9 0.1 reduce_sum.84
  181.0 0.8 broadcast_in_dim.60
  181.8 3.5 %all-to-all-start.5 = ((bf16[4,256,256]{2,1,0:T(8,128)(2,1)}), bf16[4,256,256]{2,1,0:T(8,128)(2,1)S(1)}, u32[]{:S(2)}, u32[]{:S(2)}) async-start(bf16[4,256,256]{2,1,0:T(8,128)(2,1)} %broadcast_in_dim.60), calls=%async_computation.5 | async-start | bytes 1048576 | tf_op jit(solution)/shard_map/all_to_all | solution.py:312
  185.3 0.0 collective-permute-done.2
  185.3 0.8 fusion.1
  186.1 0.6 slice_bitcast_fusion
  186.7 5.9 %all-to-all-done.5 = bf16[4,256,256]{2,1,0:T(8,128)(2,1)S(1)} async-done(((bf16[4,256,256]{2,1,0:T(8,128)(2,1)}), bf16[4,256,256]{2,1,0:T(8,128)(2,1)S(1)}, u32[]{:S(2)}, u32[]{:S(2)}) %all-to-all-start.5) | async-done | bytes 524320 | tf_op jit(solution)/shard_map/all_to_all | solution.py:312
  192.5 0.1 convert_reduce_fusion
  192.6 0.7 fusion.5
  (16 shorter events, 0.1 us)
Async XLA Ops:
  2.5 13.1 %copy-start.1 = (bf16[1,128,1024]{2,1,0:T(8,128)(2,1)S(1)}, bf16[1,128,1024]{2,1,0:T(8,128)(2,1)}, u32[]{:S(2)}) copy-start(bf16[1,128,1024]{2,1,0:T(8,128)(2,1)} %param.7) | copy-start | bytes 786436
  2.5 13.2 %copy-start.2 = (bf16[1,128,1024]{2,1,0:T(8,128)(2,1)S(1)}, bf16[1,128,1024]{2,1,0:T(8,128)(2,1)}, u32[]{:S(2)}) copy-start(bf16[1,128,1024]{2,1,0:T(8,128)(2,1)} %param.10) | copy-start | bytes 786436
  2.5 41.6 %all-to-all-start = ((bf16[16,128,256]{2,1,0:T(8,128)(2,1)}), bf16[16,128,256]{2,1,0:T(8,128)(2,1)S(1)}, u32[]{:S(2)}, u32[]{:S(2)}) async-start(bf16[16,128,256]{2,1,0:T(8,128)(2,1)} %broadcast_in_dim.32), calls=%async_computation | async-start | bytes 2097152 | tf_op jit(solution)/shard_map/all_to_all | solution.py:267
  15.7 7.3 %copy-start = (bf16[1,128,2048]{2,1,0:T(8,128)(2,1)S(1)}, bf16[1,128,2048]{2,1,0:T(8,128)(2,1)}, u32[]{:S(2)}) copy-start(bf16[1,128,2048]{2,1,0:T(8,128)(2,1)} %param.11) | copy-start | bytes 1572868
  15.7 33.0 %collective-permute-start = (bf16[2,128,1024]{2,1,0:T(8,128)(2,1)S(1)}, bf16[2,128,1024]{2,1,0:T(8,128)(2,1)S(1)}, u32[]{:S(2)}, u32[]{:S(2)}) collective-permute-start(bf16[2,128,1024]{2,1,0:T(8,128)(2,1)S(1)} %constant_dynamic-update-slice_fusion.own), channel_id=1, source_target_pairs={{0,32},{32,0},{1,33},{33,1},{2,34},{34,2},{3,35},{35,3},{4,36},{36... | collective-permute-start | bytes 1572872 | tf_op jit(solution)/shard_map/ppermute | solution.py:225
  19.1 0.7 copy-start.3
  20.1 0.7 copy-start.4
  44.1 23.6 %all-to-all-start.2 = ((bf16[128,8,256]{0,2,1:T(8,128)(2,1)}), bf16[128,8,256]{0,2,1:T(8,128)(2,1)S(1)}, u32[]{:S(2)}, u32[]{:S(2)}) async-start(bf16[128,8,256]{0,2,1:T(8,128)(2,1)} %bitcast.13), calls=%async_computation.2 | async-start | bytes 1048576 | tf_op jit(solution)/shard_map/all_to_all | solution.py:280
  53.8 5.0 %collective-permute-start.1 = (f32[16,512]{1,0:T(8,128)S(1)}, f32[16,512]{1,0:T(8,128)S(1)}, u32[]{:S(2)}, u32[]{:S(2)}) collective-permute-start(f32[16,512]{1,0:T(8,128)S(1)} %stats.1), channel_id=1, source_target_pairs={{0,32},{32,0},{1,33},{33,1},{2,34},{34,2},{3,35},{35,3},{4,36},{36... | collective-permute-start | bytes 98312 | tf_op jit(solution)/shard_map/ppermute | solution.py:225
  67.7 65.7 %all-to-all-start.1 = ((bf16[16,128,256]{2,1,0:T(8,128)(2,1)}), bf16[16,128,256]{2,1,0:T(8,128)(2,1)S(1)}, u32[]{:S(2)}, u32[]{:S(2)}) async-start(bf16[16,128,256]{2,1,0:T(8,128)(2,1)} %get-tuple-element.10), calls=%async_computation.1 | async-start | bytes 2097152 | tf_op jit(solution)/shard_map/all_to_all | solution.py:289
  82.7 56.1 %collective-permute-start.3 = (bf16[1024,256]{0,1:T(8,128)(2,1)S(1)}, bf16[1024,256]{0,1:T(8,128)(2,1)}, u32[]{:S(2)}, u32[]{:S(2)}) collective-permute-start(bf16[1024,256]{0,1:T(8,128)(2,1)S(1)} %bitcast.48), channel_id=1, source_target_pairs={{0,2},{2,0},{1,3},{3,1},{4,6},{6,4},{5,7},{7,5},{8,10},{10,8},{9,1... | collective-permute-start | bytes 1572872 | tf_op jit(solution)/shard_map/ppermute | solution.py:225
  134.4 19.3 %all-to-all-start.3 = ((bf16[8,128,256]{2,1,0:T(8,128)(2,1)}), bf16[8,128,256]{2,1,0:T(8,128)(2,1)S(1)}, u32[]{:S(2)}, u32[]{:S(2)}) async-start(bf16[8,128,256]{2,1,0:T(8,128)(2,1)} %broadcast_in_dim.59), calls=%async_computation.3 | async-start | bytes 1048576 | tf_op jit(solution)/shard_map/all_to_all | solution.py:293
  140.0 15.2 %collective-permute-start.4 = (bf16[2,1024,256]{1,2,0:T(8,128)(2,1)S(1)}, bf16[2,1024,256]{1,2,0:T(8,128)(2,1)}, u32[]{:S(2)}, u32[]{:S(2)}) collective-permute-start(bf16[2,1024,256]{1,2,0:T(8,128)(2,1)S(1)} %pad_maximum_fusion), channel_id=1, source_target_pairs={{0,1},{1,0},{2,3},{3,2},{4,5},{5,4},{6,7},{7,6},{8,9},{9,8},{10,11... | collective-permute-start | bytes 3145736 | tf_op jit(solution)/shard_map/ppermute | solution.py:225
  157.9 23.1 %all-to-all-start.4 = ((bf16[4,256,256]{2,1,0:T(8,128)(2,1)}), bf16[4,256,256]{2,1,0:T(8,128)(2,1)S(1)}, u32[]{:S(2)}, u32[]{:S(2)}) async-start(bf16[4,256,256]{2,1,0:T(8,128)(2,1)} %bitcast.23), calls=%async_computation.4 | async-start | bytes 1048576 | tf_op jit(solution)/shard_map/all_to_all | solution.py:310
  167.3 18.0 %collective-permute-start.2 = (bf16[128,1024]{1,0:T(8,128)(2,1)S(1)}, bf16[128,1024]{1,0:T(8,128)(2,1)S(1)}, u32[]{:S(2)}, u32[]{:S(2)}) collective-permute-start(bf16[128,1024]{1,0:T(8,128)(2,1)S(1)} %get-tuple-element.9), channel_id=1, source_target_pairs={{0,32},{32,0},{1,33},{33,1},{2,34},{34,2},{3,35},{35,3},{4,36},{36... | collective-permute-start | bytes 786440 | tf_op jit(solution)/shard_map/ppermute | solution.py:225
  181.8 10.7 %all-to-all-start.5 = ((bf16[4,256,256]{2,1,0:T(8,128)(2,1)}), bf16[4,256,256]{2,1,0:T(8,128)(2,1)S(1)}, u32[]{:S(2)}, u32[]{:S(2)}) async-start(bf16[4,256,256]{2,1,0:T(8,128)(2,1)} %broadcast_in_dim.60), calls=%async_computation.5 | async-start | bytes 1048576 | tf_op jit(solution)/shard_map/all_to_all | solution.py:312

commit v2 on v1

--- a/solution.py
+++ b/solution.py
@@ -1,5 +1,3 @@
-import functools
-
 import jax
 import jax.numpy as jnp
 from jax import lax
@@ -221,6 +219,66 @@
     )(meta, qmeta, own, other, kv, stats, far)
 
 
+def reduce_copies_kernel(parts, copies, *halves):
+    total = parts[0].astype(jnp.float32)
+    for part in range(1, parts.shape[0]):
+        total += parts[part].astype(jnp.float32)
+    rounded = total.astype(copies.dtype)
+    for copy in range(copies.shape[0]):
+        copies[copy] = rounded
+    for place, half in enumerate(halves):
+        half[...] = rounded[:, place * HEAD:(place + 1) * HEAD]
+
+
+def reduce_copies(parts, count, dtype, split, name):
+    height, width = parts.shape[1:]
+    halves = [jax.ShapeDtypeStruct((height, HEAD), dtype)] * (2 if split else 0)
+    return pl.pallas_call(
+        reduce_copies_kernel,
+        out_shape=[jax.ShapeDtypeStruct((count, height, width), dtype)] + halves,
+        in_specs=[pl.BlockSpec(memory_space=pltpu.VMEM)],
+        out_specs=[pl.BlockSpec(memory_space=pltpu.VMEM)] * (1 + len(halves)),
+        compiler_params=pltpu.CompilerParams(vmem_limit_bytes=VMEM_LIMIT),
+        cost_estimate=pl.CostEstimate(flops=10**6, bytes_accessed=2 * 10**6, transcendentals=0),
+        name=name,
+    )(parts)
+
+
+def weights_kernel(place, *refs):
+    arrays, grads, out = refs[:-2], refs[-2], refs[-1]
+    count = grads.shape[0] // 2
+    rows = out.shape[1]
+    slots = out.shape[0] // 2
+    sources = [lax.rem(place[0] - back + count, count) * 2 for back in range(count)]
+    here, there = place[2], 1 - place[2]
+    right = jnp.concatenate([grads[s + here] for s in sources] + [grads[s + there] for s in sources], axis=0)
+    each = len(arrays) // 2
+    for high in range(2):
+        blocks = [ref[i] for ref in arrays[high * each:(high + 1) * each] for i in range(ref.shape[0])]
+        result = nn(jnp.concatenate(blocks, axis=1), right).astype(jnp.bfloat16)
+        block = lax.bitwise_xor(place[1], high)
+        for slot in range(slots):
+            out[block * slots + slot] = result[slot * rows:(slot + 1) * rows]
+
+
+def weights_call(place, arrays, grads, slots):
+    rows = arrays[0].shape[1] // slots
+    return pl.pallas_call(
+        weights_kernel,
+        out_shape=jax.ShapeDtypeStruct((2 * slots, rows, grads.shape[2]), jnp.bfloat16),
+        in_specs=in_vmem(1 + len(arrays)),
+        out_specs=pl.BlockSpec(memory_space=pltpu.VMEM),
+        compiler_params=pltpu.CompilerParams(vmem_limit_bytes=VMEM_LIMIT),
+        cost_estimate=pl.CostEstimate(flops=10**9, bytes_accessed=4 * 10**6, transcendentals=0),
+        name="weights",
+    )(place, *arrays, grads)
+
+
+def around(array, axis, by):
+    size = lax.axis_size(axis)
+    return lax.ppermute(array, axis, [(i, (i + by) % size) for i in range(size)])
+
+
 def swapped(array, axis):
     return lax.ppermute(array, axis, [(0, 1), (1, 0)])
 
@@ -273,53 +331,52 @@
     q_start = doc_start(q_pos)
     qmeta = jnp.tile(jnp.concatenate([q_pos, q_start], axis=0), (1, heads))
 
+    other, features = lax.optimization_barrier((other, normed_input))
+    copies_of = lax.axis_size("dp")
+    replica = lax.axis_index("dp")
+    rows = normed_input.shape[2] // (depth * copies_of)
+    slabs = features[0].reshape(height, depth, copies_of, rows).transpose(2, 1, 3, 0)
+    slabs = slabs.reshape(copies_of, depth * rows, height)
+    columns = []
+    for by in range(copies_of):
+        place = lax.rem(replica + by, copies_of)
+        slab = lax.dynamic_index_in_dim(slabs, place, 0, keepdims=False)
+        columns.append(
+            lax.ppermute(
+                slab,
+                ("dp", "yb", "core"),
+                [
+                    (d * 4 + b * 2 + c, (d + by) % copies_of * 4 + c * 2 + b)
+                    for d in range(copies_of) for b in range(2) for c in range(2)
+                ],
+            )
+        )
+    half = copies_of // 2
+    near = jnp.stack(columns[:half]), jnp.stack(columns[half:])
+
+    beside_a = swapped(near[0], "yh")
     stats = stats_call(meta, qmeta, own, other, kv)
+    stats, near_b = lax.optimization_barrier((stats, near[1]))
+    beside_b = swapped(near_b, "yh")
     far = swapped(stats, "yb")
-
-    width = normed_input.shape[2] // depth
-    columns = lax.all_to_all(
-        normed_input[0].reshape(height, depth, width), "z", split_axis=1, concat_axis=0, tiled=True
-    ).reshape(depth * height, width)
-    beside = swapped(columns, "yh")
-    both = jnp.stack([columns, beside])
-    across = swapped(both, "core")
-
+    far, beside_a = lax.optimization_barrier((far, beside_a))
     dq_own, dq_other, dkv = grad_call(meta, qmeta, own, other, kv, stats, far)
+    dkv, beside_b = lax.optimization_barrier((dkv, beside_b))
+    near, beside = [near[0], near_b], [beside_a, beside_b]
     dq_far = swapped(dq_other, "yb")
+    across = [swapped(part, "core") for part in (*near, *beside)]
     parts = lax.all_to_all(dkv, group, 0, 0, tiled=True)
-    own_grads = jnp.sum(parts.astype(jnp.float32), axis=0).astype(jnp.bfloat16)
+    parts, across, dq_far = lax.optimization_barrier((parts, across, dq_far))
+    copies, key_grad, value_grad = reduce_copies(parts, 2 * copies_of, jnp.bfloat16, True, "sum_grads")
     query_grad = (dq_own + dq_far.astype(jnp.float32)).astype(jnp.bfloat16)[None]
 
-    all_grads = lax.all_to_all(
-        jnp.broadcast_to(own_grads[None], (depth,) + own_grads.shape), "z", 0, 0, tiled=True
-    ).reshape(depth * height, 2 * HEAD)
-
-    def weights(features):
-        return lax.dot_general(
-            features, all_grads, (((1,), (0,)), ((), ())), preferred_element_type=jnp.float32
-        )
-
-    near = weights(both)
-    far_weights = weights(across)
-    core, high = lax.axis_index("core"), lax.axis_index("yh")
-    by_core = jnp.where(
-        core == 0, jnp.stack([near, far_weights], axis=1), jnp.stack([far_weights, near], axis=1)
-    )
-    by_high = jnp.where(high == 0, by_core, by_core[::-1]).astype(jnp.bfloat16)
-    blocks = by_high.reshape((4,) + by_high.shape[2:])
-    pieces = lax.all_to_all(blocks, ("ya", "yb"), 0, 0, tiled=True)
-    partial = jnp.sum(pieces.astype(jnp.float32), axis=0).astype(jnp.bfloat16)
-    spread = lax.all_to_all(
-        jnp.broadcast_to(partial[None], (lax.axis_size("dp"),) + partial.shape), "dp", 0, 0, tiled=True
-    )
-    weight_total = jnp.sum(spread.astype(jnp.float32), axis=0)
-    return (
-        query_grad,
-        own_grads[None, :, :HEAD],
-        own_grads[None, :, HEAD:],
-        weight_total[:, :HEAD],
-        weight_total[:, HEAD:],
-    )
+    all_grads = lax.all_to_all(copies, ("dp", "yb"), 0, 0, tiled=True)
+    place = jnp.stack([replica, lax.axis_index("yh"), lax.axis_index("core")]).astype(jnp.int32)
+    blocks = weights_call(place, (*near, *across[:2], *beside, *across[2:]), all_grads, depth)
+    pieces = lax.all_to_all(blocks, group, 0, 0, tiled=True)
+    (spread,) = reduce_copies(pieces, copies_of, jnp.float32, False, "sum_rows")
+    weight = lax.all_to_all(spread, "dp", 0, 0, tiled=True).reshape(copies_of * rows, 2 * HEAD)
+    return (query_grad, key_grad[None], value_grad[None], weight[:, :HEAD], weight[:, HEAD:])
 
 
 def solution(mesh):

time: 195 us -> 170 us (0.87)
  waiting for transfers between devices: 94.7 us -> 45.1 us
  blocking collectives: 0 us -> 24.6 us
  starting transfers between devices: 64.5 us -> 68.9 us
  matrix products: 3.14 us -> 0 us
  other arithmetic: 6.25 us -> 3.99 us
    all_to_all x1, waiting for transfers between devices: 48.3 us -> 8.59 us  [shards(): parts = lax.all_to_all(dkv, group, 0, 0, tiled=True)]
    all_to_all x0 -> x1, blocking collectives: none -> 24.6 us  [shards(): pieces = lax.all_to_all(blocks, group, 0, 0, tiled=True)]
    all_to_all x1, waiting for transfers between devices: 18.2 us -> 0.01 us  [shards(): lax.all_to_all(jnp.broadcast_to(pair[None], (group_size,) + pair.shape),...]
    ppermute x0 -> x4, starting transfers between devices: none -> 15.1 us  [shards(): lax.ppermute(slab, ('dp', 'yb', 'core'), [(d * 4 + b * 2 + c, (d + by) %...]
    all_to_all x4 -> x2, starting transfers between devices: 21.6 us -> 7.03 us  [the longest x1 3.54 us: shards(): lax.all_to_all(spread, 'dp', 0, 0, tiled=True)]
    ppermute x5 -> x9, starting transfers between devices: 15.2 us -> 28.1 us  [swapped(): return lax.ppermute(array, axis, [(0, 1), (1, 0)])]
    all_to_all x4 -> x2, waiting for transfers between devices: 25.2 us -> 14.1 us  [the longest x1 9.22 us: shards(): all_grads = lax.all_to_all(copies, ('dp', 'yb'), 0, 0, tiled=True)]
    ppermute x0 -> x4, waiting for transfers between devices: none -> 9.99 us  [shards(): lax.ppermute(slab, ('dp', 'yb', 'core'), [(d * 4 + b * 2 + c, (d + by) %...]
  transfers between devices with their start and end apart: 11 -> 17, of which waited for: 6 -> 7; matrix products, arithmetic and copies ran while one was open for 6% -> 4% of each run, Pallas kernels for 7% -> 7%
where the time goes in v2:
time: 170 us; the launch traced here: 169 us
  starting transfers between devices  68.9 us (41%)
  waiting for transfers between devices  45.1 us (27%)
  blocking collectives  24.6 us (14%)
  Pallas kernels  15.1 us (9%)
  local copies, waits for them, and re-layouts  8.81 us (5%)
  other arithmetic  3.99 us (2%)
  between operations  2.37 us (1%)
    ppermute x9, starting transfers between devices, swapped(): return lax.ppermute(array, axis, [(0, 1), (1, 0)])  28.1 us
    all_to_all x1, blocking collectives, shards(): pieces = lax.all_to_all(blocks, group, 0, 0, tiled=True)  24.6 us
    ppermute x4, starting transfers between devices, shards(): lax.ppermute(slab, ('dp', 'yb', 'core'), [(d * 4 + b * 2 + c, (d + by) %...  15.1 us
    ppermute x9, waiting for transfers between devices, swapped(): return lax.ppermute(array, axis, [(0, 1), (1, 0)])  12.4 us
    all_to_all x1, starting transfers between devices, shards(): lax.all_to_all(jnp.broadcast_to(pair[None], (group_size,) + pair.shape),...  12.3 us
    ppermute x4, waiting for transfers between devices, shards(): lax.ppermute(slab, ('dp', 'yb', 'core'), [(d * 4 + b * 2 + c, (d + by) %...  9.99 us
    all_to_all x1, waiting for transfers between devices, shards(): all_grads = lax.all_to_all(copies, ('dp', 'yb'), 0, 0, tiled=True)  9.22 us
    all_to_all x1, waiting for transfers between devices, shards(): parts = lax.all_to_all(dkv, group, 0, 0, tiled=True)  8.59 us
  transfers between devices with their start and end apart: 17, of which 7 were waited for; matrix products, arithmetic and copies ran while one was open for 4% of the time, Pallas kernels for 7%

profile of v2, /device:TPU:1, one launch (start us, length us, event | category | flops | bytes accessed | tf_op | source)
XLA Modules:
  0.0 168.9 jit_solution(5157403774367921474)
XLA Ops:
  0.6 1.0 constant_dynamic-update-slice_fusion.1
  1.7 0.0 copy-done.5
  1.7 0.0 copy-start.8
  1.7 0.0 copy-start.9
  1.7 4.0 %collective-permute-start = (bf16[2,128,1024]{2,1,0:T(8,128)(2,1)S(1)}, bf16[2,128,1024]{2,1,0:T(8,128)(2,1)S(1)}, u32[]{:S(2)}, u32[]{:S(2)}) collective-permute-start(bf16[2,128,1024]{2,1,0:T(8,128)(2,1)S(1)} %constant_dynamic-update-slice_fusion.own), channel_id=1, source_target_pairs={{0,32},{32,0},{1,33},{33,1},{2,34},{34,2},{3,35},{35,3},{4,36},{36... | collective-permute-start | bytes 1572872 | tf_op jit(solution)/shard_map/ppermute | solution.py:283
  5.8 1.1 broadcast_in_dim.43
  6.9 12.3 %all-to-all-start = ((bf16[16,128,256]{2,1,0:T(8,128)(2,1)}), bf16[16,128,256]{2,1,0:T(8,128)(2,1)S(1)}, u32[]{:S(2)}, u32[]{:S(2)}) async-start(bf16[16,128,256]{2,1,0:T(8,128)(2,1)} %broadcast_in_dim.43), calls=%async_computation | async-start | bytes 2097152 | tf_op jit(solution)/shard_map/all_to_all | solution.py:325
  19.2 0.0 copy-start.10
  19.2 0.6 copy-done.10
  19.9 0.1 reshape.165
  19.9 0.6 fusion.2
  20.6 0.1 select_n.68
  22.0 0.0 copy-start.11
  22.0 0.6 copy-done.11
  22.7 0.2 reduce-window.8
  22.9 0.1 copy.22
  22.9 0.1 lt.41
  23.0 1.4 broadcast_multiply_fusion
  24.4 0.1 iota_add_fusion
  24.5 0.1 select_reduce_fusion
  24.6 0.2 select_reduce_fusion.1
  24.8 0.2 convert_reduce_fusion
  25.0 0.2 convert_reduce_fusion.2
  25.2 0.0 collective-permute-done.other
  25.2 0.3 copy.24
  25.6 0.7 dynamic-slice_bitcast_fusion.1
  26.3 3.2 %collective-permute-start.4 = (bf16[512,128]{1,0:T(8,128)(2,1)S(1)}, bf16[512,128]{1,0:T(8,128)(2,1)S(1)}, u32[]{:S(2)}, u32[]{:S(2)}) collective-permute-start(bf16[512,128]{1,0:T(8,128)(2,1)S(1)} %get-tuple-element.51), channel_id=1, source_target_pairs={{0,0},{1,32},{32,1},{33,33},{128,128},{129,160},{160,129},{161,161... | collective-permute-start | bytes 393224 | tf_op jit(solution)/shard_map/ppermute | solution.py:345
  29.5 3.3 %collective-permute-start.5 = (bf16[512,128]{1,0:T(8,128)(2,1)S(1)}, bf16[512,128]{1,0:T(8,128)(2,1)S(1)}, u32[]{:S(2)}, u32[]{:S(2)}) collective-permute-start(bf16[512,128]{1,0:T(8,128)(2,1)S(1)} %get-tuple-element.52), channel_id=1, source_target_pairs={{0,128},{1,160},{32,129},{33,161},{128,256},{129,288},{160,257},{1... | collective-permute-start | bytes 393224 | tf_op jit(solution)/shard_map/ppermute | solution.py:345
  32.8 0.1 add_bitcast_fusion
  32.9 0.1 broadcast_in_dim_reshape.2
  33.0 5.4 %collective-permute-start.1 = (bf16[512,128]{1,0:T(8,128)(2,1)}, bf16[512,128]{1,0:T(8,128)(2,1)S(1)}, u32[]{:S(2)}, u32[]{:S(2)}) collective-permute-start(bf16[512,128]{1,0:T(8,128)(2,1)} %get-tuple-element.54), channel_id=1, source_target_pairs={{0,256},{1,288},{32,257},{33,289},{128,384},{129,416},{160,385},{1... | collective-permute-start | bytes 393224 | tf_op jit(solution)/shard_map/ppermute | solution.py:345
  38.3 3.2 %collective-permute-start.2 = (bf16[512,128]{1,0:T(8,128)(2,1)}, bf16[512,128]{1,0:T(8,128)(2,1)S(1)}, u32[]{:S(2)}, u32[]{:S(2)}) collective-permute-start(bf16[512,128]{1,0:T(8,128)(2,1)} %get-tuple-element.53), channel_id=1, source_target_pairs={{0,384},{1,416},{32,385},{33,417},{128,0},{129,32},{160,1},{161,33... | collective-permute-start | bytes 393224 | tf_op jit(solution)/shard_map/ppermute | solution.py:345
  41.6 0.1 tile.10.qmeta
  41.7 5.8 %collective-permute-start.6 = (bf16[2,512,128]{2,1,0:T(8,128)(2,1)S(1)}, bf16[2,512,128]{2,1,0:T(8,128)(2,1)S(1)}, u32[]{:S(2)}, u32[]{:S(2)}) collective-permute-start(bf16[2,512,128]{2,1,0:T(8,128)(2,1)S(1)} %pad_maximum_fusion.1.refs_0_), channel_id=1, source_target_pairs={{0,2},{2,0},{1,3},{3,1},{4,6},{6,4},{5,7},{7,5},{8,10},{10,8},{9,1... | collective-permute-start | bytes 786440 | tf_op jit(solution)/shard_map/ppermute | solution.py:283
  47.6 8.2 %collective-permute-done.1 = bf16[512,128]{1,0:T(8,128)(2,1)S(1)} collective-permute-done((bf16[512,128]{1,0:T(8,128)(2,1)}, bf16[512,128]{1,0:T(8,128)(2,1)S(1)}, u32[]{:S(2)}, u32[]{:S(2)}) %collective-permute-start.1) | collective-permute-done | bytes 131104 | tf_op jit(solution)/shard_map/ppermute | solution.py:345
  55.7 1.8 %collective-permute-done.2 = bf16[512,128]{1,0:T(8,128)(2,1)S(1)} collective-permute-done((bf16[512,128]{1,0:T(8,128)(2,1)}, bf16[512,128]{1,0:T(8,128)(2,1)S(1)}, u32[]{:S(2)}, u32[]{:S(2)}) %collective-permute-start.2) | collective-permute-done | bytes 131104 | tf_op jit(solution)/shard_map/ppermute | solution.py:345
  57.6 4.3 %stats.1 = f32[16,512]{1,0:T(8,128)S(1)} custom-call(s32[3,32]{1,0:T(4,128)S(1)} %pad_add_fusion.1.meta, s32[8,512]{1,0:T(8,128)S(1)} %tile.10.qmeta, bf16[2,128,1024]{2,1,0:T(8,128)(2,1)S(1)} %constant_dynamic-update-slice_fusion.own, bf16[2,128,1024]{2,1,0:T(8,128)(2,1)S(1)} %collective-permute-done.other, bf16[16,128,256]{2,1,0:T(8,128)(2,1)S(1)} %all-to-all-done.kv), custom_call_target="tpu_custom_call" | custom-call | flops 2000000000 | bytes 4000000 | tf_op jit(solution)/shard_map/stats/pallas_call | solution.py:184
  61.9 1.9 %collective-permute-start.3 = (f32[16,512]{1,0:T(8,128)S(1)}, f32[16,512]{1,0:T(8,128)S(1)}, u32[]{:S(2)}, u32[]{:S(2)}) collective-permute-start(f32[16,512]{1,0:T(8,128)S(1)} %stats.1), channel_id=1, source_target_pairs={{0,32},{32,0},{1,33},{33,1},{2,34},{34,2},{3,35},{35,3},{4,36},{36... | collective-permute-start | bytes 98312 | tf_op jit(solution)/shard_map/ppermute | solution.py:283
  63.8 5.7 %collective-permute-start.7 = (bf16[2,512,128]{2,1,0:T(8,128)(2,1)S(1)}, bf16[2,512,128]{2,1,0:T(8,128)(2,1)S(1)}, u32[]{:S(2)}, u32[]{:S(2)}) collective-permute-start(bf16[2,512,128]{2,1,0:T(8,128)(2,1)S(1)} %pad_maximum_fusion.refs_1_), channel_id=1, source_target_pairs={{0,2},{2,0},{1,3},{3,1},{4,6},{6,4},{5,7},{7,5},{8,10},{10,8},{9,1... | collective-permute-start | bytes 786440 | tf_op jit(solution)/shard_map/ppermute | solution.py:283
  69.5 7.9 %grads.1 = (f32[128,1024]{1,0:T(8,128)S(1)}, bf16[128,1024]{1,0:T(8,128)(2,1)}, bf16[16,128,256]{2,1,0:T(8,128)(2,1)}) custom-call(s32[3,32]{1,0:T(4,128)S(1)} %pad_add_fusion.1.meta, s32[8,512]{1,0:T(8,128)S(1)} %tile.10.qmeta, bf16[2,128,1024]{2,1,0:T(8,128)(2,1)S(1)} %constant_dynamic-update-slice_fusion.own, ...), custom_call_target="tpu_custom_call" | custom-call | flops 5000000000 | bytes 6000000 | tf_op jit(solution)/shard_map/grads/pallas_call | solution.py:200
  77.4 4.0 %collective-permute-done.7.refs_5_ = bf16[2,512,128]{2,1,0:T(8,128)(2,1)S(1)} collective-permute-done((bf16[2,512,128]{2,1,0:T(8,128)(2,1)S(1)}, bf16[2,512,128]{2,1,0:T(8,128)(2,1)S(1)}, u32[]{:S(2)}, u32[]{:S(2)}) %collective-permute-start.7) | collective-permute-done | bytes 262176 | tf_op jit(solution)/shard_map/ppermute | solution.py:283
  81.4 0.7 copy-done
  82.2 6.5 %all-to-all-start.1 = ((bf16[16,128,256]{2,1,0:T(8,128)(2,1)}), bf16[16,128,256]{2,1,0:T(8,128)(2,1)S(1)}, u32[]{:S(2)}, u32[]{:S(2)}) async-start(bf16[16,128,256]{2,1,0:T(8,128)(2,1)} %get-tuple-element.32), calls=%async_computation.1 | async-start | bytes 2097152 | tf_op jit(solution)/shard_map/all_to_all | solution.py:368
  88.6 2.3 %collective-permute-start.8 = (bf16[2,512,128]{2,1,0:T(8,128)(2,1)S(1)}, bf16[2,512,128]{2,1,0:T(8,128)(2,1)S(1)}, u32[]{:S(2)}, u32[]{:S(2)}) collective-permute-start(bf16[2,512,128]{2,1,0:T(8,128)(2,1)S(1)} %pad_maximum_fusion.1.refs_0_), channel_id=1, source_target_pairs={{0,1},{1,0},{2,3},{3,2},{4,5},{5,4},{6,7},{7,6},{8,9},{9,8},{10,11... | collective-permute-start | bytes 786440 | tf_op jit(solution)/shard_map/ppermute | solution.py:283
  91.0 2.0 %collective-permute-start.9 = (bf16[2,512,128]{2,1,0:T(8,128)(2,1)S(1)}, bf16[2,512,128]{2,1,0:T(8,128)(2,1)S(1)}, u32[]{:S(2)}, u32[]{:S(2)}) collective-permute-start(bf16[2,512,128]{2,1,0:T(8,128)(2,1)S(1)} %pad_maximum_fusion.refs_1_), channel_id=1, source_target_pairs={{0,1},{1,0},{2,3},{3,2},{4,5},{5,4},{6,7},{7,6},{8,9},{9,8},{10,11... | collective-permute-start | bytes 786440 | tf_op jit(solution)/shard_map/ppermute | solution.py:283
  93.0 1.9 %collective-permute-start.12 = (bf16[128,1024]{1,0:T(8,128)(2,1)}, bf16[128,1024]{1,0:T(8,128)(2,1)S(1)}, u32[]{:S(2)}, u32[]{:S(2)}) collective-permute-start(bf16[128,1024]{1,0:T(8,128)(2,1)} %get-tuple-element.35), channel_id=1, source_target_pairs={{0,32},{32,0},{1,33},{33,1},{2,34},{34,2},{3,35},{35,3},{4,36},{36... | collective-permute-start | bytes 786440 | tf_op jit(solution)/shard_map/ppermute | solution.py:283
  94.9 2.3 %collective-permute-start.10 = (bf16[2,512,128]{2,1,0:T(8,128)(2,1)S(1)}, bf16[2,512,128]{2,1,0:T(8,128)(2,1)S(1)}, u32[]{:S(2)}, u32[]{:S(2)}) collective-permute-start(bf16[2,512,128]{2,1,0:T(8,128)(2,1)S(1)} %collective-permute-done.6.refs_4_), channel_id=1, source_target_pairs={{0,1},{1,0},{2,3},{3,2},{4,5},{5,4},{6,7},{7,6},{8,9},{9,8},{10,11... | collective-permute-start | bytes 786440 | tf_op jit(solution)/shard_map/ppermute | solution.py:283
  97.3 2.0 %collective-permute-start.11 = (bf16[2,512,128]{2,1,0:T(8,128)(2,1)S(1)}, bf16[2,512,128]{2,1,0:T(8,128)(2,1)S(1)}, u32[]{:S(2)}, u32[]{:S(2)}) collective-permute-start(bf16[2,512,128]{2,1,0:T(8,128)(2,1)S(1)} %copy-done.1), channel_id=1, source_target_pairs={{0,1},{1,0},{2,3},{3,2},{4,5},{5,4},{6,7},{7,6},{8,9},{9,8},{10,11... | collective-permute-start | bytes 786440 | tf_op jit(solution)/shard_map/ppermute | solution.py:283
  99.3 8.4 %collective-permute-done.12 = bf16[128,1024]{1,0:T(8,128)(2,1)S(1)} collective-permute-done((bf16[128,1024]{1,0:T(8,128)(2,1)}, bf16[128,1024]{1,0:T(8,128)(2,1)S(1)}, u32[]{:S(2)}, u32[]{:S(2)}) %collective-permute-start.12) | collective-permute-done | bytes 262176 | tf_op jit(solution)/shard_map/ppermute | solution.py:283
  107.7 0.7 copy-done.6
  108.4 0.7 copy-done.2
  109.1 8.6 %all-to-all-done.1.parts = bf16[16,128,256]{2,1,0:T(8,128)(2,1)S(1)} async-done(((bf16[16,128,256]{2,1,0:T(8,128)(2,1)}), bf16[16,128,256]{2,1,0:T(8,128)(2,1)S(1)}, u32[]{:S(2)}, u32[]{:S(2)}) %all-to-all-start.1) | async-done | bytes 1048608 | tf_op jit(solution)/shard_map/all_to_all | solution.py:368
  117.7 0.9 sum_grads.1
  118.6 3.5 %all-to-all-start.2 = ((bf16[8,128,256]{2,1,0:T(8,128)(2,1)}), bf16[8,128,256]{2,1,0:T(8,128)(2,1)S(1)}, u32[]{:S(2)}, u32[]{:S(2)}) async-start(bf16[8,128,256]{2,1,0:T(8,128)(2,1)} %get-tuple-element.44), calls=%async_computation.2 | async-start | bytes 1048576 | tf_op jit(solution)/shard_map/all_to_all | solution.py:373
  122.1 0.1 pad_add_fusion.4.place
  122.2 9.2 %all-to-all-done.2.refs_8_ = bf16[8,128,256]{2,1,0:T(8,128)(2,1)S(1)} async-done(((bf16[8,128,256]{2,1,0:T(8,128)(2,1)}), bf16[8,128,256]{2,1,0:T(8,128)(2,1)S(1)}, u32[]{:S(2)}, u32[]{:S(2)}) %all-to-all-start.2) | async-done | bytes 524320 | tf_op jit(solution)/shard_map/all_to_all | solution.py:373
  131.4 0.9 copy-done.3
  132.4 1.3 weights.1
  133.7 24.6 %all_to_all.25.parts = bf16[16,64,256]{2,1,0:T(8,128)(2,1)S(1)} all-to-all(bf16[16,64,256]{2,1,0:T(8,128)(2,1)S(1)} %weights.1), channel_id=1, replica_groups=mesh['dp'=4,'ya'=2,'yb'=2,'z'=8,'yh'=2,'core'=2] {'ya','z'}, dimensions={0} | all-to-all | bytes 1048576 | tf_op jit(solution)/shard_map/all_to_all | solution.py:376
  158.2 0.8 sum_rows.1
  159.0 3.5 %all-to-all-start.4 = ((f32[4,64,256]{2,1,0:T(8,128)}), f32[4,64,256]{2,1,0:T(8,128)S(1)}, u32[]{:S(2)}, u32[]{:S(2)}) async-start(f32[4,64,256]{2,1,0:T(8,128)} %sum_rows.1), calls=%async_computation.4 | async-start | bytes 524288 | tf_op jit(solution)/shard_map/all_to_all | solution.py:378
  162.6 0.8 fusion
  163.3 4.9 %all-to-all-done.4 = f32[4,64,256]{2,1,0:T(8,128)S(1)} async-done(((f32[4,64,256]{2,1,0:T(8,128)}), f32[4,64,256]{2,1,0:T(8,128)S(1)}, u32[]{:S(2)}, u32[]{:S(2)}) %all-to-all-start.4) | async-done | bytes 262176 | tf_op jit(solution)/shard_map/all_to_all | solution.py:378
  168.2 0.7 fusion.4
  (36 shorter events, 0.3 us)
Async XLA Ops:
  0.6 1.0 copy-start.5
  1.7 4.1 %copy-start.8 = (bf16[1,128,128]{2,1,0:T(8,128)(2,1)S(1)}, bf16[1,128,128]{2,1,0:T(8,128)(2,1)}, u32[]{:S(2)}) copy-start(bf16[1,128,128]{2,1,0:T(8,128)(2,1)} %param.9) | copy-start | bytes 98308
  1.7 4.1 %copy-start.9 = (bf16[1,128,128]{2,1,0:T(8,128)(2,1)S(1)}, bf16[1,128,128]{2,1,0:T(8,128)(2,1)}, u32[]{:S(2)}) copy-start(bf16[1,128,128]{2,1,0:T(8,128)(2,1)} %param.8) | copy-start | bytes 98308
  1.7 23.5 %collective-permute-start = (bf16[2,128,1024]{2,1,0:T(8,128)(2,1)S(1)}, bf16[2,128,1024]{2,1,0:T(8,128)(2,1)S(1)}, u32[]{:S(2)}, u32[]{:S(2)}) collective-permute-start(bf16[2,128,1024]{2,1,0:T(8,128)(2,1)S(1)} %constant_dynamic-update-slice_fusion.own), channel_id=1, source_target_pairs={{0,32},{32,0},{1,33},{33,1},{2,34},{34,2},{3,35},{35,3},{4,36},{36... | collective-permute-start | bytes 1572872 | tf_op jit(solution)/shard_map/ppermute | solution.py:283
  6.9 18.3 %copy-start.4 = (bf16[1,128,2048]{2,1,0:T(8,128)(2,1)S(1)}, bf16[1,128,2048]{2,1,0:T(8,128)(2,1)}, u32[]{:S(2)}) copy-start(bf16[1,128,2048]{2,1,0:T(8,128)(2,1)} %param.11) | copy-start | bytes 1572868
  6.9 50.7 %all-to-all-start = ((bf16[16,128,256]{2,1,0:T(8,128)(2,1)}), bf16[16,128,256]{2,1,0:T(8,128)(2,1)S(1)}, u32[]{:S(2)}, u32[]{:S(2)}) async-start(bf16[16,128,256]{2,1,0:T(8,128)(2,1)} %broadcast_in_dim.43), calls=%async_computation | async-start | bytes 2097152 | tf_op jit(solution)/shard_map/all_to_all | solution.py:325
  19.2 0.7 copy-start.10
  22.0 0.7 copy-start.11
  26.3 15.4 %collective-permute-start.4 = (bf16[512,128]{1,0:T(8,128)(2,1)S(1)}, bf16[512,128]{1,0:T(8,128)(2,1)S(1)}, u32[]{:S(2)}, u32[]{:S(2)}) collective-permute-start(bf16[512,128]{1,0:T(8,128)(2,1)S(1)} %get-tuple-element.51), channel_id=1, source_target_pairs={{0,0},{1,32},{32,1},{33,33},{128,128},{129,160},{160,129},{161,161... | collective-permute-start | bytes 393224 | tf_op jit(solution)/shard_map/ppermute | solution.py:345
  29.5 12.2 %collective-permute-start.5 = (bf16[512,128]{1,0:T(8,128)(2,1)S(1)}, bf16[512,128]{1,0:T(8,128)(2,1)S(1)}, u32[]{:S(2)}, u32[]{:S(2)}) collective-permute-start(bf16[512,128]{1,0:T(8,128)(2,1)S(1)} %get-tuple-element.52), channel_id=1, source_target_pairs={{0,128},{1,160},{32,129},{33,161},{128,256},{129,288},{160,257},{1... | collective-permute-start | bytes 393224 | tf_op jit(solution)/shard_map/ppermute | solution.py:345
  33.0 22.8 %collective-permute-start.1 = (bf16[512,128]{1,0:T(8,128)(2,1)}, bf16[512,128]{1,0:T(8,128)(2,1)S(1)}, u32[]{:S(2)}, u32[]{:S(2)}) collective-permute-start(bf16[512,128]{1,0:T(8,128)(2,1)} %get-tuple-element.54), channel_id=1, source_target_pairs={{0,256},{1,288},{32,257},{33,289},{128,384},{129,416},{160,385},{1... | collective-permute-start | bytes 393224 | tf_op jit(solution)/shard_map/ppermute | solution.py:345
  38.3 19.2 %collective-permute-start.2 = (bf16[512,128]{1,0:T(8,128)(2,1)}, bf16[512,128]{1,0:T(8,128)(2,1)S(1)}, u32[]{:S(2)}, u32[]{:S(2)}) collective-permute-start(bf16[512,128]{1,0:T(8,128)(2,1)} %get-tuple-element.53), channel_id=1, source_target_pairs={{0,384},{1,416},{32,385},{33,417},{128,0},{129,32},{160,1},{161,33... | collective-permute-start | bytes 393224 | tf_op jit(solution)/shard_map/ppermute | solution.py:345
  41.7 27.8 %collective-permute-start.6 = (bf16[2,512,128]{2,1,0:T(8,128)(2,1)S(1)}, bf16[2,512,128]{2,1,0:T(8,128)(2,1)S(1)}, u32[]{:S(2)}, u32[]{:S(2)}) collective-permute-start(bf16[2,512,128]{2,1,0:T(8,128)(2,1)S(1)} %pad_maximum_fusion.1.refs_0_), channel_id=1, source_target_pairs={{0,2},{2,0},{1,3},{3,1},{4,6},{6,4},{5,7},{7,5},{8,10},{10,8},{9,1... | collective-permute-start | bytes 786440 | tf_op jit(solution)/shard_map/ppermute | solution.py:283
  61.9 7.6 %collective-permute-start.3 = (f32[16,512]{1,0:T(8,128)S(1)}, f32[16,512]{1,0:T(8,128)S(1)}, u32[]{:S(2)}, u32[]{:S(2)}) collective-permute-start(f32[16,512]{1,0:T(8,128)S(1)} %stats.1), channel_id=1, source_target_pairs={{0,32},{32,0},{1,33},{33,1},{2,34},{34,2},{3,35},{35,3},{4,36},{36... | collective-permute-start | bytes 98312 | tf_op jit(solution)/shard_map/ppermute | solution.py:283
  63.8 17.6 %collective-permute-start.7 = (bf16[2,512,128]{2,1,0:T(8,128)(2,1)S(1)}, bf16[2,512,128]{2,1,0:T(8,128)(2,1)S(1)}, u32[]{:S(2)}, u32[]{:S(2)}) collective-permute-start(bf16[2,512,128]{2,1,0:T(8,128)(2,1)S(1)} %pad_maximum_fusion.refs_1_), channel_id=1, source_target_pairs={{0,2},{2,0},{1,3},{3,1},{4,6},{6,4},{5,7},{7,5},{8,10},{10,8},{9,1... | collective-permute-start | bytes 786440 | tf_op jit(solution)/shard_map/ppermute | solution.py:283
  81.4 0.7 copy-start
  82.2 15.1 %copy-start.1 = (bf16[2,512,128]{2,1,0:T(8,128)(2,1)S(1)}, bf16[2,512,128]{2,1,0:T(8,128)(2,1)}, u32[]{:S(2)}) copy-start(bf16[2,512,128]{2,1,0:T(8,128)(2,1)} %copy-done) | copy-start | bytes 786436
  82.2 35.5 %all-to-all-start.1 = ((bf16[16,128,256]{2,1,0:T(8,128)(2,1)}), bf16[16,128,256]{2,1,0:T(8,128)(2,1)S(1)}, u32[]{:S(2)}, u32[]{:S(2)}) async-start(bf16[16,128,256]{2,1,0:T(8,128)(2,1)} %get-tuple-element.32), calls=%async_computation.1 | async-start | bytes 2097152 | tf_op jit(solution)/shard_map/all_to_all | solution.py:368
  88.6 10.6 %collective-permute-start.8 = (bf16[2,512,128]{2,1,0:T(8,128)(2,1)S(1)}, bf16[2,512,128]{2,1,0:T(8,128)(2,1)S(1)}, u32[]{:S(2)}, u32[]{:S(2)}) collective-permute-start(bf16[2,512,128]{2,1,0:T(8,128)(2,1)S(1)} %pad_maximum_fusion.1.refs_0_), channel_id=1, source_target_pairs={{0,1},{1,0},{2,3},{3,2},{4,5},{5,4},{6,7},{7,6},{8,9},{9,8},{10,11... | collective-permute-start | bytes 786440 | tf_op jit(solution)/shard_map/ppermute | solution.py:283
  91.0 8.3 %collective-permute-start.9 = (bf16[2,512,128]{2,1,0:T(8,128)(2,1)S(1)}, bf16[2,512,128]{2,1,0:T(8,128)(2,1)S(1)}, u32[]{:S(2)}, u32[]{:S(2)}) collective-permute-start(bf16[2,512,128]{2,1,0:T(8,128)(2,1)S(1)} %pad_maximum_fusion.refs_1_), channel_id=1, source_target_pairs={{0,1},{1,0},{2,3},{3,2},{4,5},{5,4},{6,7},{7,6},{8,9},{9,8},{10,11... | collective-permute-start | bytes 786440 | tf_op jit(solution)/shard_map/ppermute | solution.py:283
  93.0 14.7 %collective-permute-start.12 = (bf16[128,1024]{1,0:T(8,128)(2,1)}, bf16[128,1024]{1,0:T(8,128)(2,1)S(1)}, u32[]{:S(2)}, u32[]{:S(2)}) collective-permute-start(bf16[128,1024]{1,0:T(8,128)(2,1)} %get-tuple-element.35), channel_id=1, source_target_pairs={{0,32},{32,0},{1,33},{33,1},{2,34},{34,2},{3,35},{35,3},{4,36},{36... | collective-permute-start | bytes 786440 | tf_op jit(solution)/shard_map/ppermute | solution.py:283
  94.9 12.8 %collective-permute-start.10 = (bf16[2,512,128]{2,1,0:T(8,128)(2,1)S(1)}, bf16[2,512,128]{2,1,0:T(8,128)(2,1)S(1)}, u32[]{:S(2)}, u32[]{:S(2)}) collective-permute-start(bf16[2,512,128]{2,1,0:T(8,128)(2,1)S(1)} %collective-permute-done.6.refs_4_), channel_id=1, source_target_pairs={{0,1},{1,0},{2,3},{3,2},{4,5},{5,4},{6,7},{7,6},{8,9},{9,8},{10,11... | collective-permute-start | bytes 786440 | tf_op jit(solution)/shard_map/ppermute | solution.py:283
  97.3 11.1 %collective-permute-start.11 = (bf16[2,512,128]{2,1,0:T(8,128)(2,1)S(1)}, bf16[2,512,128]{2,1,0:T(8,128)(2,1)S(1)}, u32[]{:S(2)}, u32[]{:S(2)}) collective-permute-start(bf16[2,512,128]{2,1,0:T(8,128)(2,1)S(1)} %copy-done.1), channel_id=1, source_target_pairs={{0,1},{1,0},{2,3},{3,2},{4,5},{5,4},{6,7},{7,6},{8,9},{9,8},{10,11... | collective-permute-start | bytes 786440 | tf_op jit(solution)/shard_map/ppermute | solution.py:283
  107.7 0.7 copy-start.6
  108.4 0.7 copy-start.2
  118.6 12.8 %all-to-all-start.2 = ((bf16[8,128,256]{2,1,0:T(8,128)(2,1)}), bf16[8,128,256]{2,1,0:T(8,128)(2,1)S(1)}, u32[]{:S(2)}, u32[]{:S(2)}) async-start(bf16[8,128,256]{2,1,0:T(8,128)(2,1)} %get-tuple-element.44), calls=%async_computation.2 | async-start | bytes 1048576 | tf_op jit(solution)/shard_map/all_to_all | solution.py:373
  131.4 1.0 copy-start.3
  159.0 3.5 %copy-start.7 = (bf16[128,1024]{1,0:T(8,128)(2,1)S(1)}, bf16[128,1024]{1,0:T(8,128)(2,1)}, u32[]{:S(2)}) copy-start(bf16[128,1024]{1,0:T(8,128)(2,1)} %copy-done.6) | copy-start | bytes 786436
  159.0 9.2 %all-to-all-start.4 = ((f32[4,64,256]{2,1,0:T(8,128)}), f32[4,64,256]{2,1,0:T(8,128)S(1)}, u32[]{:S(2)}, u32[]{:S(2)}) async-start(f32[4,64,256]{2,1,0:T(8,128)} %sum_rows.1), calls=%async_computation.4 | async-start | bytes 524288 | tf_op jit(solution)/shard_map/all_to_all | solution.py:378

commit v3 on v2

--- a/solution.py
+++ b/solution.py
@@ -11,7 +11,9 @@
 SPANS_PER_TILE = TILE // SPAN
 NEG = -1e30
 SCALE = HEAD ** (-0.5)
-VMEM_LIMIT = 40 * 1024 * 1024
+LOG2E = 1.4426950408889634
+VMEM_LIMIT = 24 * 1024 * 1024
+SMALL_LIMIT = 12 * 1024 * 1024
 
 
 def nt(left, right):
@@ -22,16 +24,37 @@
     return lax.dot_general(left, right, (((1,), (0,)), ((), ())), preferred_element_type=jnp.float32)
 
 
-def load_operands(meta, own, other, kv, q_s, g_s, k_s, v_s, pos_s):
+def queries_kernel(own, other, q_s, g_s, qt_s, gt_s):
     heads = own.shape[2] // HEAD
     rows = heads * SPAN
     for source, block in enumerate((own, other)):
         for half in range(2):
-            base = (source * 2 + half) * rows
-            for head in range(heads):
-                here = pl.ds(base + head * SPAN, SPAN)
-                q_s[here, :] = block[0, half * SPAN:(half + 1) * SPAN, head * HEAD:(head + 1) * HEAD]
-                g_s[here, :] = block[1, half * SPAN:(half + 1) * SPAN, head * HEAD:(head + 1) * HEAD]
+            u = source * 2 + half
+            for which, plain, turned in ((0, q_s, qt_s), (1, g_s, gt_s)):
+                pieces = [
+                    block[which, half * SPAN:(half + 1) * SPAN, head * HEAD:(head + 1) * HEAD] for head in range(heads)
+                ]
+                laid = jnp.concatenate(pieces, axis=0)
+                plain[u * rows:(u + 1) * rows, :] = laid
+                turned[u] = laid.T
+
+
+def queries_call(own, other):
+    rows = own.shape[2] // HEAD * SPAN
+    plain = jax.ShapeDtypeStruct((4 * rows, HEAD), jnp.bfloat16)
+    turned = jax.ShapeDtypeStruct((4, HEAD, rows), jnp.bfloat16)
+    return pl.pallas_call(
+        queries_kernel,
+        out_shape=[plain, plain, turned, turned],
+        in_specs=[pl.BlockSpec(memory_space=pltpu.VMEM)] * 2,
+        out_specs=[pl.BlockSpec(memory_space=pltpu.VMEM)] * 4,
+        compiler_params=pltpu.CompilerParams(vmem_limit_bytes=SMALL_LIMIT),
+        cost_estimate=pl.CostEstimate(flops=10**6, bytes_accessed=3 * 10**6, transcendentals=0),
+        name="queries",
+    )(own, other)
+
+
+def place_keys(meta, kv, k_s, v_s, pos_s):
     lane_rows = lax.broadcasted_iota(jnp.int32, (SPAN, 128), 0)
 
     def place(block, carry):
@@ -47,55 +70,68 @@
     lax.fori_loop(0, kv.shape[0], place, 0)
 
 
-def masked_scores(k_tile, q_rows, pos_tile, q_pos, q_start):
-    copies = q_rows.shape[0] // 128
+def masked_scores(k_tile, q_cols, pos_tile, q_pos, q_start):
+    copies = q_cols.shape[1] // 128
     key_pos = jnp.concatenate([pos_tile] * copies, axis=1)
     mask = (key_pos <= q_pos) & (key_pos >= q_start)
-    return jnp.where(mask, nt(k_tile, q_rows) * SCALE, NEG)
-
-
-def stats_kernel(meta, qmeta, own, other, kv, out, q_s, g_s, k_s, v_s, pos_s):
-    load_operands(meta, own, other, kv, q_s, g_s, k_s, v_s, pos_s)
-    rows = q_s.shape[0] // 4
-
-    def span_step(u, carry):
-        q_rows = q_s[pl.ds(u * rows, rows), :]
-        g_rows = g_s[pl.ds(u * rows, rows), :]
-        q_pos = qmeta[pl.ds(u, 1), :]
-        q_start = qmeta[pl.ds(4 + u, 1), :]
-
-        def tile_step(t, state):
-            top, total, weighted = state
-            here = pl.ds(pl.multiple_of(t * TILE, TILE), TILE)
-            scores = masked_scores(k_s[here, :], q_rows, pos_s[here, :], q_pos, q_start)
-            new_top = jnp.maximum(top, jnp.max(scores, axis=0, keepdims=True))
-            probs = jnp.exp(scores - new_top)
-            keep = jnp.exp(top - new_top)
-            grad = nt(v_s[here, :], g_rows)
-            return (
-                new_top,
-                keep * total + jnp.sum(probs, axis=0, keepdims=True),
-                keep * weighted + jnp.sum(probs * grad, axis=0, keepdims=True),
-            )
-
-        zero = jnp.zeros((1, rows), jnp.float32)
-        top, total, weighted = lax.fori_loop(
-            meta[2, u], meta[2, 4 + u], tile_step, (jnp.full((1, rows), NEG, jnp.float32), zero, zero)
-        )
-        out[pl.ds(u, 1), :] = top
-        out[pl.ds(4 + u, 1), :] = total
-        out[pl.ds(8 + u, 1), :] = weighted
+    return jnp.where(mask, nn(k_tile, q_cols) * (SCALE * LOG2E), NEG)
+
+
+def list_tiles(meta, items, together):
+    def add(t, n, u):
+        items[n] = u * 32 + t
+        return n + 1
+
+    count = jnp.int32(0)
+    for u in range(4):
+        count = lax.fori_loop(meta[2, u], meta[2, 4 + u], lambda t, n, u=u: add(t, n, u), count)
+    for spare in range(together - 1):
+        items[count + spare] = 4 * 32
+    return lax.div(count + together - 1, together)
+
+
+def tile_scores(item, qmeta, qt_s, k_s, pos_s):
+    u, t = lax.shift_right_logical(item, 5), item & 31
+    here = pl.ds(pl.multiple_of(t * TILE, TILE), TILE)
+    span = lax.rem(u, 4)
+    scores = masked_scores(
+        k_s[here, :], qt_s[span], pos_s[here, :], qmeta[pl.ds(2 * u, 1), :], qmeta[pl.ds(2 * u + 1, 1), :]
+    )
+    return span, here, t, scores
+
+
+def stats_kernel(meta, qmeta, qt_s, gt_s, kv, out, k_s, v_s, pos_s, items):
+    place_keys(meta, kv, k_s, v_s, pos_s)
+    rows = qt_s.shape[2]
+    out[0:4, :] = jnp.full((4, rows), NEG, jnp.float32)
+    out[4:16, :] = jnp.zeros((12, rows), jnp.float32)
+    groups = list_tiles(meta, items, 2)
+
+    def group_step(group, carry):
+        found = []
+        for slot in range(2):
+            span, here, t, scores = tile_scores(items[group * 2 + slot], qmeta, qt_s, k_s, pos_s)
+            top = jnp.max(scores, axis=0, keepdims=True)
+            probs = jnp.exp2(scores - top)
+            grad = nn(v_s[here, :], gt_s[span])
+            total = jnp.sum(probs, axis=0, keepdims=True)
+            found.append((span, top, total, jnp.sum(probs * grad, axis=0, keepdims=True)))
+        for span, top, total, weighted in found:
+            before = out[pl.ds(span, 1), :]
+            new_top = jnp.maximum(before, top)
+            keep, scale = jnp.exp2(before - new_top), jnp.exp2(top - new_top)
+            out[pl.ds(span, 1), :] = new_top
+            out[pl.ds(4 + span, 1), :] = keep * out[pl.ds(4 + span, 1), :] + scale * total
+            out[pl.ds(8 + span, 1), :] = keep * out[pl.ds(8 + span, 1), :] + scale * weighted
         return carry
 
-    lax.fori_loop(0, 4, span_step, 0)
-    out[12:16, :] = jnp.zeros((4, rows), jnp.float32)
+    lax.fori_loop(0, groups, group_step, 0)
 
 
 def grad_kernel(
-    meta, qmeta, own, other, kv, stats, far, dq_own, dq_other, dkv,
-    q_s, g_s, k_s, v_s, pos_s, kt_s, dk_s, dv_s, dq_s, fin_s,
+    meta, qmeta, q_s, g_s, qt_s, gt_s, k_s, v_s, pos_s, stats, far, dq_own, dq_other, dkv,
+    items, kt_s, dk_s, dv_s, dq_s, fin_s,
 ):
-    load_operands(meta, own, other, kv, q_s, g_s, k_s, v_s, pos_s)
     rows = q_s.shape[0] // 4
     heads = rows // SPAN
     tiles = k_s.shape[0] // TILE
@@ -103,55 +139,46 @@
         kt_s[t] = k_s[t * TILE:(t + 1) * TILE, :].T
     dk_s[...] = jnp.zeros_like(dk_s)
     dv_s[...] = jnp.zeros_like(dv_s)
+    dq_s[...] = jnp.zeros_like(dq_s)
     for u in range(4):
         v = (u + 2) % 4
         top_a, top_b = stats[u:u + 1, :], far[v:v + 1, :]
         top = jnp.maximum(top_a, top_b)
-        scale_a, scale_b = jnp.exp(top_a - top), jnp.exp(top_b - top)
+        scale_a, scale_b = jnp.exp2(top_a - top), jnp.exp2(top_b - top)
         total = scale_a * stats[4 + u:5 + u, :] + scale_b * far[4 + v:5 + v, :]
         weighted = scale_a * stats[8 + u:9 + u, :] + scale_b * far[8 + v:9 + v, :]
-        fin_s[u:u + 1, :] = top + jnp.log(total)
+        fin_s[u:u + 1, :] = top + jnp.log(total) * LOG2E
         fin_s[4 + u:5 + u, :] = weighted / total
-
-    def span_step(u, carry):
-        q_rows = q_s[pl.ds(u * rows, rows), :]
-        g_rows = g_s[pl.ds(u * rows, rows), :]
-        q_pos = qmeta[pl.ds(u, 1), :]
-        q_start = qmeta[pl.ds(4 + u, 1), :]
-        log_norm = fin_s[pl.ds(u, 1), :]
-        drift = fin_s[pl.ds(4 + u, 1), :]
-        dq_s[...] = jnp.zeros_like(dq_s)
-
-        def tile_step(t, inner):
-            here = pl.ds(pl.multiple_of(t * TILE, TILE), TILE)
-            scores = masked_scores(k_s[here, :], q_rows, pos_s[here, :], q_pos, q_start)
-            probs = jnp.exp(scores - log_norm)
-            grad = nt(v_s[here, :], g_rows)
-            score_grad = (probs * (grad - drift)).astype(jnp.bfloat16)
-            dv_s[here, :] += nn(probs.astype(jnp.bfloat16), g_rows)
-            dk_s[here, :] += nn(score_grad, q_rows)
-            dq_s[...] += nn(kt_s[t], score_grad)
-            return inner
-
-        lax.fori_loop(meta[2, u], meta[2, 4 + u], tile_step, 0)
-        flat = (dq_s[...] * SCALE).T
-        half = pl.multiple_of(lax.rem(u, 2) * SPAN, SPAN)
-
-        @pl.when(u < 2)
-        def _():
-            for head in range(heads):
-                dq_own[pl.ds(half, SPAN), head * HEAD:(head + 1) * HEAD] = flat[head * SPAN:(head + 1) * SPAN, :]
-
-        @pl.when(u >= 2)
-        def _():
-            for head in range(heads):
-                dq_other[pl.ds(half, SPAN), head * HEAD:(head + 1) * HEAD] = flat[
-                    head * SPAN:(head + 1) * SPAN, :
-                ].astype(jnp.bfloat16)
-
+    groups = list_tiles(meta, items, 2)
+
+    def group_step(group, carry):
+        found = []
+        for slot in range(2):
+            span, here, t, scores = tile_scores(items[group * 2 + slot], qmeta, qt_s, k_s, pos_s)
+            probs = jnp.exp2(scores - fin_s[pl.ds(span, 1), :])
+            grad = nn(v_s[here, :], gt_s[span])
+            score_grad = (probs * (grad - fin_s[pl.ds(4 + span, 1), :])).astype(jnp.bfloat16)
+            base = pl.ds(pl.multiple_of(span * rows, rows), rows)
+            found.append((
+                span, here, nn(probs.astype(jnp.bfloat16), g_s[base, :]), nn(score_grad, q_s[base, :]),
+                nn(kt_s[t], score_grad),
+            ))
+        for span, here, value_part, key_part, query_part in found:
+            dv_s[here, :] += value_part
+            dk_s[here, :] += key_part
+            dq_s[span] += query_part
         return carry
 
-    lax.fori_loop(0, 4, span_step, 0)
+    lax.fori_loop(0, groups, group_step, 0)
+    for u in range(4):
+        flat = (dq_s[u] * SCALE).T
+        half = (u % 2) * SPAN
+        for head in range(heads):
+            piece = flat[head * SPAN:(head + 1) * SPAN, :]
+            if u < 2:
+                dq_own[half:half + SPAN, head * HEAD:(head + 1) * HEAD] = piece
+            else:
+                dq_other[half:half + SPAN, head * HEAD:(head + 1) * HEAD] = piece.astype(jnp.bfloat16)
 
     def unplace(block, carry):
         for half in range(2):
@@ -164,59 +191,60 @@
     lax.fori_loop(0, dkv.shape[0], unplace, 0)
 
 
-def operand_scratch(rows, keys):
-    return [
-        pltpu.VMEM((4 * rows, HEAD), jnp.bfloat16),
-        pltpu.VMEM((4 * rows, HEAD), jnp.bfloat16),
-        pltpu.VMEM((keys, HEAD), jnp.bfloat16),
-        pltpu.VMEM((keys, HEAD), jnp.bfloat16),
-        pltpu.VMEM((keys, 128), jnp.int32),
-    ]
+def item_scratch(keys):
+    return pltpu.SMEM((4 * (keys // TILE) + 8,), jnp.int32)
 
 
 def in_vmem(count):
     return [pl.BlockSpec(memory_space=pltpu.SMEM)] + [pl.BlockSpec(memory_space=pltpu.VMEM)] * count
 
 
-def stats_call(meta, qmeta, own, other, kv):
-    rows = own.shape[2] // HEAD * SPAN
+def stats_call(meta, qmeta, turned, kv):
+    rows = turned[0].shape[2]
     keys = kv.shape[0] * kv.shape[1]
+    sorted_keys = jax.ShapeDtypeStruct((keys, HEAD), jnp.bfloat16)
     return pl.pallas_call(
         stats_kernel,
-        out_shape=jax.ShapeDtypeStruct((16, rows), jnp.float32),
+        out_shape=[
+            jax.ShapeDtypeStruct((16, rows), jnp.float32),
+            sorted_keys,
+            sorted_keys,
+            jax.ShapeDtypeStruct((keys, 128), jnp.int32),
+        ],
         in_specs=in_vmem(4),
-        out_specs=pl.BlockSpec(memory_space=pltpu.VMEM),
-        scratch_shapes=operand_scratch(rows, keys),
+        out_specs=[pl.BlockSpec(memory_space=pltpu.VMEM)] * 4,
+        scratch_shapes=[item_scratch(keys)],
         compiler_params=pltpu.CompilerParams(vmem_limit_bytes=VMEM_LIMIT),
         cost_estimate=pl.CostEstimate(flops=2 * 10**9, bytes_accessed=4 * 10**6, transcendentals=10**6),
         name="stats",
-    )(meta, qmeta, own, other, kv)
-
-
-def grad_call(meta, qmeta, own, other, kv, stats, far):
-    rows = own.shape[2] // HEAD * SPAN
-    keys = kv.shape[0] * kv.shape[1]
-    height, width = own.shape[1:]
+    )(meta, qmeta, *turned, kv)
+
+
+def grad_call(meta, qmeta, laid, turned, placed, stats, far, shape, heads):
+    rows = turned[0].shape[2]
+    keys = shape[0] * shape[1]
+    height, width = 2 * SPAN, heads * HEAD
     return pl.pallas_call(
         grad_kernel,
         out_shape=(
             jax.ShapeDtypeStruct((height, width), jnp.float32),
             jax.ShapeDtypeStruct((height, width), jnp.bfloat16),
-            jax.ShapeDtypeStruct(kv.shape, jnp.bfloat16),
+            jax.ShapeDtypeStruct(shape, jnp.bfloat16),
         ),
-        in_specs=in_vmem(6),
+        in_specs=in_vmem(10),
         out_specs=[pl.BlockSpec(memory_space=pltpu.VMEM)] * 3,
-        scratch_shapes=operand_scratch(rows, keys) + [
+        scratch_shapes=[
+            item_scratch(keys),
             pltpu.VMEM((keys // TILE, HEAD, TILE), jnp.bfloat16),
             pltpu.VMEM((keys, HEAD), jnp.float32),
             pltpu.VMEM((keys, HEAD), jnp.float32),
-            pltpu.VMEM((HEAD, rows), jnp.float32),
+            pltpu.VMEM((4, HEAD, rows), jnp.float32),
             pltpu.VMEM((8, rows), jnp.float32),
         ],
         compiler_params=pltpu.CompilerParams(vmem_limit_bytes=VMEM_LIMIT),
         cost_estimate=pl.CostEstimate(flops=5 * 10**9, bytes_accessed=6 * 10**6, transcendentals=10**6),
         name="grads",
-    )(meta, qmeta, own, other, kv, stats, far)
+    )(meta, qmeta, *laid, *turned, *placed, stats, far)
 
 
 def reduce_copies_kernel(parts, copies, *halves):
@@ -238,7 +266,7 @@
         out_shape=[jax.ShapeDtypeStruct((count, height, width), dtype)] + halves,
         in_specs=[pl.BlockSpec(memory_space=pltpu.VMEM)],
         out_specs=[pl.BlockSpec(memory_space=pltpu.VMEM)] * (1 + len(halves)),
-        compiler_params=pltpu.CompilerParams(vmem_limit_bytes=VMEM_LIMIT),
+        compiler_params=pltpu.CompilerParams(vmem_limit_bytes=SMALL_LIMIT),
         cost_estimate=pl.CostEstimate(flops=10**6, bytes_accessed=2 * 10**6, transcendentals=0),
         name=name,
     )(parts)
@@ -268,7 +296,7 @@
         out_shape=jax.ShapeDtypeStruct((2 * slots, rows, grads.shape[2]), jnp.bfloat16),
         in_specs=in_vmem(1 + len(arrays)),
         out_specs=pl.BlockSpec(memory_space=pltpu.VMEM),
-        compiler_params=pltpu.CompilerParams(vmem_limit_bytes=VMEM_LIMIT),
+        compiler_params=pltpu.CompilerParams(vmem_limit_bytes=SMALL_LIMIT),
         cost_estimate=pl.CostEstimate(flops=10**9, bytes_accessed=4 * 10**6, transcendentals=0),
         name="weights",
     )(place, *arrays, grads)
@@ -329,7 +357,8 @@
     meta, q_spans, doc_start = tables(doc_lengths, span_order)
     q_pos = q_spans[:, None] * SPAN + jnp.arange(SPAN, dtype=jnp.int32)[None, :]
     q_start = doc_start(q_pos)
-    qmeta = jnp.tile(jnp.concatenate([q_pos, q_start], axis=0), (1, heads))
+    qmeta = jnp.pad(jnp.stack([q_pos, q_start], axis=1).reshape(8, SPAN), ((0, 8), (0, 0)), constant_values=-1)
+    qmeta = jnp.tile(qmeta, (1, heads))
 
     other, features = lax.optimization_barrier((other, normed_input))
     copies_of = lax.axis_size("dp")
@@ -352,17 +381,19 @@
             )
         )
     half = copies_of // 2
-    near = jnp.stack(columns[:half]), jnp.stack(columns[half:])
-
-    beside_a = swapped(near[0], "yh")
-    stats = stats_call(meta, qmeta, own, other, kv)
-    stats, near_b = lax.optimization_barrier((stats, near[1]))
+    near_a = jnp.stack(columns[:half])
+
+    beside_a = swapped(near_a, "yh")
+    *laid, qt, gt = queries_call(own, other)
+    stats, *placed = stats_call(meta, qmeta, (qt, gt), kv)
+    stats, columns = lax.optimization_barrier((stats, columns[half:]))
+    near_b = jnp.stack(columns)
     beside_b = swapped(near_b, "yh")
     far = swapped(stats, "yb")
     far, beside_a = lax.optimization_barrier((far, beside_a))
-    dq_own, dq_other, dkv = grad_call(meta, qmeta, own, other, kv, stats, far)
+    dq_own, dq_other, dkv = grad_call(meta, qmeta, laid, (qt, gt), placed, stats, far, kv.shape, heads)
     dkv, beside_b = lax.optimization_barrier((dkv, beside_b))
-    near, beside = [near[0], near_b], [beside_a, beside_b]
+    near, beside = [near_a, near_b], [beside_a, beside_b]
     dq_far = swapped(dq_other, "yb")
     across = [swapped(part, "core") for part in (*near, *beside)]
     parts = lax.all_to_all(dkv, group, 0, 0, tiled=True)

time: 170 us -> 169 us (level)
  waiting for transfers between devices: 45.1 us -> 32.5 us
  starting transfers between devices: 68.9 us -> 74.6 us
  local copies, waits for them, and re-layouts: 8.81 us -> 11.5 us
  Pallas kernels: 15.1 us -> 17.6 us
    ppermute x4, waiting for transfers between devices: 9.99 us -> 0.01 us  [shards(): lax.ppermute(slab, ('dp', 'yb', 'core'), [(d * 4 + b * 2 + c, (d + by) %...]
    all_to_all x1, waiting for transfers between devices: 8.59 us -> 0.16 us  [shards(): parts = lax.all_to_all(dkv, group, 0, 0, tiled=True)]
    ppermute x9, waiting for transfers between devices: 12.4 us -> 18.5 us  [swapped(): return lax.ppermute(array, axis, [(0, 1), (1, 0)])]
    unnamed x25 -> x35, local copies, waits for them, and re-layouts: 5.44 us -> 8 us
    ppermute x9, starting transfers between devices: 28.1 us -> 30.5 us  [swapped(): return lax.ppermute(array, axis, [(0, 1), (1, 0)])]
    all_to_all x1, starting transfers between devices: 3.49 us -> 5.24 us  [shards(): all_grads = lax.all_to_all(copies, ('dp', 'yb'), 0, 0, tiled=True)]
    pallas_call x1 -> x2, Pallas kernels: 4.28 us -> 5.62 us  [the longest x1 5.23 us: stats_call(): pl.pallas_call(stats_kernel, out_shape=[jax.ShapeDtypeStruct((16, rows),...]
  transfers between devices with their start and end apart: 17 -> 17, of which waited for: 7 -> 5; matrix products, arithmetic and copies ran while one was open for 4% -> 5% of each run, Pallas kernels for 7% -> 9%
where the time goes in v3:
time: 169 us; the launch traced here: 168 us
  starting transfers between devices  74.6 us (44%)
  waiting for transfers between devices  32.5 us (19%)
  blocking collectives  24.5 us (14%)
  Pallas kernels  17.6 us (10%)
  local copies, waits for them, and re-layouts  11.5 us (7%)
  other arithmetic  5.02 us (3%)
  between operations  2.39 us (1%)
    ppermute x9, starting transfers between devices, swapped(): return lax.ppermute(array, axis, [(0, 1), (1, 0)])  30.5 us
    all_to_all x1, blocking collectives, shards(): pieces = lax.all_to_all(blocks, group, 0, 0, tiled=True)  24.5 us
    ppermute x9, waiting for transfers between devices, swapped(): return lax.ppermute(array, axis, [(0, 1), (1, 0)])  18.5 us
    ppermute x4, starting transfers between devices, shards(): lax.ppermute(slab, ('dp', 'yb', 'core'), [(d * 4 + b * 2 + c, (d + by) %...  15.1 us
    all_to_all x1, starting transfers between devices, shards(): lax.all_to_all(jnp.broadcast_to(pair[None], (group_size,) + pair.shape),...  12.3 us
    pallas_call x1, Pallas kernels, grad_call(): pl.pallas_call(grad_kernel, out_shape=(jax.ShapeDtypeStruct((height, widt...  9.03 us
    all_to_all x1, waiting for transfers between devices, shards(): all_grads = lax.all_to_all(copies, ('dp', 'yb'), 0, 0, tiled=True)  8.94 us
    unnamed x35, local copies, waits for them, and re-layouts  8 us
  transfers between devices with their start and end apart: 17, of which 5 were waited for; matrix products, arithmetic and copies ran while one was open for 5% of the time, Pallas kernels for 9%

profile of v3, /device:TPU:1, one launch (start us, length us, event | category | flops | bytes accessed | tf_op | source)
XLA Modules:
  0.0 168.1 jit_solution(11495720171161198405)
XLA Ops:
  0.6 1.0 constant_dynamic-update-slice_fusion.1
  1.7 0.0 copy-done.10
  1.7 0.0 copy-start.13
  1.7 4.0 %collective-permute-start = (bf16[2,128,1024]{2,1,0:T(8,128)(2,1)S(1)}, bf16[2,128,1024]{2,1,0:T(8,128)(2,1)S(1)}, u32[]{:S(2)}, u32[]{:S(2)}) collective-permute-start(bf16[2,128,1024]{2,1,0:T(8,128)(2,1)S(1)} %constant_dynamic-update-slice_fusion.own), channel_id=1, source_target_pairs={{0,32},{32,0},{1,33},{33,1},{2,34},{34,2},{3,35},{35,3},{4,36},{36... | collective-permute-start | bytes 1572872 | tf_op jit(solution)/shard_map/ppermute | solution.py:311
  5.8 1.1 broadcast_in_dim.43
  6.9 12.3 %all-to-all-start = ((bf16[16,128,256]{2,1,0:T(8,128)(2,1)}), bf16[16,128,256]{2,1,0:T(8,128)(2,1)S(1)}, u32[]{:S(2)}, u32[]{:S(2)}) async-start(bf16[16,128,256]{2,1,0:T(8,128)(2,1)} %broadcast_in_dim.43), calls=%async_computation | async-start | bytes 2097152 | tf_op jit(solution)/shard_map/all_to_all | solution.py:353
  19.2 0.6 copy-done.15
  19.9 0.1 reshape.195
  20.0 0.1 select_n.68
  20.1 0.6 fusion.2
  22.0 1.4 broadcast_multiply_fusion
  23.4 0.1 copy.26
  23.5 0.1 lt.41
  23.6 0.6 copy-done.16
  24.2 0.2 reduce-window.8
  24.4 0.1 iota_add_fusion
  24.5 0.1 select_reduce_fusion
  24.6 0.1 iota_add_fusion.1
  24.6 0.2 select_reduce_fusion.1
  24.8 0.2 convert_reduce_fusion
  25.0 0.2 convert_reduce_fusion.2
  25.3 0.3 copy.29
  25.6 0.8 dynamic-slice_bitcast_fusion.1
  26.4 4.1 %collective-permute-start.5 = (bf16[512,128]{1,0:T(8,128)(2,1)}, bf16[512,128]{1,0:T(8,128)(2,1)S(1)}, u32[]{:S(2)}, u32[]{:S(2)}) collective-permute-start(bf16[512,128]{1,0:T(8,128)(2,1)} %get-tuple-element.70), channel_id=1, source_target_pairs={{0,128},{1,160},{32,129},{33,161},{128,256},{129,288},{160,257},{1... | collective-permute-start | bytes 393224 | tf_op jit(solution)/shard_map/ppermute | solution.py:374
  30.5 2.4 %collective-permute-start.4 = (bf16[512,128]{1,0:T(8,128)(2,1)}, bf16[512,128]{1,0:T(8,128)(2,1)S(1)}, u32[]{:S(2)}, u32[]{:S(2)}) collective-permute-start(bf16[512,128]{1,0:T(8,128)(2,1)} %get-tuple-element.69), channel_id=1, source_target_pairs={{0,0},{1,32},{32,1},{33,33},{128,128},{129,160},{160,129},{161,161... | collective-permute-start | bytes 393224 | tf_op jit(solution)/shard_map/ppermute | solution.py:374
  32.9 0.1 add_bitcast_fusion
  33.0 0.1 broadcast_in_dim_reshape.2
  33.1 0.1 tile.10.qmeta
  33.2 5.4 %collective-permute-start.1 = (bf16[512,128]{1,0:T(8,128)(2,1)}, bf16[512,128]{1,0:T(8,128)(2,1)}, u32[]{:S(2)}, u32[]{:S(2)}) collective-permute-start(bf16[512,128]{1,0:T(8,128)(2,1)} %get-tuple-element.72), channel_id=1, source_target_pairs={{0,256},{1,288},{32,257},{33,289},{128,384},{129,416},{160,385},{1... | collective-permute-start | bytes 393224 | tf_op jit(solution)/shard_map/ppermute | solution.py:374
  38.6 3.2 %collective-permute-start.2 = (bf16[512,128]{1,0:T(8,128)(2,1)}, bf16[512,128]{1,0:T(8,128)(2,1)}, u32[]{:S(2)}, u32[]{:S(2)}) collective-permute-start(bf16[512,128]{1,0:T(8,128)(2,1)} %get-tuple-element.71), channel_id=1, source_target_pairs={{0,384},{1,416},{32,385},{33,417},{128,0},{129,32},{160,1},{161,33... | collective-permute-start | bytes 393224 | tf_op jit(solution)/shard_map/ppermute | solution.py:374
  41.8 0.4 queries.1
  42.2 0.8 copy-done.2
  43.1 0.8 copy-done
  43.8 5.2 %collective-permute-start.6 = (bf16[2,512,128]{2,1,0:T(8,128)(2,1)S(1)}, bf16[2,512,128]{2,1,0:T(8,128)(2,1)S(1)}, u32[]{:S(2)}, u32[]{:S(2)}) collective-permute-start(bf16[2,512,128]{2,1,0:T(8,128)(2,1)S(1)} %pad_maximum_fusion.refs_0_), channel_id=1, source_target_pairs={{0,2},{2,0},{1,3},{3,1},{4,6},{6,4},{5,7},{7,5},{8,10},{10,8},{9,1... | collective-permute-start | bytes 786440 | tf_op jit(solution)/shard_map/ppermute | solution.py:311
  49.1 1.0 copy-done.1
  50.1 5.2 %stats.1 = (f32[16,512]{1,0:T(8,128)S(1)}, bf16[2048,128]{1,0:T(8,128)(2,1)S(1)}, bf16[2048,128]{1,0:T(8,128)(2,1)S(1)}, s32[2048,128]{1,0:T(8,128)S(1)}) custom-call(s32[3,32]{1,0:T(4,128)S(1)} %pad_add_fusion.1.meta, s32[16,512]{1,0:T(8,128)S(1)} %tile.10.qmeta, bf16[4,128,512]{2,1,0:T(8,128)(2,1)S(1)} %copy-done.1, bf16[4,128,512]{2,1,0:T(8,128)(2,1)S(1)} %copy-done.3, ...), custom_call_target="tpu_custom_call" | custom-call | flops 2000000000 | bytes 4000000 | tf_op jit(solution)/shard_map/stats/pallas_call | solution.py:206
  55.3 1.9 %collective-permute-start.3 = (f32[16,512]{1,0:T(8,128)S(1)}, f32[16,512]{1,0:T(8,128)S(1)}, u32[]{:S(2)}, u32[]{:S(2)}) collective-permute-start(f32[16,512]{1,0:T(8,128)S(1)} %get-tuple-element.44.stats), channel_id=1, source_target_pairs={{0,32},{32,0},{1,33},{33,1},{2,34},{34,2},{3,35},{35,3},{4,36},{36... | collective-permute-start | bytes 98312 | tf_op jit(solution)/shard_map/ppermute | solution.py:311
  57.3 1.0 pad_maximum_fusion.1.refs_1_
  58.3 6.4 %collective-permute-start.7 = (bf16[2,512,128]{2,1,0:T(8,128)(2,1)S(1)}, bf16[2,512,128]{2,1,0:T(8,128)(2,1)S(1)}, u32[]{:S(2)}, u32[]{:S(2)}) collective-permute-start(bf16[2,512,128]{2,1,0:T(8,128)(2,1)S(1)} %pad_maximum_fusion.1.refs_1_), channel_id=1, source_target_pairs={{0,2},{2,0},{1,3},{3,1},{4,6},{6,4},{5,7},{7,5},{8,10},{10,8},{9,1... | collective-permute-start | bytes 786440 | tf_op jit(solution)/shard_map/ppermute | solution.py:311
  64.7 9.0 %grads.1 = (f32[128,1024]{1,0:T(8,128)S(1)}, bf16[128,1024]{1,0:T(8,128)(2,1)S(1)}, bf16[16,128,256]{2,1,0:T(8,128)(2,1)}) custom-call(s32[3,32]{1,0:T(4,128)S(1)} %pad_add_fusion.1.meta, s32[16,512]{1,0:T(8,128)S(1)} %tile.10.qmeta, bf16[2048,128]{1,0:T(8,128)(2,1)S(1)} %get-tuple-element.35.q_s, bf16[2048,128]{1,0:T(8,128)(2,1)S(1)} %get-tuple-element.36.g_s, ...), custom_call_target="tpu_custom_call" | custom-call | flops 5000000000 | bytes 6000000 | tf_op jit(solution)/shard_map/grads/pallas_call | solution.py:227
  73.7 3.6 %collective-permute-done.7.refs_5_ = bf16[2,512,128]{2,1,0:T(8,128)(2,1)S(1)} collective-permute-done((bf16[2,512,128]{2,1,0:T(8,128)(2,1)S(1)}, bf16[2,512,128]{2,1,0:T(8,128)(2,1)S(1)}, u32[]{:S(2)}, u32[]{:S(2)}) %collective-permute-start.7) | collective-permute-done | bytes 262176 | tf_op jit(solution)/shard_map/ppermute | solution.py:311
  77.3 0.7 copy-done.4
  78.0 8.0 %all-to-all-start.1 = ((bf16[16,128,256]{2,1,0:T(8,128)(2,1)}), bf16[16,128,256]{2,1,0:T(8,128)(2,1)S(1)}, u32[]{:S(2)}, u32[]{:S(2)}) async-start(bf16[16,128,256]{2,1,0:T(8,128)(2,1)} %get-tuple-element.50), calls=%async_computation.1 | async-start | bytes 2097152 | tf_op jit(solution)/shard_map/all_to_all | solution.py:399
  85.9 3.6 %collective-permute-start.8 = (bf16[2,512,128]{2,1,0:T(8,128)(2,1)S(1)}, bf16[2,512,128]{2,1,0:T(8,128)(2,1)S(1)}, u32[]{:S(2)}, u32[]{:S(2)}) collective-permute-start(bf16[2,512,128]{2,1,0:T(8,128)(2,1)S(1)} %pad_maximum_fusion.refs_0_), channel_id=1, source_target_pairs={{0,1},{1,0},{2,3},{3,2},{4,5},{5,4},{6,7},{7,6},{8,9},{9,8},{10,11... | collective-permute-start | bytes 786440 | tf_op jit(solution)/shard_map/ppermute | solution.py:311
  89.5 1.9 %collective-permute-start.9 = (bf16[2,512,128]{2,1,0:T(8,128)(2,1)S(1)}, bf16[2,512,128]{2,1,0:T(8,128)(2,1)S(1)}, u32[]{:S(2)}, u32[]{:S(2)}) collective-permute-start(bf16[2,512,128]{2,1,0:T(8,128)(2,1)S(1)} %pad_maximum_fusion.1.refs_1_), channel_id=1, source_target_pairs={{0,1},{1,0},{2,3},{3,2},{4,5},{5,4},{6,7},{7,6},{8,9},{9,8},{10,11... | collective-permute-start | bytes 786440 | tf_op jit(solution)/shard_map/ppermute | solution.py:311
  91.4 2.4 %collective-permute-start.10 = (bf16[2,512,128]{2,1,0:T(8,128)(2,1)S(1)}, bf16[2,512,128]{2,1,0:T(8,128)(2,1)S(1)}, u32[]{:S(2)}, u32[]{:S(2)}) collective-permute-start(bf16[2,512,128]{2,1,0:T(8,128)(2,1)S(1)} %collective-permute-done.6.refs_4_), channel_id=1, source_target_pairs={{0,1},{1,0},{2,3},{3,2},{4,5},{5,4},{6,7},{7,6},{8,9},{9,8},{10,11... | collective-permute-start | bytes 786440 | tf_op jit(solution)/shard_map/ppermute | solution.py:311
  93.8 2.9 %collective-permute-start.12 = (bf16[128,1024]{1,0:T(8,128)(2,1)}, bf16[128,1024]{1,0:T(8,128)(2,1)S(1)}, u32[]{:S(2)}, u32[]{:S(2)}) collective-permute-start(bf16[128,1024]{1,0:T(8,128)(2,1)} %copy-done.8), channel_id=1, source_target_pairs={{0,32},{32,0},{1,33},{33,1},{2,34},{34,2},{3,35},{35,3},{4,36},{36... | collective-permute-start | bytes 786440 | tf_op jit(solution)/shard_map/ppermute | solution.py:311
  96.7 2.2 %collective-permute-start.11 = (bf16[2,512,128]{2,1,0:T(8,128)(2,1)S(1)}, bf16[2,512,128]{2,1,0:T(8,128)(2,1)S(1)}, u32[]{:S(2)}, u32[]{:S(2)}) collective-permute-start(bf16[2,512,128]{2,1,0:T(8,128)(2,1)S(1)} %copy-done.5), channel_id=1, source_target_pairs={{0,1},{1,0},{2,3},{3,2},{4,5},{5,4},{6,7},{7,6},{8,9},{9,8},{10,11... | collective-permute-start | bytes 786440 | tf_op jit(solution)/shard_map/ppermute | solution.py:311
  99.0 14.9 %collective-permute-done.12 = bf16[128,1024]{1,0:T(8,128)(2,1)S(1)} collective-permute-done((bf16[128,1024]{1,0:T(8,128)(2,1)}, bf16[128,1024]{1,0:T(8,128)(2,1)S(1)}, u32[]{:S(2)}, u32[]{:S(2)}) %collective-permute-start.12) | collective-permute-done | bytes 262176 | tf_op jit(solution)/shard_map/ppermute | solution.py:311
  113.9 0.7 copy-done.11
  114.6 0.7 copy-done.6
  115.3 0.2 all-to-all-done.1.parts
  115.4 1.0 sum_grads.1
  116.4 5.2 %all-to-all-start.2 = ((bf16[8,128,256]{2,1,0:T(8,128)(2,1)}), bf16[8,128,256]{2,1,0:T(8,128)(2,1)S(1)}, u32[]{:S(2)}, u32[]{:S(2)}) async-start(bf16[8,128,256]{2,1,0:T(8,128)(2,1)} %get-tuple-element.62), calls=%async_computation.2 | async-start | bytes 1048576 | tf_op jit(solution)/shard_map/all_to_all | solution.py:404
  121.6 0.1 pad_add_fusion.4.place
  121.7 8.9 %all-to-all-done.2.refs_8_ = bf16[8,128,256]{2,1,0:T(8,128)(2,1)S(1)} async-done(((bf16[8,128,256]{2,1,0:T(8,128)(2,1)}), bf16[8,128,256]{2,1,0:T(8,128)(2,1)S(1)}, u32[]{:S(2)}, u32[]{:S(2)}) %all-to-all-start.2) | async-done | bytes 524320 | tf_op jit(solution)/shard_map/all_to_all | solution.py:404
  130.6 0.9 copy-done.7
  131.6 1.3 weights.1
  132.9 24.5 %all_to_all.25.parts = bf16[16,64,256]{2,1,0:T(8,128)(2,1)S(1)} all-to-all(bf16[16,64,256]{2,1,0:T(8,128)(2,1)S(1)} %weights.1), channel_id=1, replica_groups=mesh['dp'=4,'ya'=2,'yb'=2,'z'=8,'yh'=2,'core'=2] {'ya','z'}, dimensions={0} | all-to-all | bytes 1048576 | tf_op jit(solution)/shard_map/all_to_all | solution.py:407
  157.3 0.8 sum_rows.1
  158.1 3.5 %all-to-all-start.4 = ((f32[4,64,256]{2,1,0:T(8,128)}), f32[4,64,256]{2,1,0:T(8,128)S(1)}, u32[]{:S(2)}, u32[]{:S(2)}) async-start(f32[4,64,256]{2,1,0:T(8,128)} %sum_rows.1), calls=%async_computation.4 | async-start | bytes 524288 | tf_op jit(solution)/shard_map/all_to_all | solution.py:409
  161.7 0.8 fusion
  162.4 5.0 %all-to-all-done.4 = f32[4,64,256]{2,1,0:T(8,128)S(1)} async-done(((f32[4,64,256]{2,1,0:T(8,128)}), f32[4,64,256]{2,1,0:T(8,128)S(1)}, u32[]{:S(2)}, u32[]{:S(2)}) %all-to-all-start.4) | async-done | bytes 262176 | tf_op jit(solution)/shard_map/all_to_all | solution.py:409
  167.4 0.7 fusion.4
  (50 shorter events, 0.3 us)
Async XLA Ops:
  0.6 1.0 copy-start.10
  1.7 4.1 %copy-start.13 = (bf16[1,128,128]{2,1,0:T(8,128)(2,1)S(1)}, bf16[1,128,128]{2,1,0:T(8,128)(2,1)}, u32[]{:S(2)}) copy-start(bf16[1,128,128]{2,1,0:T(8,128)(2,1)} %param.9) | copy-start | bytes 98308
  1.7 4.1 %copy-start.14 = (bf16[1,128,128]{2,1,0:T(8,128)(2,1)S(1)}, bf16[1,128,128]{2,1,0:T(8,128)(2,1)}, u32[]{:S(2)}) copy-start(bf16[1,128,128]{2,1,0:T(8,128)(2,1)} %param.8) | copy-start | bytes 98308
  1.7 23.5 %collective-permute-start = (bf16[2,128,1024]{2,1,0:T(8,128)(2,1)S(1)}, bf16[2,128,1024]{2,1,0:T(8,128)(2,1)S(1)}, u32[]{:S(2)}, u32[]{:S(2)}) collective-permute-start(bf16[2,128,1024]{2,1,0:T(8,128)(2,1)S(1)} %constant_dynamic-update-slice_fusion.own), channel_id=1, source_target_pairs={{0,32},{32,0},{1,33},{33,1},{2,34},{34,2},{3,35},{35,3},{4,36},{36... | collective-permute-start | bytes 1572872 | tf_op jit(solution)/shard_map/ppermute | solution.py:311
  6.9 18.4 %copy-start.9 = (bf16[1,128,2048]{2,1,0:T(8,128)(2,1)S(1)}, bf16[1,128,2048]{2,1,0:T(8,128)(2,1)}, u32[]{:S(2)}) copy-start(bf16[1,128,2048]{2,1,0:T(8,128)(2,1)} %param.11) | copy-start | bytes 1572868
  6.9 42.1 %all-to-all-start = ((bf16[16,128,256]{2,1,0:T(8,128)(2,1)}), bf16[16,128,256]{2,1,0:T(8,128)(2,1)S(1)}, u32[]{:S(2)}, u32[]{:S(2)}) async-start(bf16[16,128,256]{2,1,0:T(8,128)(2,1)} %broadcast_in_dim.43), calls=%async_computation | async-start | bytes 2097152 | tf_op jit(solution)/shard_map/all_to_all | solution.py:353
  19.2 0.7 copy-start.15
  23.6 0.7 copy-start.16
  26.4 16.6 %collective-permute-start.5 = (bf16[512,128]{1,0:T(8,128)(2,1)}, bf16[512,128]{1,0:T(8,128)(2,1)S(1)}, u32[]{:S(2)}, u32[]{:S(2)}) collective-permute-start(bf16[512,128]{1,0:T(8,128)(2,1)} %get-tuple-element.70), channel_id=1, source_target_pairs={{0,128},{1,160},{32,129},{33,161},{128,256},{129,288},{160,257},{1... | collective-permute-start | bytes 393224 | tf_op jit(solution)/shard_map/ppermute | solution.py:374
  30.5 12.5 %collective-permute-start.4 = (bf16[512,128]{1,0:T(8,128)(2,1)}, bf16[512,128]{1,0:T(8,128)(2,1)S(1)}, u32[]{:S(2)}, u32[]{:S(2)}) collective-permute-start(bf16[512,128]{1,0:T(8,128)(2,1)} %get-tuple-element.69), channel_id=1, source_target_pairs={{0,0},{1,32},{32,1},{33,33},{128,128},{129,160},{160,129},{161,161... | collective-permute-start | bytes 393224 | tf_op jit(solution)/shard_map/ppermute | solution.py:374
  33.2 22.1 %collective-permute-start.1 = (bf16[512,128]{1,0:T(8,128)(2,1)}, bf16[512,128]{1,0:T(8,128)(2,1)}, u32[]{:S(2)}, u32[]{:S(2)}) collective-permute-start(bf16[512,128]{1,0:T(8,128)(2,1)} %get-tuple-element.72), channel_id=1, source_target_pairs={{0,256},{1,288},{32,257},{33,289},{128,384},{129,416},{160,385},{1... | collective-permute-start | bytes 393224 | tf_op jit(solution)/shard_map/ppermute | solution.py:374
  38.6 16.8 %collective-permute-start.2 = (bf16[512,128]{1,0:T(8,128)(2,1)}, bf16[512,128]{1,0:T(8,128)(2,1)}, u32[]{:S(2)}, u32[]{:S(2)}) collective-permute-start(bf16[512,128]{1,0:T(8,128)(2,1)} %get-tuple-element.71), channel_id=1, source_target_pairs={{0,384},{1,416},{32,385},{33,417},{128,0},{129,32},{160,1},{161,33... | collective-permute-start | bytes 393224 | tf_op jit(solution)/shard_map/ppermute | solution.py:374
  42.2 0.8 copy-start.2
  43.0 0.8 copy-start
  43.0 6.0 %copy-start.3 = (bf16[4,128,512]{2,1,0:T(8,128)(2,1)S(1)}, bf16[4,128,512]{2,1,0:T(8,128)(2,1)}, u32[]{:S(2)}) copy-start(bf16[4,128,512]{2,1,0:T(8,128)(2,1)} %copy-done.2) | copy-start | bytes 1572868
  43.8 20.8 %collective-permute-start.6 = (bf16[2,512,128]{2,1,0:T(8,128)(2,1)S(1)}, bf16[2,512,128]{2,1,0:T(8,128)(2,1)S(1)}, u32[]{:S(2)}, u32[]{:S(2)}) collective-permute-start(bf16[2,512,128]{2,1,0:T(8,128)(2,1)S(1)} %pad_maximum_fusion.refs_0_), channel_id=1, source_target_pairs={{0,2},{2,0},{1,3},{3,1},{4,6},{6,4},{5,7},{7,5},{8,10},{10,8},{9,1... | collective-permute-start | bytes 786440 | tf_op jit(solution)/shard_map/ppermute | solution.py:311
  49.0 1.0 copy-start.1
  55.3 9.3 %collective-permute-start.3 = (f32[16,512]{1,0:T(8,128)S(1)}, f32[16,512]{1,0:T(8,128)S(1)}, u32[]{:S(2)}, u32[]{:S(2)}) collective-permute-start(f32[16,512]{1,0:T(8,128)S(1)} %get-tuple-element.44.stats), channel_id=1, source_target_pairs={{0,32},{32,0},{1,33},{33,1},{2,34},{34,2},{3,35},{35,3},{4,36},{36... | collective-permute-start | bytes 98312 | tf_op jit(solution)/shard_map/ppermute | solution.py:311
  58.3 19.0 %collective-permute-start.7 = (bf16[2,512,128]{2,1,0:T(8,128)(2,1)S(1)}, bf16[2,512,128]{2,1,0:T(8,128)(2,1)S(1)}, u32[]{:S(2)}, u32[]{:S(2)}) collective-permute-start(bf16[2,512,128]{2,1,0:T(8,128)(2,1)S(1)} %pad_maximum_fusion.1.refs_1_), channel_id=1, source_target_pairs={{0,2},{2,0},{1,3},{3,1},{4,6},{6,4},{5,7},{7,5},{8,10},{10,8},{9,1... | collective-permute-start | bytes 786440 | tf_op jit(solution)/shard_map/ppermute | solution.py:311
  73.7 3.6 %copy-start.8 = (bf16[128,1024]{1,0:T(8,128)(2,1)}, bf16[128,1024]{1,0:T(8,128)(2,1)S(1)}, u32[]{:S(2)}) copy-start(bf16[128,1024]{1,0:T(8,128)(2,1)S(1)} %get-tuple-element.53) | copy-start | bytes 786436
  77.3 0.7 copy-start.4
  78.0 18.8 %copy-start.5 = (bf16[2,512,128]{2,1,0:T(8,128)(2,1)S(1)}, bf16[2,512,128]{2,1,0:T(8,128)(2,1)}, u32[]{:S(2)}) copy-start(bf16[2,512,128]{2,1,0:T(8,128)(2,1)} %copy-done.4) | copy-start | bytes 786436
  78.0 37.5 %all-to-all-start.1 = ((bf16[16,128,256]{2,1,0:T(8,128)(2,1)}), bf16[16,128,256]{2,1,0:T(8,128)(2,1)S(1)}, u32[]{:S(2)}, u32[]{:S(2)}) async-start(bf16[16,128,256]{2,1,0:T(8,128)(2,1)} %get-tuple-element.50), calls=%async_computation.1 | async-start | bytes 2097152 | tf_op jit(solution)/shard_map/all_to_all | solution.py:399
  85.9 13.0 %collective-permute-start.8 = (bf16[2,512,128]{2,1,0:T(8,128)(2,1)S(1)}, bf16[2,512,128]{2,1,0:T(8,128)(2,1)S(1)}, u32[]{:S(2)}, u32[]{:S(2)}) collective-permute-start(bf16[2,512,128]{2,1,0:T(8,128)(2,1)S(1)} %pad_maximum_fusion.refs_0_), channel_id=1, source_target_pairs={{0,1},{1,0},{2,3},{3,2},{4,5},{5,4},{6,7},{7,6},{8,9},{9,8},{10,11... | collective-permute-start | bytes 786440 | tf_op jit(solution)/shard_map/ppermute | solution.py:311
  89.5 9.4 %collective-permute-start.9 = (bf16[2,512,128]{2,1,0:T(8,128)(2,1)S(1)}, bf16[2,512,128]{2,1,0:T(8,128)(2,1)S(1)}, u32[]{:S(2)}, u32[]{:S(2)}) collective-permute-start(bf16[2,512,128]{2,1,0:T(8,128)(2,1)S(1)} %pad_maximum_fusion.1.refs_1_), channel_id=1, source_target_pairs={{0,1},{1,0},{2,3},{3,2},{4,5},{5,4},{6,7},{7,6},{8,9},{9,8},{10,11... | collective-permute-start | bytes 786440 | tf_op jit(solution)/shard_map/ppermute | solution.py:311
  91.4 7.5 %collective-permute-start.10 = (bf16[2,512,128]{2,1,0:T(8,128)(2,1)S(1)}, bf16[2,512,128]{2,1,0:T(8,128)(2,1)S(1)}, u32[]{:S(2)}, u32[]{:S(2)}) collective-permute-start(bf16[2,512,128]{2,1,0:T(8,128)(2,1)S(1)} %collective-permute-done.6.refs_4_), channel_id=1, source_target_pairs={{0,1},{1,0},{2,3},{3,2},{4,5},{5,4},{6,7},{7,6},{8,9},{9,8},{10,11... | collective-permute-start | bytes 786440 | tf_op jit(solution)/shard_map/ppermute | solution.py:311
  93.8 20.0 %collective-permute-start.12 = (bf16[128,1024]{1,0:T(8,128)(2,1)}, bf16[128,1024]{1,0:T(8,128)(2,1)S(1)}, u32[]{:S(2)}, u32[]{:S(2)}) collective-permute-start(bf16[128,1024]{1,0:T(8,128)(2,1)} %copy-done.8), channel_id=1, source_target_pairs={{0,32},{32,0},{1,33},{33,1},{2,34},{34,2},{3,35},{35,3},{4,36},{36... | collective-permute-start | bytes 786440 | tf_op jit(solution)/shard_map/ppermute | solution.py:311
  96.7 17.8 %collective-permute-start.11 = (bf16[2,512,128]{2,1,0:T(8,128)(2,1)S(1)}, bf16[2,512,128]{2,1,0:T(8,128)(2,1)S(1)}, u32[]{:S(2)}, u32[]{:S(2)}) collective-permute-start(bf16[2,512,128]{2,1,0:T(8,128)(2,1)S(1)} %copy-done.5), channel_id=1, source_target_pairs={{0,1},{1,0},{2,3},{3,2},{4,5},{5,4},{6,7},{7,6},{8,9},{9,8},{10,11... | collective-permute-start | bytes 786440 | tf_op jit(solution)/shard_map/ppermute | solution.py:311
  113.9 0.7 copy-start.11
  114.6 0.7 copy-start.6
  116.4 14.3 %all-to-all-start.2 = ((bf16[8,128,256]{2,1,0:T(8,128)(2,1)}), bf16[8,128,256]{2,1,0:T(8,128)(2,1)S(1)}, u32[]{:S(2)}, u32[]{:S(2)}) async-start(bf16[8,128,256]{2,1,0:T(8,128)(2,1)} %get-tuple-element.62), calls=%async_computation.2 | async-start | bytes 1048576 | tf_op jit(solution)/shard_map/all_to_all | solution.py:404
  130.6 1.0 copy-start.7
  158.1 3.5 %copy-start.12 = (bf16[128,1024]{1,0:T(8,128)(2,1)S(1)}, bf16[128,1024]{1,0:T(8,128)(2,1)}, u32[]{:S(2)}) copy-start(bf16[128,1024]{1,0:T(8,128)(2,1)} %copy-done.11) | copy-start | bytes 786436
  158.1 9.3 %all-to-all-start.4 = ((f32[4,64,256]{2,1,0:T(8,128)}), f32[4,64,256]{2,1,0:T(8,128)S(1)}, u32[]{:S(2)}, u32[]{:S(2)}) async-start(f32[4,64,256]{2,1,0:T(8,128)} %sum_rows.1), calls=%async_computation.4 | async-start | bytes 524288 | tf_op jit(solution)/shard_map/all_to_all | solution.py:409

commit v4 on v3

--- a/solution.py
+++ b/solution.py
@@ -24,37 +24,11 @@
     return lax.dot_general(left, right, (((1,), (0,)), ((), ())), preferred_element_type=jnp.float32)
 
 
-def queries_kernel(own, other, q_s, g_s, qt_s, gt_s):
-    heads = own.shape[2] // HEAD
-    rows = heads * SPAN
+def load_operands(meta, own, other, kv, q_s, g_s, k_s, v_s, pos_s):
+    rows = own.shape[1]
     for source, block in enumerate((own, other)):
-        for half in range(2):
-            u = source * 2 + half
-            for which, plain, turned in ((0, q_s, qt_s), (1, g_s, gt_s)):
-                pieces = [
-                    block[which, half * SPAN:(half + 1) * SPAN, head * HEAD:(head + 1) * HEAD] for head in range(heads)
-                ]
-                laid = jnp.concatenate(pieces, axis=0)
-                plain[u * rows:(u + 1) * rows, :] = laid
-                turned[u] = laid.T
-
-
-def queries_call(own, other):
-    rows = own.shape[2] // HEAD * SPAN
-    plain = jax.ShapeDtypeStruct((4 * rows, HEAD), jnp.bfloat16)
-    turned = jax.ShapeDtypeStruct((4, HEAD, rows), jnp.bfloat16)
-    return pl.pallas_call(
-        queries_kernel,
-        out_shape=[plain, plain, turned, turned],
-        in_specs=[pl.BlockSpec(memory_space=pltpu.VMEM)] * 2,
-        out_specs=[pl.BlockSpec(memory_space=pltpu.VMEM)] * 4,
-        compiler_params=pltpu.CompilerParams(vmem_limit_bytes=SMALL_LIMIT),
-        cost_estimate=pl.CostEstimate(flops=10**6, bytes_accessed=3 * 10**6, transcendentals=0),
-        name="queries",
-    )(own, other)
-
-
-def place_keys(meta, kv, k_s, v_s, pos_s):
+        q_s[source * rows:(source + 1) * rows, :] = block[0]
+        g_s[source * rows:(source + 1) * rows, :] = block[1]
     lane_rows = lax.broadcasted_iota(jnp.int32, (SPAN, 128), 0)
 
     def place(block, carry):
@@ -70,11 +44,11 @@
     lax.fori_loop(0, kv.shape[0], place, 0)
 
 
-def masked_scores(k_tile, q_cols, pos_tile, q_pos, q_start):
-    copies = q_cols.shape[1] // 128
+def masked_scores(k_tile, q_rows, pos_tile, q_pos, q_start):
+    copies = q_rows.shape[0] // 128
     key_pos = jnp.concatenate([pos_tile] * copies, axis=1)
     mask = (key_pos <= q_pos) & (key_pos >= q_start)
-    return jnp.where(mask, nn(k_tile, q_cols) * (SCALE * LOG2E), NEG)
+    return jnp.where(mask, nt(k_tile, q_rows) * (SCALE * LOG2E), NEG)
 
 
 def list_tiles(meta, items, together):
@@ -90,19 +64,21 @@
     return lax.div(count + together - 1, together)
 
 
-def tile_scores(item, qmeta, qt_s, k_s, pos_s):
+def tile_scores(item, qmeta, q_s, k_s, pos_s):
     u, t = lax.shift_right_logical(item, 5), item & 31
     here = pl.ds(pl.multiple_of(t * TILE, TILE), TILE)
     span = lax.rem(u, 4)
+    rows = qmeta.shape[1]
+    base = pl.ds(pl.multiple_of(span * rows, rows), rows)
     scores = masked_scores(
-        k_s[here, :], qt_s[span], pos_s[here, :], qmeta[pl.ds(2 * u, 1), :], qmeta[pl.ds(2 * u + 1, 1), :]
+        k_s[here, :], q_s[base, :], pos_s[here, :], qmeta[pl.ds(2 * u, 1), :], qmeta[pl.ds(2 * u + 1, 1), :]
     )
-    return span, here, t, scores
-
-
-def stats_kernel(meta, qmeta, qt_s, gt_s, kv, out, k_s, v_s, pos_s, items):
-    place_keys(meta, kv, k_s, v_s, pos_s)
-    rows = qt_s.shape[2]
+    return span, base, here, t, scores
+
+
+def stats_kernel(meta, qmeta, own, other, kv, out, q_s, g_s, k_s, v_s, pos_s, items):
+    load_operands(meta, own, other, kv, q_s, g_s, k_s, v_s, pos_s)
+    rows = qmeta.shape[1]
     out[0:4, :] = jnp.full((4, rows), NEG, jnp.float32)
     out[4:16, :] = jnp.zeros((12, rows), jnp.float32)
     groups = list_tiles(meta, items, 2)
@@ -110,10 +86,10 @@
     def group_step(group, carry):
         found = []
         for slot in range(2):
-            span, here, t, scores = tile_scores(items[group * 2 + slot], qmeta, qt_s, k_s, pos_s)
+            span, base, here, t, scores = tile_scores(items[group * 2 + slot], qmeta, q_s, k_s, pos_s)
             top = jnp.max(scores, axis=0, keepdims=True)
             probs = jnp.exp2(scores - top)
-            grad = nn(v_s[here, :], gt_s[span])
+            grad = nt(v_s[here, :], g_s[base, :])
             total = jnp.sum(probs, axis=0, keepdims=True)
             found.append((span, top, total, jnp.sum(probs * grad, axis=0, keepdims=True)))
         for span, top, total, weighted in found:
@@ -129,10 +105,11 @@
 
 
 def grad_kernel(
-    meta, qmeta, q_s, g_s, qt_s, gt_s, k_s, v_s, pos_s, stats, far, dq_own, dq_other, dkv,
-    items, kt_s, dk_s, dv_s, dq_s, fin_s,
+    meta, qmeta, own, other, kv, stats, far, dq_own, dq_other, dkv,
+    q_s, g_s, k_s, v_s, pos_s, items, kt_s, dk_s, dv_s, dq_s, fin_s,
 ):
-    rows = q_s.shape[0] // 4
+    load_operands(meta, own, other, kv, q_s, g_s, k_s, v_s, pos_s)
+    rows = qmeta.shape[1]
     heads = rows // SPAN
     tiles = k_s.shape[0] // TILE
     for t in range(tiles):
@@ -154,11 +131,10 @@
     def group_step(group, carry):
         found = []
         for slot in range(2):
-            span, here, t, scores = tile_scores(items[group * 2 + slot], qmeta, qt_s, k_s, pos_s)
+            span, base, here, t, scores = tile_scores(items[group * 2 + slot], qmeta, q_s, k_s, pos_s)
             probs = jnp.exp2(scores - fin_s[pl.ds(span, 1), :])
-            grad = nn(v_s[here, :], gt_s[span])
+            grad = nt(v_s[here, :], g_s[base, :])
             score_grad = (probs * (grad - fin_s[pl.ds(4 + span, 1), :])).astype(jnp.bfloat16)
-            base = pl.ds(pl.multiple_of(span * rows, rows), rows)
             found.append((
                 span, here, nn(probs.astype(jnp.bfloat16), g_s[base, :]), nn(score_grad, q_s[base, :]),
                 nn(kt_s[t], score_grad),
@@ -180,61 +156,64 @@
             else:
                 dq_other[half:half + SPAN, head * HEAD:(head + 1) * HEAD] = piece.astype(jnp.bfloat16)
 
+    depth = dkv.shape[0] // 2
+
     def unplace(block, carry):
         for half in range(2):
             start = pl.multiple_of(meta[0, 2 * block + half] * SPAN, SPAN)
             here = pl.ds(start, SPAN)
-            dkv[block, half * SPAN:(half + 1) * SPAN, :HEAD] = (dk_s[here, :] * SCALE).astype(jnp.bfloat16)
-            dkv[block, half * SPAN:(half + 1) * SPAN, HEAD:] = dv_s[here, :].astype(jnp.bfloat16)
+            there = lax.rem(block, depth) * 2 + lax.div(block, depth)
+            dkv[there, half * SPAN:(half + 1) * SPAN, :HEAD] = (dk_s[here, :] * SCALE).astype(jnp.bfloat16)
+            dkv[there, half * SPAN:(half + 1) * SPAN, HEAD:] = dv_s[here, :].astype(jnp.bfloat16)
         return carry
 
     lax.fori_loop(0, dkv.shape[0], unplace, 0)
 
 
-def item_scratch(keys):
-    return pltpu.SMEM((4 * (keys // TILE) + 8,), jnp.int32)
+def operand_scratch(rows, keys):
+    return [
+        pltpu.VMEM((4 * rows, HEAD), jnp.bfloat16),
+        pltpu.VMEM((4 * rows, HEAD), jnp.bfloat16),
+        pltpu.VMEM((keys, HEAD), jnp.bfloat16),
+        pltpu.VMEM((keys, HEAD), jnp.bfloat16),
+        pltpu.VMEM((keys, 128), jnp.int32),
+        pltpu.SMEM((4 * (keys // TILE) + 8,), jnp.int32),
+    ]
 
 
 def in_vmem(count):
     return [pl.BlockSpec(memory_space=pltpu.SMEM)] + [pl.BlockSpec(memory_space=pltpu.VMEM)] * count
 
 
-def stats_call(meta, qmeta, turned, kv):
-    rows = turned[0].shape[2]
+def stats_call(meta, qmeta, own, other, kv):
+    rows = qmeta.shape[1]
     keys = kv.shape[0] * kv.shape[1]
-    sorted_keys = jax.ShapeDtypeStruct((keys, HEAD), jnp.bfloat16)
     return pl.pallas_call(
         stats_kernel,
-        out_shape=[
-            jax.ShapeDtypeStruct((16, rows), jnp.float32),
-            sorted_keys,
-            sorted_keys,
-            jax.ShapeDtypeStruct((keys, 128), jnp.int32),
-        ],
+        out_shape=jax.ShapeDtypeStruct((16, rows), jnp.float32),
         in_specs=in_vmem(4),
-        out_specs=[pl.BlockSpec(memory_space=pltpu.VMEM)] * 4,
-        scratch_shapes=[item_scratch(keys)],
+        out_specs=pl.BlockSpec(memory_space=pltpu.VMEM),
+        scratch_shapes=operand_scratch(rows, keys),
         compiler_params=pltpu.CompilerParams(vmem_limit_bytes=VMEM_LIMIT),
         cost_estimate=pl.CostEstimate(flops=2 * 10**9, bytes_accessed=4 * 10**6, transcendentals=10**6),
         name="stats",
-    )(meta, qmeta, *turned, kv)
-
-
-def grad_call(meta, qmeta, laid, turned, placed, stats, far, shape, heads):
-    rows = turned[0].shape[2]
-    keys = shape[0] * shape[1]
-    height, width = 2 * SPAN, heads * HEAD
+    )(meta, qmeta, own, other, kv)
+
+
+def grad_call(meta, qmeta, own, other, kv, stats, far):
+    rows = qmeta.shape[1]
+    keys = kv.shape[0] * kv.shape[1]
+    height, width = 2 * SPAN, rows // SPAN * HEAD
     return pl.pallas_call(
         grad_kernel,
         out_shape=(
             jax.ShapeDtypeStruct((height, width), jnp.float32),
             jax.ShapeDtypeStruct((height, width), jnp.bfloat16),
-            jax.ShapeDtypeStruct(shape, jnp.bfloat16),
+            jax.ShapeDtypeStruct(kv.shape, jnp.bfloat16),
         ),
-        in_specs=in_vmem(10),
+        in_specs=in_vmem(6),
         out_specs=[pl.BlockSpec(memory_space=pltpu.VMEM)] * 3,
-        scratch_shapes=[
-            item_scratch(keys),
+        scratch_shapes=operand_scratch(rows, keys) + [
             pltpu.VMEM((keys // TILE, HEAD, TILE), jnp.bfloat16),
             pltpu.VMEM((keys, HEAD), jnp.float32),
             pltpu.VMEM((keys, HEAD), jnp.float32),
@@ -244,31 +223,69 @@
         compiler_params=pltpu.CompilerParams(vmem_limit_bytes=VMEM_LIMIT),
         cost_estimate=pl.CostEstimate(flops=5 * 10**9, bytes_accessed=6 * 10**6, transcendentals=10**6),
         name="grads",
-    )(meta, qmeta, *laid, *turned, *placed, stats, far)
-
-
-def reduce_copies_kernel(parts, copies, *halves):
+    )(meta, qmeta, own, other, kv, stats, far)
+
+
+def first_sum_kernel(place, parts, kept, sent):
+    for where, out in ((place[3], kept), (1 - place[3], sent)):
+        total = parts[where].astype(jnp.float32)
+        for level in range(1, parts.shape[0] // 2):
+            total += parts[2 * level + where].astype(jnp.float32)
+        out[...] = total.astype(out.dtype)
+
+
+def first_sum(place, parts):
+    shape = parts.shape[1:]
+    return pl.pallas_call(
+        first_sum_kernel,
+        out_shape=[jax.ShapeDtypeStruct(shape, jnp.float32), jax.ShapeDtypeStruct(shape, jnp.bfloat16)],
+        in_specs=in_vmem(1),
+        out_specs=[pl.BlockSpec(memory_space=pltpu.VMEM)] * 2,
+        compiler_params=pltpu.CompilerParams(vmem_limit_bytes=SMALL_LIMIT),
+        cost_estimate=pl.CostEstimate(flops=10**6, bytes_accessed=2 * 10**6, transcendentals=0),
+        name="first_sum",
+    )(place, parts)
+
+
+def second_sum_kernel(kept, got, copies, key_out, value_out):
+    rounded = (kept[...] + got[...].astype(jnp.float32)).astype(jnp.bfloat16)
+    for copy in range(copies.shape[0]):
+        copies[copy] = rounded
+    key_out[...] = rounded[:, :HEAD]
+    value_out[...] = rounded[:, HEAD:]
+
+
+def second_sum(kept, got, count):
+    height, width = kept.shape
+    half = jax.ShapeDtypeStruct((height, HEAD), jnp.bfloat16)
+    return pl.pallas_call(
+        second_sum_kernel,
+        out_shape=[jax.ShapeDtypeStruct((count, height, width), jnp.bfloat16), half, half],
+        in_specs=[pl.BlockSpec(memory_space=pltpu.VMEM)] * 2,
+        out_specs=[pl.BlockSpec(memory_space=pltpu.VMEM)] * 3,
+        compiler_params=pltpu.CompilerParams(vmem_limit_bytes=SMALL_LIMIT),
+        cost_estimate=pl.CostEstimate(flops=10**6, bytes_accessed=10**6, transcendentals=0),
+        name="second_sum",
+    )(kept, got)
+
+
+def sum_rows_kernel(parts, copies):
     total = parts[0].astype(jnp.float32)
     for part in range(1, parts.shape[0]):
         total += parts[part].astype(jnp.float32)
-    rounded = total.astype(copies.dtype)
     for copy in range(copies.shape[0]):
-        copies[copy] = rounded
-    for place, half in enumerate(halves):
-        half[...] = rounded[:, place * HEAD:(place + 1) * HEAD]
-
-
-def reduce_copies(parts, count, dtype, split, name):
-    height, width = parts.shape[1:]
-    halves = [jax.ShapeDtypeStruct((height, HEAD), dtype)] * (2 if split else 0)
-    return pl.pallas_call(
-        reduce_copies_kernel,
-        out_shape=[jax.ShapeDtypeStruct((count, height, width), dtype)] + halves,
+        copies[copy] = total
+
+
+def sum_rows(parts, count):
+    return pl.pallas_call(
+        sum_rows_kernel,
+        out_shape=jax.ShapeDtypeStruct((count,) + parts.shape[1:], jnp.float32),
         in_specs=[pl.BlockSpec(memory_space=pltpu.VMEM)],
-        out_specs=[pl.BlockSpec(memory_space=pltpu.VMEM)] * (1 + len(halves)),
+        out_specs=pl.BlockSpec(memory_space=pltpu.VMEM),
         compiler_params=pltpu.CompilerParams(vmem_limit_bytes=SMALL_LIMIT),
         cost_estimate=pl.CostEstimate(flops=10**6, bytes_accessed=2 * 10**6, transcendentals=0),
-        name=name,
+        name="sum_rows",
     )(parts)
 
 
@@ -280,9 +297,10 @@
     sources = [lax.rem(place[0] - back + count, count) * 2 for back in range(count)]
     here, there = place[2], 1 - place[2]
     right = jnp.concatenate([grads[s + here] for s in sources] + [grads[s + there] for s in sources], axis=0)
-    each = len(arrays) // 2
+    slabs = [(ref, i) for ref in arrays for i in range(ref.shape[0])]
+    each = len(slabs) // 2
     for high in range(2):
-        blocks = [ref[i] for ref in arrays[high * each:(high + 1) * each] for i in range(ref.shape[0])]
+        blocks = [ref[i] for ref, i in slabs[high * each:(high + 1) * each]]
         result = nn(jnp.concatenate(blocks, axis=1), right).astype(jnp.bfloat16)
         block = lax.bitwise_xor(place[1], high)
         for slot in range(slots):
@@ -347,7 +365,10 @@
     group_size = lax.axis_size("ya") * lax.axis_size("z")
     depth = lax.axis_size("z")
 
-    own = jnp.concatenate([queries, out_grad], axis=0)
+    def laid(array):
+        return array.reshape(2, SPAN, heads, HEAD).transpose(0, 2, 1, 3).reshape(heads * height, HEAD)
+
+    own = jnp.stack([laid(queries[0]), laid(out_grad[0])])
     other = swapped(own, "yb")
     pair = jnp.concatenate([keys[0], values[0]], axis=1)
     kv = lax.all_to_all(
@@ -380,33 +401,34 @@
                 ],
             )
         )
-    half = copies_of // 2
-    near_a = jnp.stack(columns[:half])
-
-    beside_a = swapped(near_a, "yh")
-    *laid, qt, gt = queries_call(own, other)
-    stats, *placed = stats_call(meta, qmeta, (qt, gt), kv)
-    stats, columns = lax.optimization_barrier((stats, columns[half:]))
-    near_b = jnp.stack(columns)
-    beside_b = swapped(near_b, "yh")
+    stats = stats_call(meta, qmeta, own, other, kv)
+    stats, columns = lax.optimization_barrier((stats, columns))
     far = swapped(stats, "yb")
-    far, beside_a = lax.optimization_barrier((far, beside_a))
-    dq_own, dq_other, dkv = grad_call(meta, qmeta, laid, (qt, gt), placed, stats, far, kv.shape, heads)
-    dkv, beside_b = lax.optimization_barrier((dkv, beside_b))
-    near, beside = [near_a, near_b], [beside_a, beside_b]
+    far, near = lax.optimization_barrier((far, jnp.stack(columns)))
+    dq_own, dq_other, dkv = grad_call(meta, qmeta, own, other, kv, stats, far)
+
+    place = jnp.stack(
+        [replica, lax.axis_index("yh"), lax.axis_index("core"), lax.axis_index("ya")]
+    ).astype(jnp.int32)
+    dkv, late = lax.optimization_barrier((dkv, near))
+    beside = swapped(late, "yh")
+    parts = lax.all_to_all(dkv, "z", 0, 0, tiled=True)
+    halves = late[:copies_of // 2], late[copies_of // 2:]
+    near_across = [swapped(part, "core") for part in halves]
+    parts, beside, near_across = lax.optimization_barrier((parts, beside, near_across))
+    kept, sent_grads = first_sum(place, parts)
+    got = swapped(sent_grads, "ya")
     dq_far = swapped(dq_other, "yb")
-    across = [swapped(part, "core") for part in (*near, *beside)]
-    parts = lax.all_to_all(dkv, group, 0, 0, tiled=True)
-    parts, across, dq_far = lax.optimization_barrier((parts, across, dq_far))
-    copies, key_grad, value_grad = reduce_copies(parts, 2 * copies_of, jnp.bfloat16, True, "sum_grads")
+    got, beside = lax.optimization_barrier((got, beside))
+    beside_across = swapped(beside, "core")
+    copies, key_grad, value_grad = second_sum(kept, got, 2 * copies_of)
+
+    all_grads = lax.all_to_all(copies, ("dp", "yb"), 0, 0, tiled=True)
+    blocks = weights_call(place, (late, *near_across, beside, beside_across), all_grads, depth)
+    pieces = lax.all_to_all(blocks, group, 0, 0, tiled=True)
+    spread = sum_rows(pieces, copies_of)
+    weight = lax.all_to_all(spread, "dp", 0, 0, tiled=True).reshape(copies_of * rows, 2 * HEAD)
     query_grad = (dq_own + dq_far.astype(jnp.float32)).astype(jnp.bfloat16)[None]
-
-    all_grads = lax.all_to_all(copies, ("dp", "yb"), 0, 0, tiled=True)
-    place = jnp.stack([replica, lax.axis_index("yh"), lax.axis_index("core")]).astype(jnp.int32)
-    blocks = weights_call(place, (*near, *across[:2], *beside, *across[2:]), all_grads, depth)
-    pieces = lax.all_to_all(blocks, group, 0, 0, tiled=True)
-    (spread,) = reduce_copies(pieces, copies_of, jnp.float32, False, "sum_rows")
-    weight = lax.all_to_all(spread, "dp", 0, 0, tiled=True).reshape(copies_of * rows, 2 * HEAD)
     return (query_grad, key_grad[None], value_grad[None], weight[:, :HEAD], weight[:, HEAD:])
 
 

time: 169 us -> 161 us (0.953)
  blocking collectives: 24.5 us -> 0 us
  waiting for transfers between devices: 32.5 us -> 56.5 us
  Pallas kernels: 17.6 us -> 12.9 us
  local copies, waits for them, and re-layouts: 11.5 us -> 7.51 us
    all_to_all x1 -> x0, blocking collectives: 24.5 us -> none  [shards(): pieces = lax.all_to_all(blocks, group, 0, 0, tiled=True)]
    all_to_all x1 -> x2, waiting for transfers between devices: 0.16 us -> 15.7 us  [the longest x1 15.7 us: shards(): pieces = lax.all_to_all(blocks, group, 0, 0, tiled=True)]
    all_to_all x1 -> x2, starting transfers between devices: 7.97 us -> 17.7 us  [the longest x1 10.4 us: shards(): parts = lax.all_to_all(dkv, 'z', 0, 0, tiled=True)]
    ppermute x9 -> x8, waiting for transfers between devices: 18.5 us -> 28.1 us  [swapped(): return lax.ppermute(array, axis, [(0, 1), (1, 0)])]
    all_to_all x1, waiting for transfers between devices: 8.94 us -> 1.09 us  [shards(): all_grads = lax.all_to_all(copies, ('dp', 'yb'), 0, 0, tiled=True)]
    all_to_all x1, waiting for transfers between devices: 0.01 us -> 6.21 us  [shards(): lax.all_to_all(jnp.broadcast_to(pair[None], (group_size,) + pair.shape),...]
    ppermute x9 -> x8, starting transfers between devices: 30.5 us -> 24.8 us  [swapped(): return lax.ppermute(array, axis, [(0, 1), (1, 0)])]
    unnamed x35 -> x22, local copies, waits for them, and re-layouts: 8 us -> 3.26 us
  transfers between devices with their start and end apart: 17 -> 17, of which waited for: 5 -> 11; matrix products, arithmetic and copies ran while one was open for 5% -> 5% of each run, Pallas kernels for 9% -> 2%
where the time goes in v4:
time: 161 us; the launch traced here: 160 us
  starting transfers between devices  75.7 us (47%)
  waiting for transfers between devices  56.5 us (35%)
  Pallas kernels  12.9 us (8%)
  local copies, waits for them, and re-layouts  7.51 us (5%)
  other arithmetic  5.03 us (3%)
  between operations  2.34 us (1%)
    ppermute x8, waiting for transfers between devices, swapped(): return lax.ppermute(array, axis, [(0, 1), (1, 0)])  28.1 us
    ppermute x8, starting transfers between devices, swapped(): return lax.ppermute(array, axis, [(0, 1), (1, 0)])  24.8 us
    all_to_all x1, waiting for transfers between devices, shards(): pieces = lax.all_to_all(blocks, group, 0, 0, tiled=True)  15.7 us
    ppermute x4, starting transfers between devices, shards(): lax.ppermute(slab, ('dp', 'yb', 'core'), [(d * 4 + b * 2 + c, (d + by) %...  13.9 us
    all_to_all x1, starting transfers between devices, shards(): lax.all_to_all(jnp.broadcast_to(pair[None], (group_size,) + pair.shape),...  12.3 us
    all_to_all x1, starting transfers between devices, shards(): parts = lax.all_to_all(dkv, 'z', 0, 0, tiled=True)  10.4 us
    all_to_all x1, starting transfers between devices, shards(): pieces = lax.all_to_all(blocks, group, 0, 0, tiled=True)  7.36 us
    all_to_all x1, waiting for transfers between devices, shards(): lax.all_to_all(jnp.broadcast_to(pair[None], (group_size,) + pair.shape),...  6.21 us
  transfers between devices with their start and end apart: 17, of which 11 were waited for; matrix products, arithmetic and copies ran while one was open for 5% of the time, Pallas kernels for 2%

profile of v4, /device:TPU:1, one launch (start us, length us, event | category | flops | bytes accessed | tf_op | source)
XLA Modules:
  0.0 160.0 jit_solution(1934860214716261031)
XLA Ops:
  0.6 1.0 copy.41
  1.6 0.0 copy-start.5
  1.7 0.9 copy-done.5
  2.7 0.1 pad_maximum_fusion.own
  2.8 4.0 %collective-permute-start = (bf16[2,1024,128]{2,1,0:T(8,128)(2,1)S(1)}, bf16[2,1024,128]{2,1,0:T(8,128)(2,1)S(1)}, u32[]{:S(2)}, u32[]{:S(2)}) collective-permute-start(bf16[2,1024,128]{2,1,0:T(8,128)(2,1)S(1)} %pad_maximum_fusion.own), channel_id=1, source_target_pairs={{0,32},{32,0},{1,33},{33,1},{2,34},{34,2},{3,35},{35,3},{4,36},{36... | collective-permute-start | bytes 1572872 | tf_op jit(solution)/shard_map/ppermute | solution.py:329
  6.9 1.1 broadcast_in_dim.43
  7.9 12.3 %all-to-all-start = ((bf16[16,128,256]{2,1,0:T(8,128)(2,1)}), bf16[16,128,256]{2,1,0:T(8,128)(2,1)S(1)}, u32[]{:S(2)}, u32[]{:S(2)}) async-start(bf16[16,128,256]{2,1,0:T(8,128)(2,1)} %broadcast_in_dim.43), calls=%async_computation | async-start | bytes 2097152 | tf_op jit(solution)/shard_map/all_to_all | solution.py:374
  20.3 0.6 copy-done.8
  20.9 0.1 reshape.195
  21.0 0.6 fusion.2
  21.7 0.1 select_n.68
  21.8 0.1 copy.34
  21.9 0.1 lt.41
  21.9 0.1 broadcast_in_dim_reshape.2
  23.4 0.6 copy-done.9
  24.0 0.2 reduce-window.8
  24.2 1.4 broadcast_multiply_fusion
  25.5 0.1 iota_add_fusion
  25.6 0.1 select_reduce_fusion
  25.7 0.1 iota_add_fusion.1
  25.8 0.1 tile.10.qmeta
  25.9 0.2 select_reduce_fusion.1
  26.1 0.2 convert_reduce_fusion.2
  26.3 0.1 add_bitcast_fusion
  26.4 0.2 convert_reduce_fusion
  26.6 0.3 copy.39
  27.0 0.7 dynamic-slice_bitcast_fusion
  27.7 5.4 %collective-permute-start.4 = (bf16[512,128]{1,0:T(8,128)(2,1)}, bf16[512,128]{1,0:T(8,128)(2,1)S(1)}, u32[]{:S(2)}, u32[]{:S(2)}) collective-permute-start(bf16[512,128]{1,0:T(8,128)(2,1)} %get-tuple-element.63), channel_id=1, source_target_pairs={{0,384},{1,416},{32,385},{33,417},{128,0},{129,32},{160,1},{161,33... | collective-permute-start | bytes 393224 | tf_op jit(solution)/shard_map/ppermute | solution.py:395
  33.0 2.6 %collective-permute-start.3 = (bf16[512,128]{1,0:T(8,128)(2,1)S(1)}, bf16[512,128]{1,0:T(8,128)(2,1)S(1)}, u32[]{:S(2)}, u32[]{:S(2)}) collective-permute-start(bf16[512,128]{1,0:T(8,128)(2,1)S(1)} %get-tuple-element.64), channel_id=1, source_target_pairs={{0,256},{1,288},{32,257},{33,289},{128,384},{129,416},{160,385},{1... | collective-permute-start | bytes 393224 | tf_op jit(solution)/shard_map/ppermute | solution.py:395
  35.7 3.5 %collective-permute-start.2 = (bf16[512,128]{1,0:T(8,128)(2,1)S(1)}, bf16[512,128]{1,0:T(8,128)(2,1)S(1)}, u32[]{:S(2)}, u32[]{:S(2)}) collective-permute-start(bf16[512,128]{1,0:T(8,128)(2,1)S(1)} %get-tuple-element.65), channel_id=1, source_target_pairs={{0,128},{1,160},{32,129},{33,161},{128,256},{129,288},{160,257},{1... | collective-permute-start | bytes 393224 | tf_op jit(solution)/shard_map/ppermute | solution.py:395
  39.2 2.4 %collective-permute-start.1 = (bf16[512,128]{1,0:T(8,128)(2,1)S(1)}, bf16[512,128]{1,0:T(8,128)(2,1)}, u32[]{:S(2)}, u32[]{:S(2)}) collective-permute-start(bf16[512,128]{1,0:T(8,128)(2,1)S(1)} %get-tuple-element.66), channel_id=1, source_target_pairs={{0,0},{1,32},{32,1},{33,33},{128,128},{129,160},{160,129},{161,161... | collective-permute-start | bytes 393224 | tf_op jit(solution)/shard_map/ppermute | solution.py:395
  41.6 6.2 %all-to-all-done.kv = bf16[16,128,256]{2,1,0:T(8,128)(2,1)S(1)} async-done(((bf16[16,128,256]{2,1,0:T(8,128)(2,1)}), bf16[16,128,256]{2,1,0:T(8,128)(2,1)S(1)}, u32[]{:S(2)}, u32[]{:S(2)}) %all-to-all-start) | async-done | bytes 1048608 | tf_op jit(solution)/shard_map/all_to_all | solution.py:374
  47.8 2.8 %stats.1 = f32[16,512]{1,0:T(8,128)S(1)} custom-call(s32[3,32]{1,0:T(4,128)S(1)} %pad_add_fusion.1.meta, s32[16,512]{1,0:T(8,128)S(1)} %tile.10.qmeta, bf16[2,1024,128]{2,1,0:T(8,128)(2,1)S(1)} %pad_maximum_fusion.own, bf16[2,1024,128]{2,1,0:T(8,128)(2,1)S(1)} %collective-permute-done.other, bf16[16,128,256]{2,1,0:T(8,128)(2,1)S(1)} %all-to-all-done.kv), custom_call_target="tpu_custom_call" | custom-call | flops 2000000000 | bytes 4000000 | tf_op jit(solution)/shard_map/stats/pallas_call | solution.py:191
  50.6 0.5 collective-permute-done.2
  51.2 0.1 collective-permute-done.1
  51.2 1.9 %collective-permute-start.5 = (f32[16,512]{1,0:T(8,128)S(1)}, f32[16,512]{1,0:T(8,128)S(1)}, u32[]{:S(2)}, u32[]{:S(2)}) collective-permute-start(f32[16,512]{1,0:T(8,128)S(1)} %stats.1), channel_id=1, source_target_pairs={{0,32},{32,0},{1,33},{33,1},{2,34},{34,2},{3,35},{35,3},{4,36},{36... | collective-permute-start | bytes 98312 | tf_op jit(solution)/shard_map/ppermute | solution.py:329
  53.1 1.0 pad_maximum_fusion.1.refs_0_
  54.1 1.8 %collective-permute-done.5.far = f32[16,512]{1,0:T(8,128)S(1)} collective-permute-done((f32[16,512]{1,0:T(8,128)S(1)}, f32[16,512]{1,0:T(8,128)S(1)}, u32[]{:S(2)}, u32[]{:S(2)}) %collective-permute-start.5) | collective-permute-done | bytes 32800 | tf_op jit(solution)/shard_map/ppermute | solution.py:329
  55.9 5.7 %grads.1 = (f32[128,1024]{1,0:T(8,128)S(1)}, bf16[128,1024]{1,0:T(8,128)(2,1)S(1)}, bf16[16,128,256]{2,1,0:T(8,128)(2,1)}) custom-call(s32[3,32]{1,0:T(4,128)S(1)} %pad_add_fusion.1.meta, s32[16,512]{1,0:T(8,128)S(1)} %tile.10.qmeta, bf16[2,1024,128]{2,1,0:T(8,128)(2,1)S(1)} %pad_maximum_fusion.own, bf16[2,1024,128]{2,1,0:T(8,128)(2,1)S(1)} %collective-permute-done.other, ...), custom_call_target="tpu_custom_call" | custom-call | flops 5000000000 | bytes 6000000 | tf_op jit(solution)/shard_map/grads/pallas_call | solution.py:207
  61.5 10.4 %all-to-all-start.1 = ((bf16[16,128,256]{2,1,0:T(8,128)(2,1)}), bf16[16,128,256]{2,1,0:T(8,128)(2,1)S(1)}, u32[]{:S(2)}, u32[]{:S(2)}) async-start(bf16[16,128,256]{2,1,0:T(8,128)(2,1)} %get-tuple-element.42), calls=%async_computation.1 | async-start | bytes 2097152 | tf_op jit(solution)/shard_map/all_to_all | solution.py:415
  71.9 2.8 %collective-permute-start.7 = (bf16[4,512,128]{2,1,0:T(8,128)(2,1)S(1)}, bf16[4,512,128]{2,1,0:T(8,128)(2,1)S(1)}, u32[]{:S(2)}, u32[]{:S(2)}) collective-permute-start(bf16[4,512,128]{2,1,0:T(8,128)(2,1)S(1)} %pad_maximum_fusion.1.refs_0_), channel_id=1, source_target_pairs={{0,2},{2,0},{1,3},{3,1},{4,6},{6,4},{5,7},{7,5},{8,10},{10,8},{9,1... | collective-permute-start | bytes 1572872 | tf_op jit(solution)/shard_map/ppermute | solution.py:329
  74.7 0.8 fusion.4
  75.6 5.2 %collective-permute-start.9 = (bf16[2,512,128]{2,1,0:T(8,128)(2,1)}, bf16[2,512,128]{2,1,0:T(8,128)(2,1)S(1)}, u32[]{:S(2)}, u32[]{:S(2)}) collective-permute-start(bf16[2,512,128]{2,1,0:T(8,128)(2,1)} %get-tuple-element.61), channel_id=1, source_target_pairs={{0,1},{1,0},{2,3},{3,2},{4,5},{5,4},{6,7},{7,6},{8,9},{9,8},{10,11... | collective-permute-start | bytes 786440 | tf_op jit(solution)/shard_map/ppermute | solution.py:329
  80.8 1.9 %collective-permute-start.8 = (bf16[2,512,128]{2,1,0:T(8,128)(2,1)}, bf16[2,512,128]{2,1,0:T(8,128)(2,1)S(1)}, u32[]{:S(2)}, u32[]{:S(2)}) collective-permute-start(bf16[2,512,128]{2,1,0:T(8,128)(2,1)} %get-tuple-element.62), channel_id=1, source_target_pairs={{0,1},{1,0},{2,3},{3,2},{4,5},{5,4},{6,7},{7,6},{8,9},{9,8},{10,11... | collective-permute-start | bytes 786440 | tf_op jit(solution)/shard_map/ppermute | solution.py:329
  82.7 0.1 pad_add_fusion.4.place
  82.8 1.6 %collective-permute-done.8.refs_1_ = bf16[2,512,128]{2,1,0:T(8,128)(2,1)S(1)} collective-permute-done((bf16[2,512,128]{2,1,0:T(8,128)(2,1)}, bf16[2,512,128]{2,1,0:T(8,128)(2,1)S(1)}, u32[]{:S(2)}, u32[]{:S(2)}) %collective-permute-start.8) | collective-permute-done | bytes 262176 | tf_op jit(solution)/shard_map/ppermute | solution.py:329
  84.4 17.4 %collective-permute-done.7.refs_3_ = bf16[4,512,128]{2,1,0:T(8,128)(2,1)S(1)} collective-permute-done((bf16[4,512,128]{2,1,0:T(8,128)(2,1)S(1)}, bf16[4,512,128]{2,1,0:T(8,128)(2,1)S(1)}, u32[]{:S(2)}, u32[]{:S(2)}) %collective-permute-start.7) | collective-permute-done | bytes 524320 | tf_op jit(solution)/shard_map/ppermute | solution.py:329
  101.9 0.7 first_sum.1
  102.6 1.9 %collective-permute-start.10 = (bf16[128,256]{1,0:T(8,128)(2,1)S(1)}, bf16[128,256]{1,0:T(8,128)(2,1)S(1)}, u32[]{:S(2)}, u32[]{:S(2)}) collective-permute-start(bf16[128,256]{1,0:T(8,128)(2,1)S(1)} %get-tuple-element.46), channel_id=1, source_target_pairs={{0,64},{64,0},{1,65},{65,1},{2,66},{66,2},{3,67},{67,3},{4,68},{68... | collective-permute-start | bytes 196616 | tf_op jit(solution)/shard_map/ppermute | solution.py:329
  104.5 5.8 %collective-permute-done.10.got = bf16[128,256]{1,0:T(8,128)(2,1)S(1)} collective-permute-done((bf16[128,256]{1,0:T(8,128)(2,1)S(1)}, bf16[128,256]{1,0:T(8,128)(2,1)S(1)}, u32[]{:S(2)}, u32[]{:S(2)}) %collective-permute-start.10) | collective-permute-done | bytes 65568 | tf_op jit(solution)/shard_map/ppermute | solution.py:329
  110.3 0.8 second_sum.1
  111.1 3.6 %all-to-all-start.2 = ((bf16[8,128,256]{2,1,0:T(8,128)(2,1)}), bf16[8,128,256]{2,1,0:T(8,128)(2,1)S(1)}, u32[]{:S(2)}, u32[]{:S(2)}) async-start(bf16[8,128,256]{2,1,0:T(8,128)(2,1)} %get-tuple-element.54), calls=%async_computation.2 | async-start | bytes 1048576 | tf_op jit(solution)/shard_map/all_to_all | solution.py:426
  114.8 4.9 %collective-permute-start.11 = (bf16[4,512,128]{2,1,0:T(8,128)(2,1)S(1)}, bf16[4,512,128]{2,1,0:T(8,128)(2,1)S(1)}, u32[]{:S(2)}, u32[]{:S(2)}) collective-permute-start(bf16[4,512,128]{2,1,0:T(8,128)(2,1)S(1)} %collective-permute-done.7.refs_3_), channel_id=1, source_target_pairs={{0,1},{1,0},{2,3},{3,2},{4,5},{5,4},{6,7},{7,6},{8,9},{9,8},{10,11... | collective-permute-start | bytes 1572872 | tf_op jit(solution)/shard_map/ppermute | solution.py:329
  119.7 1.5 collective-permute-done.11.refs_4_
  121.2 1.1 all-to-all-done.2.refs_5_
  122.3 2.1 %weights.1 = bf16[16,64,256]{2,1,0:T(8,128)(2,1)} custom-call(s32[4]{0:T(128)S(1)} %pad_add_fusion.4.place, bf16[4,512,128]{2,1,0:T(8,128)(2,1)S(1)} %pad_maximum_fusion.1.refs_0_, bf16[2,512,128]{2,1,0:T(8,128)(2,1)S(1)} %copy-done.3, bf16[2,512,128]{2,1,0:T(8,128)(2,1)S(1)} %copy-done.1, bf16[4,512,128]{2,1,0:T(8,128)(2,1)S(1)} %collective-permute-done.7.refs_3_, ...), custom_call_target="tpu_custom_call" | custom-call | flops 1000000000 | bytes 4000000 | tf_op jit(solution)/shard_map/weights/pallas_call | solution.py:312
  124.3 7.4 %all-to-all-start.3 = ((bf16[16,64,256]{2,1,0:T(8,128)(2,1)}), bf16[16,64,256]{2,1,0:T(8,128)(2,1)S(1)}, u32[]{:S(2)}, u32[]{:S(2)}) async-start(bf16[16,64,256]{2,1,0:T(8,128)(2,1)} %weights.1), calls=%async_computation.3 | async-start | bytes 1048576 | tf_op jit(solution)/shard_map/all_to_all | solution.py:428
  131.7 2.2 %collective-permute-start.6 = (bf16[128,1024]{1,0:T(8,128)(2,1)S(1)}, bf16[128,1024]{1,0:T(8,128)(2,1)S(1)}, u32[]{:S(2)}, u32[]{:S(2)}) collective-permute-start(bf16[128,1024]{1,0:T(8,128)(2,1)S(1)} %get-tuple-element.39), channel_id=1, source_target_pairs={{0,32},{32,0},{1,33},{33,1},{2,34},{34,2},{3,35},{35,3},{4,36},{36... | collective-permute-start | bytes 786440 | tf_op jit(solution)/shard_map/ppermute | solution.py:329
  133.9 15.7 %all-to-all-done.3.parts = bf16[16,64,256]{2,1,0:T(8,128)(2,1)S(1)} async-done(((bf16[16,64,256]{2,1,0:T(8,128)(2,1)}), bf16[16,64,256]{2,1,0:T(8,128)(2,1)S(1)}, u32[]{:S(2)}, u32[]{:S(2)}) %all-to-all-start.3) | async-done | bytes 524320 | tf_op jit(solution)/shard_map/all_to_all | solution.py:428
  149.5 0.8 sum_rows.1
  150.3 3.4 %all-to-all-start.4 = ((f32[4,64,256]{2,1,0:T(8,128)}), f32[4,64,256]{2,1,0:T(8,128)S(1)}, u32[]{:S(2)}, u32[]{:S(2)}) async-start(f32[4,64,256]{2,1,0:T(8,128)} %sum_rows.1), calls=%async_computation.4 | async-start | bytes 524288 | tf_op jit(solution)/shard_map/all_to_all | solution.py:430
  153.7 0.8 fusion
  154.5 4.8 %all-to-all-done.4 = f32[4,64,256]{2,1,0:T(8,128)S(1)} async-done(((f32[4,64,256]{2,1,0:T(8,128)}), f32[4,64,256]{2,1,0:T(8,128)S(1)}, u32[]{:S(2)}, u32[]{:S(2)}) %all-to-all-start.4) | async-done | bytes 262176 | tf_op jit(solution)/shard_map/all_to_all | solution.py:430
  159.3 0.7 fusion.5
  (38 shorter events, 0.3 us)
Async XLA Ops:
  1.6 1.0 copy-start.5
  2.7 4.1 %copy-start.6 = (bf16[1,128,128]{2,1,0:T(8,128)(2,1)S(1)}, bf16[1,128,128]{2,1,0:T(8,128)(2,1)}, u32[]{:S(2)}) copy-start(bf16[1,128,128]{2,1,0:T(8,128)(2,1)} %param.9) | copy-start | bytes 98308
  2.7 4.1 %copy-start.7 = (bf16[1,128,128]{2,1,0:T(8,128)(2,1)S(1)}, bf16[1,128,128]{2,1,0:T(8,128)(2,1)}, u32[]{:S(2)}) copy-start(bf16[1,128,128]{2,1,0:T(8,128)(2,1)} %param.8) | copy-start | bytes 98308
  2.8 23.8 %collective-permute-start = (bf16[2,1024,128]{2,1,0:T(8,128)(2,1)S(1)}, bf16[2,1024,128]{2,1,0:T(8,128)(2,1)S(1)}, u32[]{:S(2)}, u32[]{:S(2)}) collective-permute-start(bf16[2,1024,128]{2,1,0:T(8,128)(2,1)S(1)} %pad_maximum_fusion.own), channel_id=1, source_target_pairs={{0,32},{32,0},{1,33},{33,1},{2,34},{34,2},{3,35},{35,3},{4,36},{36... | collective-permute-start | bytes 1572872 | tf_op jit(solution)/shard_map/ppermute | solution.py:329
  7.9 18.7 %copy-start.4 = (bf16[1,128,2048]{2,1,0:T(8,128)(2,1)S(1)}, bf16[1,128,2048]{2,1,0:T(8,128)(2,1)}, u32[]{:S(2)}) copy-start(bf16[1,128,2048]{2,1,0:T(8,128)(2,1)} %param.11) | copy-start | bytes 1572868
  7.9 39.8 %all-to-all-start = ((bf16[16,128,256]{2,1,0:T(8,128)(2,1)}), bf16[16,128,256]{2,1,0:T(8,128)(2,1)S(1)}, u32[]{:S(2)}, u32[]{:S(2)}) async-start(bf16[16,128,256]{2,1,0:T(8,128)(2,1)} %broadcast_in_dim.43), calls=%async_computation | async-start | bytes 2097152 | tf_op jit(solution)/shard_map/all_to_all | solution.py:374
  20.3 0.7 copy-start.8
  23.3 0.7 copy-start.9
  27.7 23.0 %collective-permute-start.4 = (bf16[512,128]{1,0:T(8,128)(2,1)}, bf16[512,128]{1,0:T(8,128)(2,1)S(1)}, u32[]{:S(2)}, u32[]{:S(2)}) collective-permute-start(bf16[512,128]{1,0:T(8,128)(2,1)} %get-tuple-element.63), channel_id=1, source_target_pairs={{0,384},{1,416},{32,385},{33,417},{128,0},{129,32},{160,1},{161,33... | collective-permute-start | bytes 393224 | tf_op jit(solution)/shard_map/ppermute | solution.py:395
  33.0 17.6 %collective-permute-start.3 = (bf16[512,128]{1,0:T(8,128)(2,1)S(1)}, bf16[512,128]{1,0:T(8,128)(2,1)S(1)}, u32[]{:S(2)}, u32[]{:S(2)}) collective-permute-start(bf16[512,128]{1,0:T(8,128)(2,1)S(1)} %get-tuple-element.64), channel_id=1, source_target_pairs={{0,256},{1,288},{32,257},{33,289},{128,384},{129,416},{160,385},{1... | collective-permute-start | bytes 393224 | tf_op jit(solution)/shard_map/ppermute | solution.py:395
  35.7 15.5 %collective-permute-start.2 = (bf16[512,128]{1,0:T(8,128)(2,1)S(1)}, bf16[512,128]{1,0:T(8,128)(2,1)S(1)}, u32[]{:S(2)}, u32[]{:S(2)}) collective-permute-start(bf16[512,128]{1,0:T(8,128)(2,1)S(1)} %get-tuple-element.65), channel_id=1, source_target_pairs={{0,128},{1,160},{32,129},{33,161},{128,256},{129,288},{160,257},{1... | collective-permute-start | bytes 393224 | tf_op jit(solution)/shard_map/ppermute | solution.py:395
  39.2 12.0 %collective-permute-start.1 = (bf16[512,128]{1,0:T(8,128)(2,1)S(1)}, bf16[512,128]{1,0:T(8,128)(2,1)}, u32[]{:S(2)}, u32[]{:S(2)}) collective-permute-start(bf16[512,128]{1,0:T(8,128)(2,1)S(1)} %get-tuple-element.66), channel_id=1, source_target_pairs={{0,0},{1,32},{32,1},{33,33},{128,128},{129,160},{160,129},{161,161... | collective-permute-start | bytes 393224 | tf_op jit(solution)/shard_map/ppermute | solution.py:395
  51.2 4.6 %collective-permute-start.5 = (f32[16,512]{1,0:T(8,128)S(1)}, f32[16,512]{1,0:T(8,128)S(1)}, u32[]{:S(2)}, u32[]{:S(2)}) collective-permute-start(f32[16,512]{1,0:T(8,128)S(1)} %stats.1), channel_id=1, source_target_pairs={{0,32},{32,0},{1,33},{33,1},{2,34},{34,2},{3,35},{35,3},{4,36},{36... | collective-permute-start | bytes 98312 | tf_op jit(solution)/shard_map/ppermute | solution.py:329
  61.5 40.3 %all-to-all-start.1 = ((bf16[16,128,256]{2,1,0:T(8,128)(2,1)}), bf16[16,128,256]{2,1,0:T(8,128)(2,1)S(1)}, u32[]{:S(2)}, u32[]{:S(2)}) async-start(bf16[16,128,256]{2,1,0:T(8,128)(2,1)} %get-tuple-element.42), calls=%async_computation.1 | async-start | bytes 2097152 | tf_op jit(solution)/shard_map/all_to_all | solution.py:415
  71.9 29.9 %collective-permute-start.7 = (bf16[4,512,128]{2,1,0:T(8,128)(2,1)S(1)}, bf16[4,512,128]{2,1,0:T(8,128)(2,1)S(1)}, u32[]{:S(2)}, u32[]{:S(2)}) collective-permute-start(bf16[4,512,128]{2,1,0:T(8,128)(2,1)S(1)} %pad_maximum_fusion.1.refs_0_), channel_id=1, source_target_pairs={{0,2},{2,0},{1,3},{3,1},{4,6},{6,4},{5,7},{7,5},{8,10},{10,8},{9,1... | collective-permute-start | bytes 1572872 | tf_op jit(solution)/shard_map/ppermute | solution.py:329
  75.6 7.2 %collective-permute-start.9 = (bf16[2,512,128]{2,1,0:T(8,128)(2,1)}, bf16[2,512,128]{2,1,0:T(8,128)(2,1)S(1)}, u32[]{:S(2)}, u32[]{:S(2)}) collective-permute-start(bf16[2,512,128]{2,1,0:T(8,128)(2,1)} %get-tuple-element.61), channel_id=1, source_target_pairs={{0,1},{1,0},{2,3},{3,2},{4,5},{5,4},{6,7},{7,6},{8,9},{9,8},{10,11... | collective-permute-start | bytes 786440 | tf_op jit(solution)/shard_map/ppermute | solution.py:329
  80.8 3.6 %collective-permute-start.8 = (bf16[2,512,128]{2,1,0:T(8,128)(2,1)}, bf16[2,512,128]{2,1,0:T(8,128)(2,1)S(1)}, u32[]{:S(2)}, u32[]{:S(2)}) collective-permute-start(bf16[2,512,128]{2,1,0:T(8,128)(2,1)} %get-tuple-element.62), channel_id=1, source_target_pairs={{0,1},{1,0},{2,3},{3,2},{4,5},{5,4},{6,7},{7,6},{8,9},{9,8},{10,11... | collective-permute-start | bytes 786440 | tf_op jit(solution)/shard_map/ppermute | solution.py:329
  82.8 19.8 %copy-start = (bf16[2,512,128]{2,1,0:T(8,128)(2,1)}, bf16[2,512,128]{2,1,0:T(8,128)(2,1)S(1)}, u32[]{:S(2)}) copy-start(bf16[2,512,128]{2,1,0:T(8,128)(2,1)S(1)} %collective-permute-done.9.refs_2_) | copy-start | bytes 786436
  84.4 18.2 %copy-start.2 = (bf16[2,512,128]{2,1,0:T(8,128)(2,1)}, bf16[2,512,128]{2,1,0:T(8,128)(2,1)S(1)}, u32[]{:S(2)}) copy-start(bf16[2,512,128]{2,1,0:T(8,128)(2,1)S(1)} %collective-permute-done.8.refs_1_) | copy-start | bytes 786436
  102.6 7.7 %collective-permute-start.10 = (bf16[128,256]{1,0:T(8,128)(2,1)S(1)}, bf16[128,256]{1,0:T(8,128)(2,1)S(1)}, u32[]{:S(2)}, u32[]{:S(2)}) collective-permute-start(bf16[128,256]{1,0:T(8,128)(2,1)S(1)} %get-tuple-element.46), channel_id=1, source_target_pairs={{0,64},{64,0},{1,65},{65,1},{2,66},{66,2},{3,67},{67,3},{4,68},{68... | collective-permute-start | bytes 196616 | tf_op jit(solution)/shard_map/ppermute | solution.py:329
  111.1 11.1 %copy-start.1 = (bf16[2,512,128]{2,1,0:T(8,128)(2,1)S(1)}, bf16[2,512,128]{2,1,0:T(8,128)(2,1)}, u32[]{:S(2)}) copy-start(bf16[2,512,128]{2,1,0:T(8,128)(2,1)} %copy-done) | copy-start | bytes 786436
  111.1 11.1 %copy-start.3 = (bf16[2,512,128]{2,1,0:T(8,128)(2,1)S(1)}, bf16[2,512,128]{2,1,0:T(8,128)(2,1)}, u32[]{:S(2)}) copy-start(bf16[2,512,128]{2,1,0:T(8,128)(2,1)} %copy-done.2) | copy-start | bytes 786436
  111.1 11.1 %all-to-all-start.2 = ((bf16[8,128,256]{2,1,0:T(8,128)(2,1)}), bf16[8,128,256]{2,1,0:T(8,128)(2,1)S(1)}, u32[]{:S(2)}, u32[]{:S(2)}) async-start(bf16[8,128,256]{2,1,0:T(8,128)(2,1)} %get-tuple-element.54), calls=%async_computation.2 | async-start | bytes 1048576 | tf_op jit(solution)/shard_map/all_to_all | solution.py:426
  114.8 6.4 %collective-permute-start.11 = (bf16[4,512,128]{2,1,0:T(8,128)(2,1)S(1)}, bf16[4,512,128]{2,1,0:T(8,128)(2,1)S(1)}, u32[]{:S(2)}, u32[]{:S(2)}) collective-permute-start(bf16[4,512,128]{2,1,0:T(8,128)(2,1)S(1)} %collective-permute-done.7.refs_3_), channel_id=1, source_target_pairs={{0,1},{1,0},{2,3},{3,2},{4,5},{5,4},{6,7},{7,6},{8,9},{9,8},{10,11... | collective-permute-start | bytes 1572872 | tf_op jit(solution)/shard_map/ppermute | solution.py:329
  124.3 25.2 %all-to-all-start.3 = ((bf16[16,64,256]{2,1,0:T(8,128)(2,1)}), bf16[16,64,256]{2,1,0:T(8,128)(2,1)S(1)}, u32[]{:S(2)}, u32[]{:S(2)}) async-start(bf16[16,64,256]{2,1,0:T(8,128)(2,1)} %weights.1), calls=%async_computation.3 | async-start | bytes 1048576 | tf_op jit(solution)/shard_map/all_to_all | solution.py:428
  131.7 22.0 %collective-permute-start.6 = (bf16[128,1024]{1,0:T(8,128)(2,1)S(1)}, bf16[128,1024]{1,0:T(8,128)(2,1)S(1)}, u32[]{:S(2)}, u32[]{:S(2)}) collective-permute-start(bf16[128,1024]{1,0:T(8,128)(2,1)S(1)} %get-tuple-element.39), channel_id=1, source_target_pairs={{0,32},{32,0},{1,33},{33,1},{2,34},{34,2},{3,35},{35,3},{4,36},{36... | collective-permute-start | bytes 786440 | tf_op jit(solution)/shard_map/ppermute | solution.py:329
  150.3 8.9 %all-to-all-start.4 = ((f32[4,64,256]{2,1,0:T(8,128)}), f32[4,64,256]{2,1,0:T(8,128)S(1)}, u32[]{:S(2)}, u32[]{:S(2)}) async-start(f32[4,64,256]{2,1,0:T(8,128)} %sum_rows.1), calls=%async_computation.4 | async-start | bytes 524288 | tf_op jit(solution)/shard_map/all_to_all | solution.py:430

commit v5 on v4

--- a/solution.py
+++ b/solution.py
@@ -20,6 +20,10 @@
     return lax.dot_general(left, right, (((1,), (1,)), ((), ())), preferred_element_type=jnp.float32)
 
 
+def tn(left, right):
+    return lax.dot_general(left, right, (((0,), (0,)), ((), ())), preferred_element_type=jnp.float32)
+
+
 def nn(left, right):
     return lax.dot_general(left, right, (((1,), (0,)), ((), ())), preferred_element_type=jnp.float32)
 
@@ -41,13 +45,13 @@
             pos_s[pl.ds(start, SPAN), :] = lane_rows + meta[1, span] * SPAN
         return carry
 
-    lax.fori_loop(0, kv.shape[0], place, 0)
+    lax.fori_loop(0, kv.shape[0], place, 0, unroll=True)
 
 
 def masked_scores(k_tile, q_rows, pos_tile, q_pos, q_start):
     copies = q_rows.shape[0] // 128
     key_pos = jnp.concatenate([pos_tile] * copies, axis=1)
-    mask = (key_pos <= q_pos) & (key_pos >= q_start)
+    mask = (key_pos - q_start).astype(jnp.uint32) <= (q_pos - q_start).astype(jnp.uint32)
     return jnp.where(mask, nt(k_tile, q_rows) * (SCALE * LOG2E), NEG)
 
 
@@ -106,14 +110,11 @@
 
 def grad_kernel(
     meta, qmeta, own, other, kv, stats, far, dq_own, dq_other, dkv,
-    q_s, g_s, k_s, v_s, pos_s, items, kt_s, dk_s, dv_s, dq_s, fin_s,
+    q_s, g_s, k_s, v_s, pos_s, items, dk_s, dv_s, dq_s, fin_s,
 ):
     load_operands(meta, own, other, kv, q_s, g_s, k_s, v_s, pos_s)
     rows = qmeta.shape[1]
     heads = rows // SPAN
-    tiles = k_s.shape[0] // TILE
-    for t in range(tiles):
-        kt_s[t] = k_s[t * TILE:(t + 1) * TILE, :].T
     dk_s[...] = jnp.zeros_like(dk_s)
     dv_s[...] = jnp.zeros_like(dv_s)
     dq_s[...] = jnp.zeros_like(dq_s)
@@ -137,7 +138,7 @@
             score_grad = (probs * (grad - fin_s[pl.ds(4 + span, 1), :])).astype(jnp.bfloat16)
             found.append((
                 span, here, nn(probs.astype(jnp.bfloat16), g_s[base, :]), nn(score_grad, q_s[base, :]),
-                nn(kt_s[t], score_grad),
+                tn(k_s[here, :], score_grad),
             ))
         for span, here, value_part, key_part, query_part in found:
             dv_s[here, :] += value_part
@@ -167,7 +168,7 @@
             dkv[there, half * SPAN:(half + 1) * SPAN, HEAD:] = dv_s[here, :].astype(jnp.bfloat16)
         return carry
 
-    lax.fori_loop(0, dkv.shape[0], unplace, 0)
+    lax.fori_loop(0, dkv.shape[0], unplace, 0, unroll=True)
 
 
 def operand_scratch(rows, keys):
@@ -214,7 +215,6 @@
         in_specs=in_vmem(6),
         out_specs=[pl.BlockSpec(memory_space=pltpu.VMEM)] * 3,
         scratch_shapes=operand_scratch(rows, keys) + [
-            pltpu.VMEM((keys // TILE, HEAD, TILE), jnp.bfloat16),
             pltpu.VMEM((keys, HEAD), jnp.float32),
             pltpu.VMEM((keys, HEAD), jnp.float32),
             pltpu.VMEM((4, HEAD, rows), jnp.float32),
@@ -318,11 +318,6 @@
         cost_estimate=pl.CostEstimate(flops=10**9, bytes_accessed=4 * 10**6, transcendentals=0),
         name="weights",
     )(place, *arrays, grads)
-
-
-def around(array, axis, by):
-    size = lax.axis_size(axis)
-    return lax.ppermute(array, axis, [(i, (i + by) % size) for i in range(size)])
 
 
 def swapped(array, axis):

time: 161 us -> 160 us (level)
  Pallas kernels: 12.9 us -> 10.6 us
    all_to_all x1, starting transfers between devices: 10.4 us -> 13.7 us  [shards(): parts = lax.all_to_all(dkv, 'z', 0, 0, tiled=True)]
    all_to_all x1, waiting for transfers between devices: 1.09 us -> 3.33 us  [shards(): all_grads = lax.all_to_all(copies, ('dp', 'yb'), 0, 0, tiled=True)]
    ppermute x8, waiting for transfers between devices: 28.1 us -> 26 us  [swapped(): return lax.ppermute(array, axis, [(0, 1), (1, 0)])]
    ppermute x8, starting transfers between devices: 24.8 us -> 23 us  [swapped(): return lax.ppermute(array, axis, [(0, 1), (1, 0)])]
  transfers between devices with their start and end apart: 17 -> 17, of which waited for: 11 -> 12; matrix products, arithmetic and copies ran while one was open for 5% -> 5% of each run, Pallas kernels for 2% -> 2%
where the time goes in v5:
time: 160 us; the launch traced here: 159 us
  starting transfers between devices  76.7 us (48%)
  waiting for transfers between devices  57.3 us (36%)
  Pallas kernels  10.6 us (7%)
  local copies, waits for them, and re-layouts  7.51 us (5%)
  other arithmetic  5.03 us (3%)
  between operations  2.34 us (1%)
    ppermute x8, waiting for transfers between devices, swapped(): return lax.ppermute(array, axis, [(0, 1), (1, 0)])  26 us
    ppermute x8, starting transfers between devices, swapped(): return lax.ppermute(array, axis, [(0, 1), (1, 0)])  23 us
    all_to_all x1, waiting for transfers between devices, shards(): pieces = lax.all_to_all(blocks, group, 0, 0, tiled=True)  15.5 us
    ppermute x4, starting transfers between devices, shards(): lax.ppermute(slab, ('dp', 'yb', 'core'), [(d * 4 + b * 2 + c, (d + by) %...  13.9 us
    all_to_all x1, starting transfers between devices, shards(): parts = lax.all_to_all(dkv, 'z', 0, 0, tiled=True)  13.7 us
    all_to_all x1, starting transfers between devices, shards(): lax.all_to_all(jnp.broadcast_to(pair[None], (group_size,) + pair.shape),...  12.3 us
    all_to_all x1, starting transfers between devices, shards(): pieces = lax.all_to_all(blocks, group, 0, 0, tiled=True)  6.84 us
    all_to_all x1, waiting for transfers between devices, shards(): lax.all_to_all(jnp.broadcast_to(pair[None], (group_size,) + pair.shape),...  6.21 us
  transfers between devices with their start and end apart: 17, of which 12 were waited for; matrix products, arithmetic and copies ran while one was open for 5% of the time, Pallas kernels for 2%

profile of v5, /device:TPU:1, one launch (start us, length us, event | category | flops | bytes accessed | tf_op | source)
XLA Modules:
  0.0 159.5 jit_solution(4847983451715231742)
XLA Ops:
  0.6 1.0 copy.41
  1.7 0.9 copy-done.5
  2.7 0.1 pad_maximum_fusion.own
  2.8 4.0 %collective-permute-start = (bf16[2,1024,128]{2,1,0:T(8,128)(2,1)S(1)}, bf16[2,1024,128]{2,1,0:T(8,128)(2,1)S(1)}, u32[]{:S(2)}, u32[]{:S(2)}) collective-permute-start(bf16[2,1024,128]{2,1,0:T(8,128)(2,1)S(1)} %pad_maximum_fusion.own), channel_id=1, source_target_pairs={{0,32},{32,0},{1,33},{33,1},{2,34},{34,2},{3,35},{35,3},{4,36},{36... | collective-permute-start | bytes 1572872 | tf_op jit(solution)/shard_map/ppermute | solution.py:324
  6.9 1.1 broadcast_in_dim.43
  7.9 12.3 %all-to-all-start = ((bf16[16,128,256]{2,1,0:T(8,128)(2,1)}), bf16[16,128,256]{2,1,0:T(8,128)(2,1)S(1)}, u32[]{:S(2)}, u32[]{:S(2)}) async-start(bf16[16,128,256]{2,1,0:T(8,128)(2,1)} %broadcast_in_dim.43), calls=%async_computation | async-start | bytes 2097152 | tf_op jit(solution)/shard_map/all_to_all | solution.py:369
  20.3 0.6 copy-done.8
  20.9 0.1 reshape.195
  21.0 0.6 fusion.2
  21.7 0.1 select_n.68
  21.8 0.1 copy.34
  21.9 0.1 lt.41
  21.9 0.1 broadcast_in_dim_reshape.2
  23.4 0.6 copy-done.9
  24.0 0.2 reduce-window.8
  24.2 1.4 broadcast_multiply_fusion
  25.5 0.1 iota_add_fusion
  25.6 0.1 select_reduce_fusion
  25.7 0.1 iota_add_fusion.1
  25.8 0.1 tile.10.qmeta
  25.9 0.2 select_reduce_fusion.1
  26.1 0.2 convert_reduce_fusion.2
  26.3 0.1 add_bitcast_fusion
  26.4 0.2 convert_reduce_fusion
  26.6 0.3 copy.39
  27.0 0.7 dynamic-slice_bitcast_fusion
  27.7 5.4 %collective-permute-start.4 = (bf16[512,128]{1,0:T(8,128)(2,1)}, bf16[512,128]{1,0:T(8,128)(2,1)S(1)}, u32[]{:S(2)}, u32[]{:S(2)}) collective-permute-start(bf16[512,128]{1,0:T(8,128)(2,1)} %get-tuple-element.63), channel_id=1, source_target_pairs={{0,384},{1,416},{32,385},{33,417},{128,0},{129,32},{160,1},{161,33... | collective-permute-start | bytes 393224 | tf_op jit(solution)/shard_map/ppermute | solution.py:390
  33.0 2.6 %collective-permute-start.3 = (bf16[512,128]{1,0:T(8,128)(2,1)S(1)}, bf16[512,128]{1,0:T(8,128)(2,1)S(1)}, u32[]{:S(2)}, u32[]{:S(2)}) collective-permute-start(bf16[512,128]{1,0:T(8,128)(2,1)S(1)} %get-tuple-element.64), channel_id=1, source_target_pairs={{0,256},{1,288},{32,257},{33,289},{128,384},{129,416},{160,385},{1... | collective-permute-start | bytes 393224 | tf_op jit(solution)/shard_map/ppermute | solution.py:390
  35.7 3.5 %collective-permute-start.2 = (bf16[512,128]{1,0:T(8,128)(2,1)S(1)}, bf16[512,128]{1,0:T(8,128)(2,1)S(1)}, u32[]{:S(2)}, u32[]{:S(2)}) collective-permute-start(bf16[512,128]{1,0:T(8,128)(2,1)S(1)} %get-tuple-element.65), channel_id=1, source_target_pairs={{0,128},{1,160},{32,129},{33,161},{128,256},{129,288},{160,257},{1... | collective-permute-start | bytes 393224 | tf_op jit(solution)/shard_map/ppermute | solution.py:390
  39.2 2.4 %collective-permute-start.1 = (bf16[512,128]{1,0:T(8,128)(2,1)S(1)}, bf16[512,128]{1,0:T(8,128)(2,1)}, u32[]{:S(2)}, u32[]{:S(2)}) collective-permute-start(bf16[512,128]{1,0:T(8,128)(2,1)S(1)} %get-tuple-element.66), channel_id=1, source_target_pairs={{0,0},{1,32},{32,1},{33,33},{128,128},{129,160},{160,129},{161,161... | collective-permute-start | bytes 393224 | tf_op jit(solution)/shard_map/ppermute | solution.py:390
  41.6 6.2 %all-to-all-done.kv = bf16[16,128,256]{2,1,0:T(8,128)(2,1)S(1)} async-done(((bf16[16,128,256]{2,1,0:T(8,128)(2,1)}), bf16[16,128,256]{2,1,0:T(8,128)(2,1)S(1)}, u32[]{:S(2)}, u32[]{:S(2)}) %all-to-all-start) | async-done | bytes 1048608 | tf_op jit(solution)/shard_map/all_to_all | solution.py:369
  47.8 2.0 %stats.1 = f32[16,512]{1,0:T(8,128)S(1)} custom-call(s32[3,32]{1,0:T(4,128)S(1)} %pad_add_fusion.1.meta, s32[16,512]{1,0:T(8,128)S(1)} %tile.10.qmeta, bf16[2,1024,128]{2,1,0:T(8,128)(2,1)S(1)} %pad_maximum_fusion.own, bf16[2,1024,128]{2,1,0:T(8,128)(2,1)S(1)} %collective-permute-done.other, bf16[16,128,256]{2,1,0:T(8,128)(2,1)S(1)} %all-to-all-done.kv), custom_call_target="tpu_custom_call" | custom-call | flops 2000000000 | bytes 4000000 | tf_op jit(solution)/shard_map/stats/pallas_call | solution.py:192
  49.8 1.4 collective-permute-done.2
  51.2 0.1 collective-permute-done.1
  51.2 1.9 %collective-permute-start.5 = (f32[16,512]{1,0:T(8,128)S(1)}, f32[16,512]{1,0:T(8,128)S(1)}, u32[]{:S(2)}, u32[]{:S(2)}) collective-permute-start(f32[16,512]{1,0:T(8,128)S(1)} %stats.1), channel_id=1, source_target_pairs={{0,32},{32,0},{1,33},{33,1},{2,34},{34,2},{3,35},{35,3},{4,36},{36... | collective-permute-start | bytes 98312 | tf_op jit(solution)/shard_map/ppermute | solution.py:324
  53.1 1.0 pad_maximum_fusion.1.refs_0_
  54.1 1.8 %collective-permute-done.5.far = f32[16,512]{1,0:T(8,128)S(1)} collective-permute-done((f32[16,512]{1,0:T(8,128)S(1)}, f32[16,512]{1,0:T(8,128)S(1)}, u32[]{:S(2)}, u32[]{:S(2)}) %collective-permute-start.5) | collective-permute-done | bytes 32800 | tf_op jit(solution)/shard_map/ppermute | solution.py:324
  55.9 4.2 %grads.1 = (f32[128,1024]{1,0:T(8,128)S(1)}, bf16[128,1024]{1,0:T(8,128)(2,1)S(1)}, bf16[16,128,256]{2,1,0:T(8,128)(2,1)}) custom-call(s32[3,32]{1,0:T(4,128)S(1)} %pad_add_fusion.1.meta, s32[16,512]{1,0:T(8,128)S(1)} %tile.10.qmeta, bf16[2,1024,128]{2,1,0:T(8,128)(2,1)S(1)} %pad_maximum_fusion.own, bf16[2,1024,128]{2,1,0:T(8,128)(2,1)S(1)} %collective-permute-done.other, ...), custom_call_target="tpu_custom_call" | custom-call | flops 5000000000 | bytes 6000000 | tf_op jit(solution)/shard_map/grads/pallas_call | solution.py:208
  60.1 13.7 %all-to-all-start.1 = ((bf16[16,128,256]{2,1,0:T(8,128)(2,1)}), bf16[16,128,256]{2,1,0:T(8,128)(2,1)S(1)}, u32[]{:S(2)}, u32[]{:S(2)}) async-start(bf16[16,128,256]{2,1,0:T(8,128)(2,1)} %get-tuple-element.42), calls=%async_computation.1 | async-start | bytes 2097152 | tf_op jit(solution)/shard_map/all_to_all | solution.py:410
  73.8 2.4 %collective-permute-start.7 = (bf16[4,512,128]{2,1,0:T(8,128)(2,1)S(1)}, bf16[4,512,128]{2,1,0:T(8,128)(2,1)S(1)}, u32[]{:S(2)}, u32[]{:S(2)}) collective-permute-start(bf16[4,512,128]{2,1,0:T(8,128)(2,1)S(1)} %pad_maximum_fusion.1.refs_0_), channel_id=1, source_target_pairs={{0,2},{2,0},{1,3},{3,1},{4,6},{6,4},{5,7},{7,5},{8,10},{10,8},{9,1... | collective-permute-start | bytes 1572872 | tf_op jit(solution)/shard_map/ppermute | solution.py:324
  76.2 0.8 fusion.4
  77.0 5.0 %collective-permute-start.9 = (bf16[2,512,128]{2,1,0:T(8,128)(2,1)}, bf16[2,512,128]{2,1,0:T(8,128)(2,1)S(1)}, u32[]{:S(2)}, u32[]{:S(2)}) collective-permute-start(bf16[2,512,128]{2,1,0:T(8,128)(2,1)} %get-tuple-element.61), channel_id=1, source_target_pairs={{0,1},{1,0},{2,3},{3,2},{4,5},{5,4},{6,7},{7,6},{8,9},{9,8},{10,11... | collective-permute-start | bytes 786440 | tf_op jit(solution)/shard_map/ppermute | solution.py:324
  82.0 1.9 %collective-permute-start.8 = (bf16[2,512,128]{2,1,0:T(8,128)(2,1)}, bf16[2,512,128]{2,1,0:T(8,128)(2,1)S(1)}, u32[]{:S(2)}, u32[]{:S(2)}) collective-permute-start(bf16[2,512,128]{2,1,0:T(8,128)(2,1)} %get-tuple-element.62), channel_id=1, source_target_pairs={{0,1},{1,0},{2,3},{3,2},{4,5},{5,4},{6,7},{7,6},{8,9},{9,8},{10,11... | collective-permute-start | bytes 786440 | tf_op jit(solution)/shard_map/ppermute | solution.py:324
  84.0 0.1 pad_add_fusion.4.place
  84.0 1.6 %collective-permute-done.8.refs_1_ = bf16[2,512,128]{2,1,0:T(8,128)(2,1)S(1)} collective-permute-done((bf16[2,512,128]{2,1,0:T(8,128)(2,1)}, bf16[2,512,128]{2,1,0:T(8,128)(2,1)S(1)}, u32[]{:S(2)}, u32[]{:S(2)}) %collective-permute-start.8) | collective-permute-done | bytes 262176 | tf_op jit(solution)/shard_map/ppermute | solution.py:324
  85.7 17.1 %collective-permute-done.7.refs_3_ = bf16[4,512,128]{2,1,0:T(8,128)(2,1)S(1)} collective-permute-done((bf16[4,512,128]{2,1,0:T(8,128)(2,1)S(1)}, bf16[4,512,128]{2,1,0:T(8,128)(2,1)S(1)}, u32[]{:S(2)}, u32[]{:S(2)}) %collective-permute-start.7) | collective-permute-done | bytes 524320 | tf_op jit(solution)/shard_map/ppermute | solution.py:324
  102.8 0.2 all-to-all-done.1.parts
  103.0 0.7 first_sum.1
  103.7 1.9 %collective-permute-start.10 = (bf16[128,256]{1,0:T(8,128)(2,1)S(1)}, bf16[128,256]{1,0:T(8,128)(2,1)S(1)}, u32[]{:S(2)}, u32[]{:S(2)}) collective-permute-start(bf16[128,256]{1,0:T(8,128)(2,1)S(1)} %get-tuple-element.46), channel_id=1, source_target_pairs={{0,64},{64,0},{1,65},{65,1},{2,66},{66,2},{3,67},{67,3},{4,68},{68... | collective-permute-start | bytes 196616 | tf_op jit(solution)/shard_map/ppermute | solution.py:324
  105.6 4.0 %collective-permute-done.10.got = bf16[128,256]{1,0:T(8,128)(2,1)S(1)} collective-permute-done((bf16[128,256]{1,0:T(8,128)(2,1)S(1)}, bf16[128,256]{1,0:T(8,128)(2,1)S(1)}, u32[]{:S(2)}, u32[]{:S(2)}) %collective-permute-start.10) | collective-permute-done | bytes 65568 | tf_op jit(solution)/shard_map/ppermute | solution.py:324
  109.6 0.8 second_sum.1
  110.4 3.6 %all-to-all-start.2 = ((bf16[8,128,256]{2,1,0:T(8,128)(2,1)}), bf16[8,128,256]{2,1,0:T(8,128)(2,1)S(1)}, u32[]{:S(2)}, u32[]{:S(2)}) async-start(bf16[8,128,256]{2,1,0:T(8,128)(2,1)} %get-tuple-element.54), calls=%async_computation.2 | async-start | bytes 1048576 | tf_op jit(solution)/shard_map/all_to_all | solution.py:421
  114.1 3.6 %collective-permute-start.11 = (bf16[4,512,128]{2,1,0:T(8,128)(2,1)S(1)}, bf16[4,512,128]{2,1,0:T(8,128)(2,1)S(1)}, u32[]{:S(2)}, u32[]{:S(2)}) collective-permute-start(bf16[4,512,128]{2,1,0:T(8,128)(2,1)S(1)} %collective-permute-done.7.refs_3_), channel_id=1, source_target_pairs={{0,1},{1,0},{2,3},{3,2},{4,5},{5,4},{6,7},{7,6},{8,9},{9,8},{10,11... | collective-permute-start | bytes 1572872 | tf_op jit(solution)/shard_map/ppermute | solution.py:324
  117.6 1.5 collective-permute-done.11.refs_4_
  119.1 3.3 %all-to-all-done.2.refs_5_ = bf16[8,128,256]{2,1,0:T(8,128)(2,1)S(1)} async-done(((bf16[8,128,256]{2,1,0:T(8,128)(2,1)}), bf16[8,128,256]{2,1,0:T(8,128)(2,1)S(1)}, u32[]{:S(2)}, u32[]{:S(2)}) %all-to-all-start.2) | async-done | bytes 524320 | tf_op jit(solution)/shard_map/all_to_all | solution.py:421
  122.5 2.1 %weights.1 = bf16[16,64,256]{2,1,0:T(8,128)(2,1)} custom-call(s32[4]{0:T(128)S(1)} %pad_add_fusion.4.place, bf16[4,512,128]{2,1,0:T(8,128)(2,1)S(1)} %pad_maximum_fusion.1.refs_0_, bf16[2,512,128]{2,1,0:T(8,128)(2,1)S(1)} %copy-done.3, bf16[2,512,128]{2,1,0:T(8,128)(2,1)S(1)} %copy-done.1, bf16[4,512,128]{2,1,0:T(8,128)(2,1)S(1)} %collective-permute-done.7.refs_3_, ...), custom_call_target="tpu_custom_call" | custom-call | flops 1000000000 | bytes 4000000 | tf_op jit(solution)/shard_map/weights/pallas_call | solution.py:312
  124.5 6.8 %all-to-all-start.3 = ((bf16[16,64,256]{2,1,0:T(8,128)(2,1)}), bf16[16,64,256]{2,1,0:T(8,128)(2,1)S(1)}, u32[]{:S(2)}, u32[]{:S(2)}) async-start(bf16[16,64,256]{2,1,0:T(8,128)(2,1)} %weights.1), calls=%async_computation.3 | async-start | bytes 1048576 | tf_op jit(solution)/shard_map/all_to_all | solution.py:423
  131.4 2.2 %collective-permute-start.6 = (bf16[128,1024]{1,0:T(8,128)(2,1)S(1)}, bf16[128,1024]{1,0:T(8,128)(2,1)S(1)}, u32[]{:S(2)}, u32[]{:S(2)}) collective-permute-start(bf16[128,1024]{1,0:T(8,128)(2,1)S(1)} %get-tuple-element.39), channel_id=1, source_target_pairs={{0,32},{32,0},{1,33},{33,1},{2,34},{34,2},{3,35},{35,3},{4,36},{36... | collective-permute-start | bytes 786440 | tf_op jit(solution)/shard_map/ppermute | solution.py:324
  133.6 15.5 %all-to-all-done.3.parts = bf16[16,64,256]{2,1,0:T(8,128)(2,1)S(1)} async-done(((bf16[16,64,256]{2,1,0:T(8,128)(2,1)}), bf16[16,64,256]{2,1,0:T(8,128)(2,1)S(1)}, u32[]{:S(2)}, u32[]{:S(2)}) %all-to-all-start.3) | async-done | bytes 524320 | tf_op jit(solution)/shard_map/all_to_all | solution.py:423
  149.1 0.8 sum_rows.1
  149.8 3.4 %all-to-all-start.4 = ((f32[4,64,256]{2,1,0:T(8,128)}), f32[4,64,256]{2,1,0:T(8,128)S(1)}, u32[]{:S(2)}, u32[]{:S(2)}) async-start(f32[4,64,256]{2,1,0:T(8,128)} %sum_rows.1), calls=%async_computation.4 | async-start | bytes 524288 | tf_op jit(solution)/shard_map/all_to_all | solution.py:425
  153.3 0.8 fusion
  154.0 4.7 %all-to-all-done.4 = f32[4,64,256]{2,1,0:T(8,128)S(1)} async-done(((f32[4,64,256]{2,1,0:T(8,128)}), f32[4,64,256]{2,1,0:T(8,128)S(1)}, u32[]{:S(2)}, u32[]{:S(2)}) %all-to-all-start.4) | async-done | bytes 262176 | tf_op jit(solution)/shard_map/all_to_all | solution.py:425
  158.8 0.7 fusion.5
  (38 shorter events, 0.3 us)
Async XLA Ops:
  1.6 1.0 copy-start.5
  2.7 4.1 %copy-start.6 = (bf16[1,128,128]{2,1,0:T(8,128)(2,1)S(1)}, bf16[1,128,128]{2,1,0:T(8,128)(2,1)}, u32[]{:S(2)}) copy-start(bf16[1,128,128]{2,1,0:T(8,128)(2,1)} %param.9) | copy-start | bytes 98308
  2.7 4.1 %copy-start.7 = (bf16[1,128,128]{2,1,0:T(8,128)(2,1)S(1)}, bf16[1,128,128]{2,1,0:T(8,128)(2,1)}, u32[]{:S(2)}) copy-start(bf16[1,128,128]{2,1,0:T(8,128)(2,1)} %param.8) | copy-start | bytes 98308
  2.8 23.8 %collective-permute-start = (bf16[2,1024,128]{2,1,0:T(8,128)(2,1)S(1)}, bf16[2,1024,128]{2,1,0:T(8,128)(2,1)S(1)}, u32[]{:S(2)}, u32[]{:S(2)}) collective-permute-start(bf16[2,1024,128]{2,1,0:T(8,128)(2,1)S(1)} %pad_maximum_fusion.own), channel_id=1, source_target_pairs={{0,32},{32,0},{1,33},{33,1},{2,34},{34,2},{3,35},{35,3},{4,36},{36... | collective-permute-start | bytes 1572872 | tf_op jit(solution)/shard_map/ppermute | solution.py:324
  7.9 18.7 %copy-start.4 = (bf16[1,128,2048]{2,1,0:T(8,128)(2,1)S(1)}, bf16[1,128,2048]{2,1,0:T(8,128)(2,1)}, u32[]{:S(2)}) copy-start(bf16[1,128,2048]{2,1,0:T(8,128)(2,1)} %param.11) | copy-start | bytes 1572868
  7.9 39.8 %all-to-all-start = ((bf16[16,128,256]{2,1,0:T(8,128)(2,1)}), bf16[16,128,256]{2,1,0:T(8,128)(2,1)S(1)}, u32[]{:S(2)}, u32[]{:S(2)}) async-start(bf16[16,128,256]{2,1,0:T(8,128)(2,1)} %broadcast_in_dim.43), calls=%async_computation | async-start | bytes 2097152 | tf_op jit(solution)/shard_map/all_to_all | solution.py:369
  20.3 0.7 copy-start.8
  23.3 0.7 copy-start.9
  27.7 22.1 %collective-permute-start.4 = (bf16[512,128]{1,0:T(8,128)(2,1)}, bf16[512,128]{1,0:T(8,128)(2,1)S(1)}, u32[]{:S(2)}, u32[]{:S(2)}) collective-permute-start(bf16[512,128]{1,0:T(8,128)(2,1)} %get-tuple-element.63), channel_id=1, source_target_pairs={{0,384},{1,416},{32,385},{33,417},{128,0},{129,32},{160,1},{161,33... | collective-permute-start | bytes 393224 | tf_op jit(solution)/shard_map/ppermute | solution.py:390
  33.0 16.7 %collective-permute-start.3 = (bf16[512,128]{1,0:T(8,128)(2,1)S(1)}, bf16[512,128]{1,0:T(8,128)(2,1)S(1)}, u32[]{:S(2)}, u32[]{:S(2)}) collective-permute-start(bf16[512,128]{1,0:T(8,128)(2,1)S(1)} %get-tuple-element.64), channel_id=1, source_target_pairs={{0,256},{1,288},{32,257},{33,289},{128,384},{129,416},{160,385},{1... | collective-permute-start | bytes 393224 | tf_op jit(solution)/shard_map/ppermute | solution.py:390
  35.7 15.5 %collective-permute-start.2 = (bf16[512,128]{1,0:T(8,128)(2,1)S(1)}, bf16[512,128]{1,0:T(8,128)(2,1)S(1)}, u32[]{:S(2)}, u32[]{:S(2)}) collective-permute-start(bf16[512,128]{1,0:T(8,128)(2,1)S(1)} %get-tuple-element.65), channel_id=1, source_target_pairs={{0,128},{1,160},{32,129},{33,161},{128,256},{129,288},{160,257},{1... | collective-permute-start | bytes 393224 | tf_op jit(solution)/shard_map/ppermute | solution.py:390
  39.2 12.0 %collective-permute-start.1 = (bf16[512,128]{1,0:T(8,128)(2,1)S(1)}, bf16[512,128]{1,0:T(8,128)(2,1)}, u32[]{:S(2)}, u32[]{:S(2)}) collective-permute-start(bf16[512,128]{1,0:T(8,128)(2,1)S(1)} %get-tuple-element.66), channel_id=1, source_target_pairs={{0,0},{1,32},{32,1},{33,33},{128,128},{129,160},{160,129},{161,161... | collective-permute-start | bytes 393224 | tf_op jit(solution)/shard_map/ppermute | solution.py:390
  51.2 4.6 %collective-permute-start.5 = (f32[16,512]{1,0:T(8,128)S(1)}, f32[16,512]{1,0:T(8,128)S(1)}, u32[]{:S(2)}, u32[]{:S(2)}) collective-permute-start(f32[16,512]{1,0:T(8,128)S(1)} %stats.1), channel_id=1, source_target_pairs={{0,32},{32,0},{1,33},{33,1},{2,34},{34,2},{3,35},{35,3},{4,36},{36... | collective-permute-start | bytes 98312 | tf_op jit(solution)/shard_map/ppermute | solution.py:324
  60.1 42.9 %all-to-all-start.1 = ((bf16[16,128,256]{2,1,0:T(8,128)(2,1)}), bf16[16,128,256]{2,1,0:T(8,128)(2,1)S(1)}, u32[]{:S(2)}, u32[]{:S(2)}) async-start(bf16[16,128,256]{2,1,0:T(8,128)(2,1)} %get-tuple-element.42), calls=%async_computation.1 | async-start | bytes 2097152 | tf_op jit(solution)/shard_map/all_to_all | solution.py:410
  73.8 29.0 %collective-permute-start.7 = (bf16[4,512,128]{2,1,0:T(8,128)(2,1)S(1)}, bf16[4,512,128]{2,1,0:T(8,128)(2,1)S(1)}, u32[]{:S(2)}, u32[]{:S(2)}) collective-permute-start(bf16[4,512,128]{2,1,0:T(8,128)(2,1)S(1)} %pad_maximum_fusion.1.refs_0_), channel_id=1, source_target_pairs={{0,2},{2,0},{1,3},{3,1},{4,6},{6,4},{5,7},{7,5},{8,10},{10,8},{9,1... | collective-permute-start | bytes 1572872 | tf_op jit(solution)/shard_map/ppermute | solution.py:324
  77.0 7.0 %collective-permute-start.9 = (bf16[2,512,128]{2,1,0:T(8,128)(2,1)}, bf16[2,512,128]{2,1,0:T(8,128)(2,1)S(1)}, u32[]{:S(2)}, u32[]{:S(2)}) collective-permute-start(bf16[2,512,128]{2,1,0:T(8,128)(2,1)} %get-tuple-element.61), channel_id=1, source_target_pairs={{0,1},{1,0},{2,3},{3,2},{4,5},{5,4},{6,7},{7,6},{8,9},{9,8},{10,11... | collective-permute-start | bytes 786440 | tf_op jit(solution)/shard_map/ppermute | solution.py:324
  82.0 3.6 %collective-permute-start.8 = (bf16[2,512,128]{2,1,0:T(8,128)(2,1)}, bf16[2,512,128]{2,1,0:T(8,128)(2,1)S(1)}, u32[]{:S(2)}, u32[]{:S(2)}) collective-permute-start(bf16[2,512,128]{2,1,0:T(8,128)(2,1)} %get-tuple-element.62), channel_id=1, source_target_pairs={{0,1},{1,0},{2,3},{3,2},{4,5},{5,4},{6,7},{7,6},{8,9},{9,8},{10,11... | collective-permute-start | bytes 786440 | tf_op jit(solution)/shard_map/ppermute | solution.py:324
  84.0 19.6 %copy-start = (bf16[2,512,128]{2,1,0:T(8,128)(2,1)}, bf16[2,512,128]{2,1,0:T(8,128)(2,1)S(1)}, u32[]{:S(2)}) copy-start(bf16[2,512,128]{2,1,0:T(8,128)(2,1)S(1)} %collective-permute-done.9.refs_2_) | copy-start | bytes 786436
  85.7 18.0 %copy-start.2 = (bf16[2,512,128]{2,1,0:T(8,128)(2,1)}, bf16[2,512,128]{2,1,0:T(8,128)(2,1)S(1)}, u32[]{:S(2)}) copy-start(bf16[2,512,128]{2,1,0:T(8,128)(2,1)S(1)} %collective-permute-done.8.refs_1_) | copy-start | bytes 786436
  103.7 5.9 %collective-permute-start.10 = (bf16[128,256]{1,0:T(8,128)(2,1)S(1)}, bf16[128,256]{1,0:T(8,128)(2,1)S(1)}, u32[]{:S(2)}, u32[]{:S(2)}) collective-permute-start(bf16[128,256]{1,0:T(8,128)(2,1)S(1)} %get-tuple-element.46), channel_id=1, source_target_pairs={{0,64},{64,0},{1,65},{65,1},{2,66},{66,2},{3,67},{67,3},{4,68},{68... | collective-permute-start | bytes 196616 | tf_op jit(solution)/shard_map/ppermute | solution.py:324
  110.4 12.0 %copy-start.1 = (bf16[2,512,128]{2,1,0:T(8,128)(2,1)S(1)}, bf16[2,512,128]{2,1,0:T(8,128)(2,1)}, u32[]{:S(2)}) copy-start(bf16[2,512,128]{2,1,0:T(8,128)(2,1)} %copy-done) | copy-start | bytes 786436
  110.4 12.0 %copy-start.3 = (bf16[2,512,128]{2,1,0:T(8,128)(2,1)S(1)}, bf16[2,512,128]{2,1,0:T(8,128)(2,1)}, u32[]{:S(2)}) copy-start(bf16[2,512,128]{2,1,0:T(8,128)(2,1)} %copy-done.2) | copy-start | bytes 786436
  110.4 12.0 %all-to-all-start.2 = ((bf16[8,128,256]{2,1,0:T(8,128)(2,1)}), bf16[8,128,256]{2,1,0:T(8,128)(2,1)S(1)}, u32[]{:S(2)}, u32[]{:S(2)}) async-start(bf16[8,128,256]{2,1,0:T(8,128)(2,1)} %get-tuple-element.54), calls=%async_computation.2 | async-start | bytes 1048576 | tf_op jit(solution)/shard_map/all_to_all | solution.py:421
  114.1 5.1 %collective-permute-start.11 = (bf16[4,512,128]{2,1,0:T(8,128)(2,1)S(1)}, bf16[4,512,128]{2,1,0:T(8,128)(2,1)S(1)}, u32[]{:S(2)}, u32[]{:S(2)}) collective-permute-start(bf16[4,512,128]{2,1,0:T(8,128)(2,1)S(1)} %collective-permute-done.7.refs_3_), channel_id=1, source_target_pairs={{0,1},{1,0},{2,3},{3,2},{4,5},{5,4},{6,7},{7,6},{8,9},{9,8},{10,11... | collective-permute-start | bytes 1572872 | tf_op jit(solution)/shard_map/ppermute | solution.py:324
  124.5 24.5 %all-to-all-start.3 = ((bf16[16,64,256]{2,1,0:T(8,128)(2,1)}), bf16[16,64,256]{2,1,0:T(8,128)(2,1)S(1)}, u32[]{:S(2)}, u32[]{:S(2)}) async-start(bf16[16,64,256]{2,1,0:T(8,128)(2,1)} %weights.1), calls=%async_computation.3 | async-start | bytes 1048576 | tf_op jit(solution)/shard_map/all_to_all | solution.py:423
  131.4 21.9 %collective-permute-start.6 = (bf16[128,1024]{1,0:T(8,128)(2,1)S(1)}, bf16[128,1024]{1,0:T(8,128)(2,1)S(1)}, u32[]{:S(2)}, u32[]{:S(2)}) collective-permute-start(bf16[128,1024]{1,0:T(8,128)(2,1)S(1)} %get-tuple-element.39), channel_id=1, source_target_pairs={{0,32},{32,0},{1,33},{33,1},{2,34},{34,2},{3,35},{35,3},{4,36},{36... | collective-permute-start | bytes 786440 | tf_op jit(solution)/shard_map/ppermute | solution.py:324
  149.8 8.9 %all-to-all-start.4 = ((f32[4,64,256]{2,1,0:T(8,128)}), f32[4,64,256]{2,1,0:T(8,128)S(1)}, u32[]{:S(2)}, u32[]{:S(2)}) async-start(f32[4,64,256]{2,1,0:T(8,128)} %sum_rows.1), calls=%async_computation.4 | async-start | bytes 524288 | tf_op jit(solution)/shard_map/all_to_all | solution.py:425

commit v6 on v5

--- a/solution.py
+++ b/solution.py
@@ -410,7 +410,7 @@
     parts = lax.all_to_all(dkv, "z", 0, 0, tiled=True)
     halves = late[:copies_of // 2], late[copies_of // 2:]
     near_across = [swapped(part, "core") for part in halves]
-    parts, beside, near_across = lax.optimization_barrier((parts, beside, near_across))
+    parts, near_across = lax.optimization_barrier((parts, near_across))
     kept, sent_grads = first_sum(place, parts)
     got = swapped(sent_grads, "ya")
     dq_far = swapped(dq_other, "yb")

time: 160 us -> 157 us (0.981); the launches traced: 159 us -> 155 us
  waiting for transfers between devices: 57.3 us -> 53.8 us
  starting transfers between devices: 76.7 us -> 74.1 us
    ppermute x8, waiting for transfers between devices: 26 us -> 8.87 us  [swapped(): return lax.ppermute(array, axis, [(0, 1), (1, 0)])]
    all_to_all x1, waiting for transfers between devices: 0.18 us -> 17.2 us  [shards(): parts = lax.all_to_all(dkv, 'z', 0, 0, tiled=True)]
    all_to_all x1, starting transfers between devices: 6.84 us -> 3.57 us  [shards(): pieces = lax.all_to_all(blocks, group, 0, 0, tiled=True)]
  transfers between devices with their start and end apart: 17 -> 17, of which waited for: 12 -> 11; matrix products, arithmetic and copies ran while one was open for 5% -> 5% of each run, Pallas kernels for 2% -> 3%
where the time goes in v6:
time: 157 us; the launch traced here: 155 us
  starting transfers between devices  74.1 us (47%)
  waiting for transfers between devices  53.8 us (34%)
  Pallas kernels  12.1 us (8%)
  local copies, waits for them, and re-layouts  7.51 us (5%)
  other arithmetic  5.03 us (3%)
  between operations  2.34 us (1%)
    ppermute x8, starting transfers between devices, swapped(): return lax.ppermute(array, axis, [(0, 1), (1, 0)])  23.9 us
    all_to_all x1, waiting for transfers between devices, shards(): parts = lax.all_to_all(dkv, 'z', 0, 0, tiled=True)  17.2 us
    all_to_all x1, waiting for transfers between devices, shards(): pieces = lax.all_to_all(blocks, group, 0, 0, tiled=True)  14.2 us
    ppermute x4, starting transfers between devices, shards(): lax.ppermute(slab, ('dp', 'yb', 'core'), [(d * 4 + b * 2 + c, (d + by) %...  13.9 us
    all_to_all x1, starting transfers between devices, shards(): parts = lax.all_to_all(dkv, 'z', 0, 0, tiled=True)  13.4 us
    all_to_all x1, starting transfers between devices, shards(): lax.all_to_all(jnp.broadcast_to(pair[None], (group_size,) + pair.shape),...  12.3 us
    ppermute x8, waiting for transfers between devices, swapped(): return lax.ppermute(array, axis, [(0, 1), (1, 0)])  8.87 us
    all_to_all x1, waiting for transfers between devices, shards(): lax.all_to_all(jnp.broadcast_to(pair[None], (group_size,) + pair.shape),...  6.21 us
  transfers between devices with their start and end apart: 17, of which 11 were waited for; matrix products, arithmetic and copies ran while one was open for 5% of the time, Pallas kernels for 3%

profile of v6, /device:TPU:1, one launch (start us, length us, event | category | flops | bytes accessed | tf_op | source)
XLA Modules:
  0.0 154.8 jit_solution(6423348516592618141)
XLA Ops:
  0.6 1.0 copy.41
  1.6 0.0 copy-start.5
  1.7 0.9 copy-done.5
  2.7 0.1 pad_maximum_fusion.own
  2.8 4.0 %collective-permute-start = (bf16[2,1024,128]{2,1,0:T(8,128)(2,1)S(1)}, bf16[2,1024,128]{2,1,0:T(8,128)(2,1)S(1)}, u32[]{:S(2)}, u32[]{:S(2)}) collective-permute-start(bf16[2,1024,128]{2,1,0:T(8,128)(2,1)S(1)} %pad_maximum_fusion.own), channel_id=1, source_target_pairs={{0,32},{32,0},{1,33},{33,1},{2,34},{34,2},{3,35},{35,3},{4,36},{36... | collective-permute-start | bytes 1572872 | tf_op jit(solution)/shard_map/ppermute | solution.py:324
  6.9 1.1 broadcast_in_dim.43
  7.9 12.3 %all-to-all-start = ((bf16[16,128,256]{2,1,0:T(8,128)(2,1)}), bf16[16,128,256]{2,1,0:T(8,128)(2,1)S(1)}, u32[]{:S(2)}, u32[]{:S(2)}) async-start(bf16[16,128,256]{2,1,0:T(8,128)(2,1)} %broadcast_in_dim.43), calls=%async_computation | async-start | bytes 2097152 | tf_op jit(solution)/shard_map/all_to_all | solution.py:369
  20.3 0.6 copy-done.8
  20.9 0.1 reshape.195
  21.0 0.6 fusion.2
  21.7 0.1 select_n.68
  21.8 0.1 copy.34
  21.9 0.1 lt.41
  21.9 0.1 broadcast_in_dim_reshape.2
  23.4 0.6 copy-done.9
  24.0 0.2 reduce-window.8
  24.2 1.4 broadcast_multiply_fusion
  25.5 0.1 iota_add_fusion
  25.6 0.1 select_reduce_fusion
  25.7 0.1 iota_add_fusion.1
  25.8 0.1 tile.10.qmeta
  25.9 0.2 select_reduce_fusion.1
  26.1 0.2 convert_reduce_fusion.2
  26.3 0.1 add_bitcast_fusion
  26.4 0.2 convert_reduce_fusion
  26.6 0.3 copy.39
  27.0 0.7 dynamic-slice_bitcast_fusion
  27.7 5.4 %collective-permute-start.4 = (bf16[512,128]{1,0:T(8,128)(2,1)}, bf16[512,128]{1,0:T(8,128)(2,1)S(1)}, u32[]{:S(2)}, u32[]{:S(2)}) collective-permute-start(bf16[512,128]{1,0:T(8,128)(2,1)} %get-tuple-element.61), channel_id=1, source_target_pairs={{0,384},{1,416},{32,385},{33,417},{128,0},{129,32},{160,1},{161,33... | collective-permute-start | bytes 393224 | tf_op jit(solution)/shard_map/ppermute | solution.py:390
  33.0 2.6 %collective-permute-start.3 = (bf16[512,128]{1,0:T(8,128)(2,1)S(1)}, bf16[512,128]{1,0:T(8,128)(2,1)S(1)}, u32[]{:S(2)}, u32[]{:S(2)}) collective-permute-start(bf16[512,128]{1,0:T(8,128)(2,1)S(1)} %get-tuple-element.62), channel_id=1, source_target_pairs={{0,256},{1,288},{32,257},{33,289},{128,384},{129,416},{160,385},{1... | collective-permute-start | bytes 393224 | tf_op jit(solution)/shard_map/ppermute | solution.py:390
  35.7 3.5 %collective-permute-start.2 = (bf16[512,128]{1,0:T(8,128)(2,1)S(1)}, bf16[512,128]{1,0:T(8,128)(2,1)S(1)}, u32[]{:S(2)}, u32[]{:S(2)}) collective-permute-start(bf16[512,128]{1,0:T(8,128)(2,1)S(1)} %get-tuple-element.63), channel_id=1, source_target_pairs={{0,128},{1,160},{32,129},{33,161},{128,256},{129,288},{160,257},{1... | collective-permute-start | bytes 393224 | tf_op jit(solution)/shard_map/ppermute | solution.py:390
  39.2 2.4 %collective-permute-start.1 = (bf16[512,128]{1,0:T(8,128)(2,1)S(1)}, bf16[512,128]{1,0:T(8,128)(2,1)}, u32[]{:S(2)}, u32[]{:S(2)}) collective-permute-start(bf16[512,128]{1,0:T(8,128)(2,1)S(1)} %get-tuple-element.64), channel_id=1, source_target_pairs={{0,0},{1,32},{32,1},{33,33},{128,128},{129,160},{160,129},{161,161... | collective-permute-start | bytes 393224 | tf_op jit(solution)/shard_map/ppermute | solution.py:390
  41.6 6.2 %all-to-all-done.kv = bf16[16,128,256]{2,1,0:T(8,128)(2,1)S(1)} async-done(((bf16[16,128,256]{2,1,0:T(8,128)(2,1)}), bf16[16,128,256]{2,1,0:T(8,128)(2,1)S(1)}, u32[]{:S(2)}, u32[]{:S(2)}) %all-to-all-start) | async-done | bytes 1048608 | tf_op jit(solution)/shard_map/all_to_all | solution.py:369
  47.8 2.6 %stats.1 = f32[16,512]{1,0:T(8,128)S(1)} custom-call(s32[3,32]{1,0:T(4,128)S(1)} %pad_add_fusion.1.meta, s32[16,512]{1,0:T(8,128)S(1)} %tile.10.qmeta, bf16[2,1024,128]{2,1,0:T(8,128)(2,1)S(1)} %pad_maximum_fusion.own, bf16[2,1024,128]{2,1,0:T(8,128)(2,1)S(1)} %collective-permute-done.other, bf16[16,128,256]{2,1,0:T(8,128)(2,1)S(1)} %all-to-all-done.kv), custom_call_target="tpu_custom_call" | custom-call | flops 2000000000 | bytes 4000000 | tf_op jit(solution)/shard_map/stats/pallas_call | solution.py:192
  50.4 0.8 collective-permute-done.2
  51.2 0.1 collective-permute-done.1
  51.2 1.9 %collective-permute-start.5 = (f32[16,512]{1,0:T(8,128)S(1)}, f32[16,512]{1,0:T(8,128)S(1)}, u32[]{:S(2)}, u32[]{:S(2)}) collective-permute-start(f32[16,512]{1,0:T(8,128)S(1)} %stats.1), channel_id=1, source_target_pairs={{0,32},{32,0},{1,33},{33,1},{2,34},{34,2},{3,35},{35,3},{4,36},{36... | collective-permute-start | bytes 98312 | tf_op jit(solution)/shard_map/ppermute | solution.py:324
  53.1 1.0 pad_maximum_fusion.1.refs_0_
  54.1 1.8 %collective-permute-done.5.far = f32[16,512]{1,0:T(8,128)S(1)} collective-permute-done((f32[16,512]{1,0:T(8,128)S(1)}, f32[16,512]{1,0:T(8,128)S(1)}, u32[]{:S(2)}, u32[]{:S(2)}) %collective-permute-start.5) | collective-permute-done | bytes 32800 | tf_op jit(solution)/shard_map/ppermute | solution.py:324
  55.9 5.1 %grads.1 = (f32[128,1024]{1,0:T(8,128)S(1)}, bf16[128,1024]{1,0:T(8,128)(2,1)S(1)}, bf16[16,128,256]{2,1,0:T(8,128)(2,1)}) custom-call(s32[3,32]{1,0:T(4,128)S(1)} %pad_add_fusion.1.meta, s32[16,512]{1,0:T(8,128)S(1)} %tile.10.qmeta, bf16[2,1024,128]{2,1,0:T(8,128)(2,1)S(1)} %pad_maximum_fusion.own, bf16[2,1024,128]{2,1,0:T(8,128)(2,1)S(1)} %collective-permute-done.other, ...), custom_call_target="tpu_custom_call" | custom-call | flops 5000000000 | bytes 6000000 | tf_op jit(solution)/shard_map/grads/pallas_call | solution.py:208
  61.0 13.4 %all-to-all-start.1 = ((bf16[16,128,256]{2,1,0:T(8,128)(2,1)}), bf16[16,128,256]{2,1,0:T(8,128)(2,1)S(1)}, u32[]{:S(2)}, u32[]{:S(2)}) async-start(bf16[16,128,256]{2,1,0:T(8,128)(2,1)} %get-tuple-element.41), calls=%async_computation.1 | async-start | bytes 2097152 | tf_op jit(solution)/shard_map/all_to_all | solution.py:410
  74.4 1.9 %collective-permute-start.10 = (bf16[4,512,128]{2,1,0:T(8,128)(2,1)S(1)}, bf16[4,512,128]{2,1,0:T(8,128)(2,1)S(1)}, u32[]{:S(2)}, u32[]{:S(2)}) collective-permute-start(bf16[4,512,128]{2,1,0:T(8,128)(2,1)S(1)} %pad_maximum_fusion.1.refs_0_), channel_id=1, source_target_pairs={{0,2},{2,0},{1,3},{3,1},{4,6},{6,4},{5,7},{7,5},{8,10},{10,8},{9,1... | collective-permute-start | bytes 1572872 | tf_op jit(solution)/shard_map/ppermute | solution.py:324
  76.3 0.8 fusion.4
  77.1 5.6 %collective-permute-start.8 = (bf16[2,512,128]{2,1,0:T(8,128)(2,1)}, bf16[2,512,128]{2,1,0:T(8,128)(2,1)S(1)}, u32[]{:S(2)}, u32[]{:S(2)}) collective-permute-start(bf16[2,512,128]{2,1,0:T(8,128)(2,1)} %get-tuple-element.59), channel_id=1, source_target_pairs={{0,1},{1,0},{2,3},{3,2},{4,5},{5,4},{6,7},{7,6},{8,9},{9,8},{10,11... | collective-permute-start | bytes 786440 | tf_op jit(solution)/shard_map/ppermute | solution.py:324
  82.7 1.9 %collective-permute-start.7 = (bf16[2,512,128]{2,1,0:T(8,128)(2,1)}, bf16[2,512,128]{2,1,0:T(8,128)(2,1)S(1)}, u32[]{:S(2)}, u32[]{:S(2)}) collective-permute-start(bf16[2,512,128]{2,1,0:T(8,128)(2,1)} %get-tuple-element.60), channel_id=1, source_target_pairs={{0,1},{1,0},{2,3},{3,2},{4,5},{5,4},{6,7},{7,6},{8,9},{9,8},{10,11... | collective-permute-start | bytes 786440 | tf_op jit(solution)/shard_map/ppermute | solution.py:324
  84.7 0.1 pad_add_fusion.4.place
  84.8 1.6 %collective-permute-done.7.refs_1_ = bf16[2,512,128]{2,1,0:T(8,128)(2,1)S(1)} collective-permute-done((bf16[2,512,128]{2,1,0:T(8,128)(2,1)}, bf16[2,512,128]{2,1,0:T(8,128)(2,1)S(1)}, u32[]{:S(2)}, u32[]{:S(2)}) %collective-permute-start.7) | collective-permute-done | bytes 262176 | tf_op jit(solution)/shard_map/ppermute | solution.py:324
  86.4 17.2 %all-to-all-done.1.parts = bf16[16,128,256]{2,1,0:T(8,128)(2,1)S(1)} async-done(((bf16[16,128,256]{2,1,0:T(8,128)(2,1)}), bf16[16,128,256]{2,1,0:T(8,128)(2,1)S(1)}, u32[]{:S(2)}, u32[]{:S(2)}) %all-to-all-start.1) | async-done | bytes 1048608 | tf_op jit(solution)/shard_map/all_to_all | solution.py:410
  103.5 0.7 first_sum.1
  104.3 1.9 %collective-permute-start.9 = (bf16[128,256]{1,0:T(8,128)(2,1)S(1)}, bf16[128,256]{1,0:T(8,128)(2,1)S(1)}, u32[]{:S(2)}, u32[]{:S(2)}) collective-permute-start(bf16[128,256]{1,0:T(8,128)(2,1)S(1)} %get-tuple-element.45), channel_id=1, source_target_pairs={{0,64},{64,0},{1,65},{65,1},{2,66},{66,2},{3,67},{67,3},{4,68},{68... | collective-permute-start | bytes 196616 | tf_op jit(solution)/shard_map/ppermute | solution.py:324
  106.2 4.0 %collective-permute-done.9.got = bf16[128,256]{1,0:T(8,128)(2,1)S(1)} collective-permute-done((bf16[128,256]{1,0:T(8,128)(2,1)S(1)}, bf16[128,256]{1,0:T(8,128)(2,1)S(1)}, u32[]{:S(2)}, u32[]{:S(2)}) %collective-permute-start.9) | collective-permute-done | bytes 65568 | tf_op jit(solution)/shard_map/ppermute | solution.py:324
  110.2 0.8 second_sum.1
  111.0 3.6 %all-to-all-start.2 = ((bf16[8,128,256]{2,1,0:T(8,128)(2,1)}), bf16[8,128,256]{2,1,0:T(8,128)(2,1)S(1)}, u32[]{:S(2)}, u32[]{:S(2)}) async-start(bf16[8,128,256]{2,1,0:T(8,128)(2,1)} %get-tuple-element.52), calls=%async_computation.2 | async-start | bytes 1048576 | tf_op jit(solution)/shard_map/all_to_all | solution.py:421
  114.6 4.3 %collective-permute-start.11 = (bf16[4,512,128]{2,1,0:T(8,128)(2,1)S(1)}, bf16[4,512,128]{2,1,0:T(8,128)(2,1)S(1)}, u32[]{:S(2)}, u32[]{:S(2)}) collective-permute-start(bf16[4,512,128]{2,1,0:T(8,128)(2,1)S(1)} %collective-permute-done.10.refs_3_), channel_id=1, source_target_pairs={{0,1},{1,0},{2,3},{3,2},{4,5},{5,4},{6,7},{7,6},{8,9},{9,8},{10,11... | collective-permute-start | bytes 1572872 | tf_op jit(solution)/shard_map/ppermute | solution.py:324
  118.9 1.5 collective-permute-done.11.refs_4_
  120.4 1.8 %all-to-all-done.2.refs_5_ = bf16[8,128,256]{2,1,0:T(8,128)(2,1)S(1)} async-done(((bf16[8,128,256]{2,1,0:T(8,128)(2,1)}), bf16[8,128,256]{2,1,0:T(8,128)(2,1)S(1)}, u32[]{:S(2)}, u32[]{:S(2)}) %all-to-all-start.2) | async-done | bytes 524320 | tf_op jit(solution)/shard_map/all_to_all | solution.py:421
  122.2 2.1 %weights.1 = bf16[16,64,256]{2,1,0:T(8,128)(2,1)} custom-call(s32[4]{0:T(128)S(1)} %pad_add_fusion.4.place, bf16[4,512,128]{2,1,0:T(8,128)(2,1)S(1)} %pad_maximum_fusion.1.refs_0_, bf16[2,512,128]{2,1,0:T(8,128)(2,1)S(1)} %copy-done.3, bf16[2,512,128]{2,1,0:T(8,128)(2,1)S(1)} %copy-done.1, bf16[4,512,128]{2,1,0:T(8,128)(2,1)S(1)} %collective-permute-done.10.refs_3_, ...), custom_call_target="tpu_custom_call" | custom-call | flops 1000000000 | bytes 4000000 | tf_op jit(solution)/shard_map/weights/pallas_call | solution.py:312
  124.3 3.6 %all-to-all-start.3 = ((bf16[16,64,256]{2,1,0:T(8,128)(2,1)}), bf16[16,64,256]{2,1,0:T(8,128)(2,1)S(1)}, u32[]{:S(2)}, u32[]{:S(2)}) async-start(bf16[16,64,256]{2,1,0:T(8,128)(2,1)} %weights.1), calls=%async_computation.3 | async-start | bytes 1048576 | tf_op jit(solution)/shard_map/all_to_all | solution.py:423
  127.9 2.4 %collective-permute-start.6 = (bf16[128,1024]{1,0:T(8,128)(2,1)S(1)}, bf16[128,1024]{1,0:T(8,128)(2,1)S(1)}, u32[]{:S(2)}, u32[]{:S(2)}) collective-permute-start(bf16[128,1024]{1,0:T(8,128)(2,1)S(1)} %get-tuple-element.38), channel_id=1, source_target_pairs={{0,32},{32,0},{1,33},{33,1},{2,34},{34,2},{3,35},{35,3},{4,36},{36... | collective-permute-start | bytes 786440 | tf_op jit(solution)/shard_map/ppermute | solution.py:324
  130.3 14.2 %all-to-all-done.3.parts = bf16[16,64,256]{2,1,0:T(8,128)(2,1)S(1)} async-done(((bf16[16,64,256]{2,1,0:T(8,128)(2,1)}), bf16[16,64,256]{2,1,0:T(8,128)(2,1)S(1)}, u32[]{:S(2)}, u32[]{:S(2)}) %all-to-all-start.3) | async-done | bytes 524320 | tf_op jit(solution)/shard_map/all_to_all | solution.py:423
  144.4 0.8 sum_rows.1
  145.2 3.4 %all-to-all-start.4 = ((f32[4,64,256]{2,1,0:T(8,128)}), f32[4,64,256]{2,1,0:T(8,128)S(1)}, u32[]{:S(2)}, u32[]{:S(2)}) async-start(f32[4,64,256]{2,1,0:T(8,128)} %sum_rows.1), calls=%async_computation.4 | async-start | bytes 524288 | tf_op jit(solution)/shard_map/all_to_all | solution.py:425
  148.6 0.8 fusion
  149.4 4.7 %all-to-all-done.4 = f32[4,64,256]{2,1,0:T(8,128)S(1)} async-done(((f32[4,64,256]{2,1,0:T(8,128)}), f32[4,64,256]{2,1,0:T(8,128)S(1)}, u32[]{:S(2)}, u32[]{:S(2)}) %all-to-all-start.4) | async-done | bytes 262176 | tf_op jit(solution)/shard_map/all_to_all | solution.py:425
  154.1 0.7 fusion.5
  (38 shorter events, 0.3 us)
Async XLA Ops:
  1.6 1.0 copy-start.5
  2.7 4.1 %copy-start.6 = (bf16[1,128,128]{2,1,0:T(8,128)(2,1)S(1)}, bf16[1,128,128]{2,1,0:T(8,128)(2,1)}, u32[]{:S(2)}) copy-start(bf16[1,128,128]{2,1,0:T(8,128)(2,1)} %param.9) | copy-start | bytes 98308
  2.7 4.1 %copy-start.7 = (bf16[1,128,128]{2,1,0:T(8,128)(2,1)S(1)}, bf16[1,128,128]{2,1,0:T(8,128)(2,1)}, u32[]{:S(2)}) copy-start(bf16[1,128,128]{2,1,0:T(8,128)(2,1)} %param.8) | copy-start | bytes 98308
  2.8 23.8 %collective-permute-start = (bf16[2,1024,128]{2,1,0:T(8,128)(2,1)S(1)}, bf16[2,1024,128]{2,1,0:T(8,128)(2,1)S(1)}, u32[]{:S(2)}, u32[]{:S(2)}) collective-permute-start(bf16[2,1024,128]{2,1,0:T(8,128)(2,1)S(1)} %pad_maximum_fusion.own), channel_id=1, source_target_pairs={{0,32},{32,0},{1,33},{33,1},{2,34},{34,2},{3,35},{35,3},{4,36},{36... | collective-permute-start | bytes 1572872 | tf_op jit(solution)/shard_map/ppermute | solution.py:324
  7.9 18.7 %copy-start.4 = (bf16[1,128,2048]{2,1,0:T(8,128)(2,1)S(1)}, bf16[1,128,2048]{2,1,0:T(8,128)(2,1)}, u32[]{:S(2)}) copy-start(bf16[1,128,2048]{2,1,0:T(8,128)(2,1)} %param.11) | copy-start | bytes 1572868
  7.9 39.8 %all-to-all-start = ((bf16[16,128,256]{2,1,0:T(8,128)(2,1)}), bf16[16,128,256]{2,1,0:T(8,128)(2,1)S(1)}, u32[]{:S(2)}, u32[]{:S(2)}) async-start(bf16[16,128,256]{2,1,0:T(8,128)(2,1)} %broadcast_in_dim.43), calls=%async_computation | async-start | bytes 2097152 | tf_op jit(solution)/shard_map/all_to_all | solution.py:369
  20.3 0.7 copy-start.8
  23.3 0.7 copy-start.9
  27.7 22.7 %collective-permute-start.4 = (bf16[512,128]{1,0:T(8,128)(2,1)}, bf16[512,128]{1,0:T(8,128)(2,1)S(1)}, u32[]{:S(2)}, u32[]{:S(2)}) collective-permute-start(bf16[512,128]{1,0:T(8,128)(2,1)} %get-tuple-element.61), channel_id=1, source_target_pairs={{0,384},{1,416},{32,385},{33,417},{128,0},{129,32},{160,1},{161,33... | collective-permute-start | bytes 393224 | tf_op jit(solution)/shard_map/ppermute | solution.py:390
  33.0 17.3 %collective-permute-start.3 = (bf16[512,128]{1,0:T(8,128)(2,1)S(1)}, bf16[512,128]{1,0:T(8,128)(2,1)S(1)}, u32[]{:S(2)}, u32[]{:S(2)}) collective-permute-start(bf16[512,128]{1,0:T(8,128)(2,1)S(1)} %get-tuple-element.62), channel_id=1, source_target_pairs={{0,256},{1,288},{32,257},{33,289},{128,384},{129,416},{160,385},{1... | collective-permute-start | bytes 393224 | tf_op jit(solution)/shard_map/ppermute | solution.py:390
  35.7 15.5 %collective-permute-start.2 = (bf16[512,128]{1,0:T(8,128)(2,1)S(1)}, bf16[512,128]{1,0:T(8,128)(2,1)S(1)}, u32[]{:S(2)}, u32[]{:S(2)}) collective-permute-start(bf16[512,128]{1,0:T(8,128)(2,1)S(1)} %get-tuple-element.63), channel_id=1, source_target_pairs={{0,128},{1,160},{32,129},{33,161},{128,256},{129,288},{160,257},{1... | collective-permute-start | bytes 393224 | tf_op jit(solution)/shard_map/ppermute | solution.py:390
  39.2 12.0 %collective-permute-start.1 = (bf16[512,128]{1,0:T(8,128)(2,1)S(1)}, bf16[512,128]{1,0:T(8,128)(2,1)}, u32[]{:S(2)}, u32[]{:S(2)}) collective-permute-start(bf16[512,128]{1,0:T(8,128)(2,1)S(1)} %get-tuple-element.64), channel_id=1, source_target_pairs={{0,0},{1,32},{32,1},{33,33},{128,128},{129,160},{160,129},{161,161... | collective-permute-start | bytes 393224 | tf_op jit(solution)/shard_map/ppermute | solution.py:390
  51.2 4.6 %collective-permute-start.5 = (f32[16,512]{1,0:T(8,128)S(1)}, f32[16,512]{1,0:T(8,128)S(1)}, u32[]{:S(2)}, u32[]{:S(2)}) collective-permute-start(f32[16,512]{1,0:T(8,128)S(1)} %stats.1), channel_id=1, source_target_pairs={{0,32},{32,0},{1,33},{33,1},{2,34},{34,2},{3,35},{35,3},{4,36},{36... | collective-permute-start | bytes 98312 | tf_op jit(solution)/shard_map/ppermute | solution.py:324
  61.0 42.6 %all-to-all-start.1 = ((bf16[16,128,256]{2,1,0:T(8,128)(2,1)}), bf16[16,128,256]{2,1,0:T(8,128)(2,1)S(1)}, u32[]{:S(2)}, u32[]{:S(2)}) async-start(bf16[16,128,256]{2,1,0:T(8,128)(2,1)} %get-tuple-element.41), calls=%async_computation.1 | async-start | bytes 2097152 | tf_op jit(solution)/shard_map/all_to_all | solution.py:410
  74.4 31.8 %collective-permute-start.10 = (bf16[4,512,128]{2,1,0:T(8,128)(2,1)S(1)}, bf16[4,512,128]{2,1,0:T(8,128)(2,1)S(1)}, u32[]{:S(2)}, u32[]{:S(2)}) collective-permute-start(bf16[4,512,128]{2,1,0:T(8,128)(2,1)S(1)} %pad_maximum_fusion.1.refs_0_), channel_id=1, source_target_pairs={{0,2},{2,0},{1,3},{3,1},{4,6},{6,4},{5,7},{7,5},{8,10},{10,8},{9,1... | collective-permute-start | bytes 1572872 | tf_op jit(solution)/shard_map/ppermute | solution.py:324
  77.1 7.6 %collective-permute-start.8 = (bf16[2,512,128]{2,1,0:T(8,128)(2,1)}, bf16[2,512,128]{2,1,0:T(8,128)(2,1)S(1)}, u32[]{:S(2)}, u32[]{:S(2)}) collective-permute-start(bf16[2,512,128]{2,1,0:T(8,128)(2,1)} %get-tuple-element.59), channel_id=1, source_target_pairs={{0,1},{1,0},{2,3},{3,2},{4,5},{5,4},{6,7},{7,6},{8,9},{9,8},{10,11... | collective-permute-start | bytes 786440 | tf_op jit(solution)/shard_map/ppermute | solution.py:324
  82.7 3.6 %collective-permute-start.7 = (bf16[2,512,128]{2,1,0:T(8,128)(2,1)}, bf16[2,512,128]{2,1,0:T(8,128)(2,1)S(1)}, u32[]{:S(2)}, u32[]{:S(2)}) collective-permute-start(bf16[2,512,128]{2,1,0:T(8,128)(2,1)} %get-tuple-element.60), channel_id=1, source_target_pairs={{0,1},{1,0},{2,3},{3,2},{4,5},{5,4},{6,7},{7,6},{8,9},{9,8},{10,11... | collective-permute-start | bytes 786440 | tf_op jit(solution)/shard_map/ppermute | solution.py:324
  84.8 19.5 %copy-start = (bf16[2,512,128]{2,1,0:T(8,128)(2,1)}, bf16[2,512,128]{2,1,0:T(8,128)(2,1)S(1)}, u32[]{:S(2)}) copy-start(bf16[2,512,128]{2,1,0:T(8,128)(2,1)S(1)} %collective-permute-done.8.refs_2_) | copy-start | bytes 786436
  86.4 17.9 %copy-start.2 = (bf16[2,512,128]{2,1,0:T(8,128)(2,1)}, bf16[2,512,128]{2,1,0:T(8,128)(2,1)S(1)}, u32[]{:S(2)}) copy-start(bf16[2,512,128]{2,1,0:T(8,128)(2,1)S(1)} %collective-permute-done.7.refs_1_) | copy-start | bytes 786436
  104.3 5.9 %collective-permute-start.9 = (bf16[128,256]{1,0:T(8,128)(2,1)S(1)}, bf16[128,256]{1,0:T(8,128)(2,1)S(1)}, u32[]{:S(2)}, u32[]{:S(2)}) collective-permute-start(bf16[128,256]{1,0:T(8,128)(2,1)S(1)} %get-tuple-element.45), channel_id=1, source_target_pairs={{0,64},{64,0},{1,65},{65,1},{2,66},{66,2},{3,67},{67,3},{4,68},{68... | collective-permute-start | bytes 196616 | tf_op jit(solution)/shard_map/ppermute | solution.py:324
  111.0 11.2 %copy-start.1 = (bf16[2,512,128]{2,1,0:T(8,128)(2,1)S(1)}, bf16[2,512,128]{2,1,0:T(8,128)(2,1)}, u32[]{:S(2)}) copy-start(bf16[2,512,128]{2,1,0:T(8,128)(2,1)} %copy-done) | copy-start | bytes 786436
  111.0 11.2 %copy-start.3 = (bf16[2,512,128]{2,1,0:T(8,128)(2,1)S(1)}, bf16[2,512,128]{2,1,0:T(8,128)(2,1)}, u32[]{:S(2)}) copy-start(bf16[2,512,128]{2,1,0:T(8,128)(2,1)} %copy-done.2) | copy-start | bytes 786436
  111.0 11.2 %all-to-all-start.2 = ((bf16[8,128,256]{2,1,0:T(8,128)(2,1)}), bf16[8,128,256]{2,1,0:T(8,128)(2,1)S(1)}, u32[]{:S(2)}, u32[]{:S(2)}) async-start(bf16[8,128,256]{2,1,0:T(8,128)(2,1)} %get-tuple-element.52), calls=%async_computation.2 | async-start | bytes 1048576 | tf_op jit(solution)/shard_map/all_to_all | solution.py:421
  114.6 5.8 %collective-permute-start.11 = (bf16[4,512,128]{2,1,0:T(8,128)(2,1)S(1)}, bf16[4,512,128]{2,1,0:T(8,128)(2,1)S(1)}, u32[]{:S(2)}, u32[]{:S(2)}) collective-permute-start(bf16[4,512,128]{2,1,0:T(8,128)(2,1)S(1)} %collective-permute-done.10.refs_3_), channel_id=1, source_target_pairs={{0,1},{1,0},{2,3},{3,2},{4,5},{5,4},{6,7},{7,6},{8,9},{9,8},{10,11... | collective-permute-start | bytes 1572872 | tf_op jit(solution)/shard_map/ppermute | solution.py:324
  124.3 20.2 %all-to-all-start.3 = ((bf16[16,64,256]{2,1,0:T(8,128)(2,1)}), bf16[16,64,256]{2,1,0:T(8,128)(2,1)S(1)}, u32[]{:S(2)}, u32[]{:S(2)}) async-start(bf16[16,64,256]{2,1,0:T(8,128)(2,1)} %weights.1), calls=%async_computation.3 | async-start | bytes 1048576 | tf_op jit(solution)/shard_map/all_to_all | solution.py:423
  127.9 20.8 %collective-permute-start.6 = (bf16[128,1024]{1,0:T(8,128)(2,1)S(1)}, bf16[128,1024]{1,0:T(8,128)(2,1)S(1)}, u32[]{:S(2)}, u32[]{:S(2)}) collective-permute-start(bf16[128,1024]{1,0:T(8,128)(2,1)S(1)} %get-tuple-element.38), channel_id=1, source_target_pairs={{0,32},{32,0},{1,33},{33,1},{2,34},{34,2},{3,35},{35,3},{4,36},{36... | collective-permute-start | bytes 786440 | tf_op jit(solution)/shard_map/ppermute | solution.py:324
  145.2 8.9 %all-to-all-start.4 = ((f32[4,64,256]{2,1,0:T(8,128)}), f32[4,64,256]{2,1,0:T(8,128)S(1)}, u32[]{:S(2)}, u32[]{:S(2)}) async-start(f32[4,64,256]{2,1,0:T(8,128)} %sum_rows.1), calls=%async_computation.4 | async-start | bytes 524288 | tf_op jit(solution)/shard_map/all_to_all | solution.py:425

commit v7 on v6

--- a/solution.py
+++ b/solution.py
@@ -12,8 +12,8 @@
 NEG = -1e30
 SCALE = HEAD ** (-0.5)
 LOG2E = 1.4426950408889634
-VMEM_LIMIT = 24 * 1024 * 1024
-SMALL_LIMIT = 12 * 1024 * 1024
+VMEM_LIMIT = 16 * 1024 * 1024
+SMALL_LIMIT = 8 * 1024 * 1024
 
 
 def nt(left, right):

time: 157 us -> 156 us (level); the launches traced: 155 us -> 156 us
  Pallas kernels: 12.1 us -> 16.4 us
  waiting for transfers between devices: 53.8 us -> 50.2 us
    all_to_all x1, starting transfers between devices: 13.4 us -> 7.19 us  [shards(): parts = lax.all_to_all(dkv, 'z', 0, 0, tiled=True)]
    all_to_all x1, starting transfers between devices: 3.62 us -> 8.24 us  [shards(): all_grads = lax.all_to_all(copies, ('dp', 'yb'), 0, 0, tiled=True)]
    all_to_all x1, waiting for transfers between devices: 17.2 us -> 14.2 us  [shards(): parts = lax.all_to_all(dkv, 'z', 0, 0, tiled=True)]
    pallas_call x1, Pallas kernels: 5.1 us -> 7.73 us  [grad_call(): pl.pallas_call(grad_kernel, out_shape=(jax.ShapeDtypeStruct((height, widt...]
    pallas_call x1, Pallas kernels: 2.58 us -> 4.3 us  [stats_call(): pl.pallas_call(stats_kernel, out_shape=jax.ShapeDtypeStruct((16, rows), j...]
  transfers between devices with their start and end apart: 17 -> 17, of which waited for: 11 -> 9; matrix products, arithmetic and copies ran while one was open for 5% -> 5% of each run, Pallas kernels for 3% -> 4%
where the time goes in v7:
time: 156 us
  starting transfers between devices  74 us (47%)
  waiting for transfers between devices  50.2 us (32%)
  Pallas kernels  16.4 us (11%)
  local copies, waits for them, and re-layouts  7.51 us (5%)
  other arithmetic  5.03 us (3%)
  between operations  2.35 us (2%)
    ppermute x8, starting transfers between devices, swapped(): return lax.ppermute(array, axis, [(0, 1), (1, 0)])  25.1 us
    all_to_all x1, waiting for transfers between devices, shards(): pieces = lax.all_to_all(blocks, group, 0, 0, tiled=True)  14.6 us
    all_to_all x1, waiting for transfers between devices, shards(): parts = lax.all_to_all(dkv, 'z', 0, 0, tiled=True)  14.2 us
    ppermute x4, starting transfers between devices, shards(): lax.ppermute(slab, ('dp', 'yb', 'core'), [(d * 4 + b * 2 + c, (d + by) %...  13.9 us
    all_to_all x1, starting transfers between devices, shards(): lax.all_to_all(jnp.broadcast_to(pair[None], (group_size,) + pair.shape),...  12.3 us
    ppermute x8, waiting for transfers between devices, swapped(): return lax.ppermute(array, axis, [(0, 1), (1, 0)])  8.97 us
    all_to_all x1, starting transfers between devices, shards(): all_grads = lax.all_to_all(copies, ('dp', 'yb'), 0, 0, tiled=True)  8.24 us
    pallas_call x1, Pallas kernels, grad_call(): pl.pallas_call(grad_kernel, out_shape=(jax.ShapeDtypeStruct((height, widt...  7.73 us
  transfers between devices with their start and end apart: 17, of which 9 were waited for; matrix products, arithmetic and copies ran while one was open for 5% of the time, Pallas kernels for 4%

profile of v7, /device:TPU:1, one launch (start us, length us, event | category | flops | bytes accessed | tf_op | source)
XLA Modules:
  0.0 155.5 jit_solution(5344046566069007724)
XLA Ops:
  0.6 1.0 copy.41
  1.6 0.0 copy-start.5
  1.7 0.9 copy-done.5
  2.7 0.0 copy-start.6
  2.7 0.0 copy-start.7
  2.7 0.1 pad_maximum_fusion.own
  2.8 4.0 %collective-permute-start = (bf16[2,1024,128]{2,1,0:T(8,128)(2,1)S(1)}, bf16[2,1024,128]{2,1,0:T(8,128)(2,1)S(1)}, u32[]{:S(2)}, u32[]{:S(2)}) collective-permute-start(bf16[2,1024,128]{2,1,0:T(8,128)(2,1)S(1)} %pad_maximum_fusion.own), channel_id=1, source_target_pairs={{0,32},{32,0},{1,33},{33,1},{2,34},{34,2},{3,35},{35,3},{4,36},{36... | collective-permute-start | bytes 1572872 | tf_op jit(solution)/shard_map/ppermute | solution.py:324
  6.9 1.1 broadcast_in_dim.43
  7.9 12.3 %all-to-all-start = ((bf16[16,128,256]{2,1,0:T(8,128)(2,1)}), bf16[16,128,256]{2,1,0:T(8,128)(2,1)S(1)}, u32[]{:S(2)}, u32[]{:S(2)}) async-start(bf16[16,128,256]{2,1,0:T(8,128)(2,1)} %broadcast_in_dim.43), calls=%async_computation | async-start | bytes 2097152 | tf_op jit(solution)/shard_map/all_to_all | solution.py:369
  20.3 0.6 copy-done.8
  20.9 0.1 reshape.195
  21.0 0.6 fusion.2
  21.7 0.1 select_n.68
  21.8 0.1 copy.34
  21.9 0.1 lt.41
  21.9 0.1 broadcast_in_dim_reshape.2
  23.4 0.6 copy-done.9
  24.0 0.2 reduce-window.8
  24.2 1.4 broadcast_multiply_fusion
  25.5 0.1 iota_add_fusion
  25.6 0.1 select_reduce_fusion
  25.7 0.1 iota_add_fusion.1
  25.8 0.1 tile.10.qmeta
  25.9 0.2 select_reduce_fusion.1
  26.1 0.2 convert_reduce_fusion.2
  26.3 0.1 add_bitcast_fusion
  26.4 0.2 convert_reduce_fusion
  26.6 0.3 copy.39
  27.0 0.7 dynamic-slice_bitcast_fusion
  27.7 5.4 %collective-permute-start.4 = (bf16[512,128]{1,0:T(8,128)(2,1)}, bf16[512,128]{1,0:T(8,128)(2,1)S(1)}, u32[]{:S(2)}, u32[]{:S(2)}) collective-permute-start(bf16[512,128]{1,0:T(8,128)(2,1)} %get-tuple-element.61), channel_id=1, source_target_pairs={{0,384},{1,416},{32,385},{33,417},{128,0},{129,32},{160,1},{161,33... | collective-permute-start | bytes 393224 | tf_op jit(solution)/shard_map/ppermute | solution.py:390
  33.0 2.6 %collective-permute-start.3 = (bf16[512,128]{1,0:T(8,128)(2,1)S(1)}, bf16[512,128]{1,0:T(8,128)(2,1)S(1)}, u32[]{:S(2)}, u32[]{:S(2)}) collective-permute-start(bf16[512,128]{1,0:T(8,128)(2,1)S(1)} %get-tuple-element.62), channel_id=1, source_target_pairs={{0,256},{1,288},{32,257},{33,289},{128,384},{129,416},{160,385},{1... | collective-permute-start | bytes 393224 | tf_op jit(solution)/shard_map/ppermute | solution.py:390
  35.7 3.5 %collective-permute-start.2 = (bf16[512,128]{1,0:T(8,128)(2,1)S(1)}, bf16[512,128]{1,0:T(8,128)(2,1)S(1)}, u32[]{:S(2)}, u32[]{:S(2)}) collective-permute-start(bf16[512,128]{1,0:T(8,128)(2,1)S(1)} %get-tuple-element.63), channel_id=1, source_target_pairs={{0,128},{1,160},{32,129},{33,161},{128,256},{129,288},{160,257},{1... | collective-permute-start | bytes 393224 | tf_op jit(solution)/shard_map/ppermute | solution.py:390
  39.2 2.4 %collective-permute-start.1 = (bf16[512,128]{1,0:T(8,128)(2,1)S(1)}, bf16[512,128]{1,0:T(8,128)(2,1)}, u32[]{:S(2)}, u32[]{:S(2)}) collective-permute-start(bf16[512,128]{1,0:T(8,128)(2,1)S(1)} %get-tuple-element.64), channel_id=1, source_target_pairs={{0,0},{1,32},{32,1},{33,33},{128,128},{129,160},{160,129},{161,161... | collective-permute-start | bytes 393224 | tf_op jit(solution)/shard_map/ppermute | solution.py:390
  41.6 6.2 %all-to-all-done.kv = bf16[16,128,256]{2,1,0:T(8,128)(2,1)S(1)} async-done(((bf16[16,128,256]{2,1,0:T(8,128)(2,1)}), bf16[16,128,256]{2,1,0:T(8,128)(2,1)S(1)}, u32[]{:S(2)}, u32[]{:S(2)}) %all-to-all-start) | async-done | bytes 1048608 | tf_op jit(solution)/shard_map/all_to_all | solution.py:369
  47.8 4.3 %stats.1 = f32[16,512]{1,0:T(8,128)S(1)} custom-call(s32[3,32]{1,0:T(4,128)S(1)} %pad_add_fusion.1.meta, s32[16,512]{1,0:T(8,128)S(1)} %tile.10.qmeta, bf16[2,1024,128]{2,1,0:T(8,128)(2,1)S(1)} %pad_maximum_fusion.own, bf16[2,1024,128]{2,1,0:T(8,128)(2,1)S(1)} %collective-permute-done.other, bf16[16,128,256]{2,1,0:T(8,128)(2,1)S(1)} %all-to-all-done.kv), custom_call_target="tpu_custom_call" | custom-call | flops 2000000000 | bytes 4000000 | tf_op jit(solution)/shard_map/stats/pallas_call | solution.py:192
  52.1 1.9 %collective-permute-start.5 = (f32[16,512]{1,0:T(8,128)S(1)}, f32[16,512]{1,0:T(8,128)S(1)}, u32[]{:S(2)}, u32[]{:S(2)}) collective-permute-start(f32[16,512]{1,0:T(8,128)S(1)} %stats.1), channel_id=1, source_target_pairs={{0,32},{32,0},{1,33},{33,1},{2,34},{34,2},{3,35},{35,3},{4,36},{36... | collective-permute-start | bytes 98312 | tf_op jit(solution)/shard_map/ppermute | solution.py:324
  54.0 1.0 pad_maximum_fusion.1.refs_0_
  55.0 1.8 %collective-permute-done.5.far = f32[16,512]{1,0:T(8,128)S(1)} collective-permute-done((f32[16,512]{1,0:T(8,128)S(1)}, f32[16,512]{1,0:T(8,128)S(1)}, u32[]{:S(2)}, u32[]{:S(2)}) %collective-permute-start.5) | collective-permute-done | bytes 32800 | tf_op jit(solution)/shard_map/ppermute | solution.py:324
  56.8 7.7 %grads.1 = (f32[128,1024]{1,0:T(8,128)S(1)}, bf16[128,1024]{1,0:T(8,128)(2,1)S(1)}, bf16[16,128,256]{2,1,0:T(8,128)(2,1)}) custom-call(s32[3,32]{1,0:T(4,128)S(1)} %pad_add_fusion.1.meta, s32[16,512]{1,0:T(8,128)S(1)} %tile.10.qmeta, bf16[2,1024,128]{2,1,0:T(8,128)(2,1)S(1)} %pad_maximum_fusion.own, bf16[2,1024,128]{2,1,0:T(8,128)(2,1)S(1)} %collective-permute-done.other, ...), custom_call_target="tpu_custom_call" | custom-call | flops 5000000000 | bytes 6000000 | tf_op jit(solution)/shard_map/grads/pallas_call | solution.py:208
  64.5 7.2 %all-to-all-start.1 = ((bf16[16,128,256]{2,1,0:T(8,128)(2,1)}), bf16[16,128,256]{2,1,0:T(8,128)(2,1)S(1)}, u32[]{:S(2)}, u32[]{:S(2)}) async-start(bf16[16,128,256]{2,1,0:T(8,128)(2,1)} %get-tuple-element.41), calls=%async_computation.1 | async-start | bytes 2097152 | tf_op jit(solution)/shard_map/all_to_all | solution.py:410
  71.7 3.2 %collective-permute-start.10 = (bf16[4,512,128]{2,1,0:T(8,128)(2,1)S(1)}, bf16[4,512,128]{2,1,0:T(8,128)(2,1)S(1)}, u32[]{:S(2)}, u32[]{:S(2)}) collective-permute-start(bf16[4,512,128]{2,1,0:T(8,128)(2,1)S(1)} %pad_maximum_fusion.1.refs_0_), channel_id=1, source_target_pairs={{0,2},{2,0},{1,3},{3,1},{4,6},{6,4},{5,7},{7,5},{8,10},{10,8},{9,1... | collective-permute-start | bytes 1572872 | tf_op jit(solution)/shard_map/ppermute | solution.py:324
  74.9 0.8 fusion.4
  75.7 5.4 %collective-permute-start.8 = (bf16[2,512,128]{2,1,0:T(8,128)(2,1)}, bf16[2,512,128]{2,1,0:T(8,128)(2,1)S(1)}, u32[]{:S(2)}, u32[]{:S(2)}) collective-permute-start(bf16[2,512,128]{2,1,0:T(8,128)(2,1)} %get-tuple-element.59), channel_id=1, source_target_pairs={{0,1},{1,0},{2,3},{3,2},{4,5},{5,4},{6,7},{7,6},{8,9},{9,8},{10,11... | collective-permute-start | bytes 786440 | tf_op jit(solution)/shard_map/ppermute | solution.py:324
  81.2 1.9 %collective-permute-start.7 = (bf16[2,512,128]{2,1,0:T(8,128)(2,1)}, bf16[2,512,128]{2,1,0:T(8,128)(2,1)S(1)}, u32[]{:S(2)}, u32[]{:S(2)}) collective-permute-start(bf16[2,512,128]{2,1,0:T(8,128)(2,1)} %get-tuple-element.60), channel_id=1, source_target_pairs={{0,1},{1,0},{2,3},{3,2},{4,5},{5,4},{6,7},{7,6},{8,9},{9,8},{10,11... | collective-permute-start | bytes 786440 | tf_op jit(solution)/shard_map/ppermute | solution.py:324
  83.1 0.1 pad_add_fusion.4.place
  83.2 1.6 %collective-permute-done.7.refs_1_ = bf16[2,512,128]{2,1,0:T(8,128)(2,1)S(1)} collective-permute-done((bf16[2,512,128]{2,1,0:T(8,128)(2,1)}, bf16[2,512,128]{2,1,0:T(8,128)(2,1)S(1)}, u32[]{:S(2)}, u32[]{:S(2)}) %collective-permute-start.7) | collective-permute-done | bytes 262176 | tf_op jit(solution)/shard_map/ppermute | solution.py:324
  84.8 14.2 %all-to-all-done.1.parts = bf16[16,128,256]{2,1,0:T(8,128)(2,1)S(1)} async-done(((bf16[16,128,256]{2,1,0:T(8,128)(2,1)}), bf16[16,128,256]{2,1,0:T(8,128)(2,1)S(1)}, u32[]{:S(2)}, u32[]{:S(2)}) %all-to-all-start.1) | async-done | bytes 1048608 | tf_op jit(solution)/shard_map/all_to_all | solution.py:410
  99.0 0.7 first_sum.1
  99.7 1.9 %collective-permute-start.9 = (bf16[128,256]{1,0:T(8,128)(2,1)S(1)}, bf16[128,256]{1,0:T(8,128)(2,1)S(1)}, u32[]{:S(2)}, u32[]{:S(2)}) collective-permute-start(bf16[128,256]{1,0:T(8,128)(2,1)S(1)} %get-tuple-element.45), channel_id=1, source_target_pairs={{0,64},{64,0},{1,65},{65,1},{2,66},{66,2},{3,67},{67,3},{4,68},{68... | collective-permute-start | bytes 196616 | tf_op jit(solution)/shard_map/ppermute | solution.py:324
  101.6 4.1 %collective-permute-done.9.got = bf16[128,256]{1,0:T(8,128)(2,1)S(1)} collective-permute-done((bf16[128,256]{1,0:T(8,128)(2,1)S(1)}, bf16[128,256]{1,0:T(8,128)(2,1)S(1)}, u32[]{:S(2)}, u32[]{:S(2)}) %collective-permute-start.9) | collective-permute-done | bytes 65568 | tf_op jit(solution)/shard_map/ppermute | solution.py:324
  105.7 0.8 second_sum.1
  106.5 8.2 %all-to-all-start.2 = ((bf16[8,128,256]{2,1,0:T(8,128)(2,1)}), bf16[8,128,256]{2,1,0:T(8,128)(2,1)S(1)}, u32[]{:S(2)}, u32[]{:S(2)}) async-start(bf16[8,128,256]{2,1,0:T(8,128)(2,1)} %get-tuple-element.52), calls=%async_computation.2 | async-start | bytes 1048576 | tf_op jit(solution)/shard_map/all_to_all | solution.py:421
  114.8 4.5 %collective-permute-start.11 = (bf16[4,512,128]{2,1,0:T(8,128)(2,1)S(1)}, bf16[4,512,128]{2,1,0:T(8,128)(2,1)S(1)}, u32[]{:S(2)}, u32[]{:S(2)}) collective-permute-start(bf16[4,512,128]{2,1,0:T(8,128)(2,1)S(1)} %collective-permute-done.10.refs_3_), channel_id=1, source_target_pairs={{0,1},{1,0},{2,3},{3,2},{4,5},{5,4},{6,7},{7,6},{8,9},{9,8},{10,11... | collective-permute-start | bytes 1572872 | tf_op jit(solution)/shard_map/ppermute | solution.py:324
  119.3 1.5 collective-permute-done.11.refs_4_
  120.8 1.6 %all-to-all-done.2.refs_5_ = bf16[8,128,256]{2,1,0:T(8,128)(2,1)S(1)} async-done(((bf16[8,128,256]{2,1,0:T(8,128)(2,1)}), bf16[8,128,256]{2,1,0:T(8,128)(2,1)S(1)}, u32[]{:S(2)}, u32[]{:S(2)}) %all-to-all-start.2) | async-done | bytes 524320 | tf_op jit(solution)/shard_map/all_to_all | solution.py:421
  122.4 2.1 %weights.1 = bf16[16,64,256]{2,1,0:T(8,128)(2,1)} custom-call(s32[4]{0:T(128)S(1)} %pad_add_fusion.4.place, bf16[4,512,128]{2,1,0:T(8,128)(2,1)S(1)} %pad_maximum_fusion.1.refs_0_, bf16[2,512,128]{2,1,0:T(8,128)(2,1)S(1)} %copy-done.3, bf16[2,512,128]{2,1,0:T(8,128)(2,1)S(1)} %copy-done.1, bf16[4,512,128]{2,1,0:T(8,128)(2,1)S(1)} %collective-permute-done.10.refs_3_, ...), custom_call_target="tpu_custom_call" | custom-call | flops 1000000000 | bytes 4000000 | tf_op jit(solution)/shard_map/weights/pallas_call | solution.py:312
  124.5 3.9 %all-to-all-start.3 = ((bf16[16,64,256]{2,1,0:T(8,128)(2,1)}), bf16[16,64,256]{2,1,0:T(8,128)(2,1)S(1)}, u32[]{:S(2)}, u32[]{:S(2)}) async-start(bf16[16,64,256]{2,1,0:T(8,128)(2,1)} %weights.1), calls=%async_computation.3 | async-start | bytes 1048576 | tf_op jit(solution)/shard_map/all_to_all | solution.py:423
  128.4 2.2 %collective-permute-start.6 = (bf16[128,1024]{1,0:T(8,128)(2,1)S(1)}, bf16[128,1024]{1,0:T(8,128)(2,1)S(1)}, u32[]{:S(2)}, u32[]{:S(2)}) collective-permute-start(bf16[128,1024]{1,0:T(8,128)(2,1)S(1)} %get-tuple-element.38), channel_id=1, source_target_pairs={{0,32},{32,0},{1,33},{33,1},{2,34},{34,2},{3,35},{35,3},{4,36},{36... | collective-permute-start | bytes 786440 | tf_op jit(solution)/shard_map/ppermute | solution.py:324
  130.5 14.6 %all-to-all-done.3.parts = bf16[16,64,256]{2,1,0:T(8,128)(2,1)S(1)} async-done(((bf16[16,64,256]{2,1,0:T(8,128)(2,1)}), bf16[16,64,256]{2,1,0:T(8,128)(2,1)S(1)}, u32[]{:S(2)}, u32[]{:S(2)}) %all-to-all-start.3) | async-done | bytes 524320 | tf_op jit(solution)/shard_map/all_to_all | solution.py:423
  145.1 0.8 sum_rows.1
  145.9 3.4 %all-to-all-start.4 = ((f32[4,64,256]{2,1,0:T(8,128)}), f32[4,64,256]{2,1,0:T(8,128)S(1)}, u32[]{:S(2)}, u32[]{:S(2)}) async-start(f32[4,64,256]{2,1,0:T(8,128)} %sum_rows.1), calls=%async_computation.4 | async-start | bytes 524288 | tf_op jit(solution)/shard_map/all_to_all | solution.py:425
  149.3 0.8 fusion
  150.1 4.7 %all-to-all-done.4 = f32[4,64,256]{2,1,0:T(8,128)S(1)} async-done(((f32[4,64,256]{2,1,0:T(8,128)}), f32[4,64,256]{2,1,0:T(8,128)S(1)}, u32[]{:S(2)}, u32[]{:S(2)}) %all-to-all-start.4) | async-done | bytes 262176 | tf_op jit(solution)/shard_map/all_to_all | solution.py:425
  154.8 0.7 fusion.5
  (38 shorter events, 0.3 us)
Async XLA Ops:
  1.6 1.0 copy-start.5
  2.7 4.1 %copy-start.6 = (bf16[1,128,128]{2,1,0:T(8,128)(2,1)S(1)}, bf16[1,128,128]{2,1,0:T(8,128)(2,1)}, u32[]{:S(2)}) copy-start(bf16[1,128,128]{2,1,0:T(8,128)(2,1)} %param.9) | copy-start | bytes 98308
  2.7 4.1 %copy-start.7 = (bf16[1,128,128]{2,1,0:T(8,128)(2,1)S(1)}, bf16[1,128,128]{2,1,0:T(8,128)(2,1)}, u32[]{:S(2)}) copy-start(bf16[1,128,128]{2,1,0:T(8,128)(2,1)} %param.8) | copy-start | bytes 98308
  2.8 23.8 %collective-permute-start = (bf16[2,1024,128]{2,1,0:T(8,128)(2,1)S(1)}, bf16[2,1024,128]{2,1,0:T(8,128)(2,1)S(1)}, u32[]{:S(2)}, u32[]{:S(2)}) collective-permute-start(bf16[2,1024,128]{2,1,0:T(8,128)(2,1)S(1)} %pad_maximum_fusion.own), channel_id=1, source_target_pairs={{0,32},{32,0},{1,33},{33,1},{2,34},{34,2},{3,35},{35,3},{4,36},{36... | collective-permute-start | bytes 1572872 | tf_op jit(solution)/shard_map/ppermute | solution.py:324
  7.9 18.7 %copy-start.4 = (bf16[1,128,2048]{2,1,0:T(8,128)(2,1)S(1)}, bf16[1,128,2048]{2,1,0:T(8,128)(2,1)}, u32[]{:S(2)}) copy-start(bf16[1,128,2048]{2,1,0:T(8,128)(2,1)} %param.11) | copy-start | bytes 1572868
  7.9 39.8 %all-to-all-start = ((bf16[16,128,256]{2,1,0:T(8,128)(2,1)}), bf16[16,128,256]{2,1,0:T(8,128)(2,1)S(1)}, u32[]{:S(2)}, u32[]{:S(2)}) async-start(bf16[16,128,256]{2,1,0:T(8,128)(2,1)} %broadcast_in_dim.43), calls=%async_computation | async-start | bytes 2097152 | tf_op jit(solution)/shard_map/all_to_all | solution.py:369
  20.3 0.7 copy-start.8
  23.3 0.7 copy-start.9
  27.7 24.4 %collective-permute-start.4 = (bf16[512,128]{1,0:T(8,128)(2,1)}, bf16[512,128]{1,0:T(8,128)(2,1)S(1)}, u32[]{:S(2)}, u32[]{:S(2)}) collective-permute-start(bf16[512,128]{1,0:T(8,128)(2,1)} %get-tuple-element.61), channel_id=1, source_target_pairs={{0,384},{1,416},{32,385},{33,417},{128,0},{129,32},{160,1},{161,33... | collective-permute-start | bytes 393224 | tf_op jit(solution)/shard_map/ppermute | solution.py:390
  33.0 19.0 %collective-permute-start.3 = (bf16[512,128]{1,0:T(8,128)(2,1)S(1)}, bf16[512,128]{1,0:T(8,128)(2,1)S(1)}, u32[]{:S(2)}, u32[]{:S(2)}) collective-permute-start(bf16[512,128]{1,0:T(8,128)(2,1)S(1)} %get-tuple-element.62), channel_id=1, source_target_pairs={{0,256},{1,288},{32,257},{33,289},{128,384},{129,416},{160,385},{1... | collective-permute-start | bytes 393224 | tf_op jit(solution)/shard_map/ppermute | solution.py:390
  35.7 16.4 %collective-permute-start.2 = (bf16[512,128]{1,0:T(8,128)(2,1)S(1)}, bf16[512,128]{1,0:T(8,128)(2,1)S(1)}, u32[]{:S(2)}, u32[]{:S(2)}) collective-permute-start(bf16[512,128]{1,0:T(8,128)(2,1)S(1)} %get-tuple-element.63), channel_id=1, source_target_pairs={{0,128},{1,160},{32,129},{33,161},{128,256},{129,288},{160,257},{1... | collective-permute-start | bytes 393224 | tf_op jit(solution)/shard_map/ppermute | solution.py:390
  39.2 12.9 %collective-permute-start.1 = (bf16[512,128]{1,0:T(8,128)(2,1)S(1)}, bf16[512,128]{1,0:T(8,128)(2,1)}, u32[]{:S(2)}, u32[]{:S(2)}) collective-permute-start(bf16[512,128]{1,0:T(8,128)(2,1)S(1)} %get-tuple-element.64), channel_id=1, source_target_pairs={{0,0},{1,32},{32,1},{33,33},{128,128},{129,160},{160,129},{161,161... | collective-permute-start | bytes 393224 | tf_op jit(solution)/shard_map/ppermute | solution.py:390
  52.1 4.7 %collective-permute-start.5 = (f32[16,512]{1,0:T(8,128)S(1)}, f32[16,512]{1,0:T(8,128)S(1)}, u32[]{:S(2)}, u32[]{:S(2)}) collective-permute-start(f32[16,512]{1,0:T(8,128)S(1)} %stats.1), channel_id=1, source_target_pairs={{0,32},{32,0},{1,33},{33,1},{2,34},{34,2},{3,35},{35,3},{4,36},{36... | collective-permute-start | bytes 98312 | tf_op jit(solution)/shard_map/ppermute | solution.py:324
  64.5 34.5 %all-to-all-start.1 = ((bf16[16,128,256]{2,1,0:T(8,128)(2,1)}), bf16[16,128,256]{2,1,0:T(8,128)(2,1)S(1)}, u32[]{:S(2)}, u32[]{:S(2)}) async-start(bf16[16,128,256]{2,1,0:T(8,128)(2,1)} %get-tuple-element.41), calls=%async_computation.1 | async-start | bytes 2097152 | tf_op jit(solution)/shard_map/all_to_all | solution.py:410
  71.7 29.9 %collective-permute-start.10 = (bf16[4,512,128]{2,1,0:T(8,128)(2,1)S(1)}, bf16[4,512,128]{2,1,0:T(8,128)(2,1)S(1)}, u32[]{:S(2)}, u32[]{:S(2)}) collective-permute-start(bf16[4,512,128]{2,1,0:T(8,128)(2,1)S(1)} %pad_maximum_fusion.1.refs_0_), channel_id=1, source_target_pairs={{0,2},{2,0},{1,3},{3,1},{4,6},{6,4},{5,7},{7,5},{8,10},{10,8},{9,1... | collective-permute-start | bytes 1572872 | tf_op jit(solution)/shard_map/ppermute | solution.py:324
  75.7 7.4 %collective-permute-start.8 = (bf16[2,512,128]{2,1,0:T(8,128)(2,1)}, bf16[2,512,128]{2,1,0:T(8,128)(2,1)S(1)}, u32[]{:S(2)}, u32[]{:S(2)}) collective-permute-start(bf16[2,512,128]{2,1,0:T(8,128)(2,1)} %get-tuple-element.59), channel_id=1, source_target_pairs={{0,1},{1,0},{2,3},{3,2},{4,5},{5,4},{6,7},{7,6},{8,9},{9,8},{10,11... | collective-permute-start | bytes 786440 | tf_op jit(solution)/shard_map/ppermute | solution.py:324
  81.2 3.6 %collective-permute-start.7 = (bf16[2,512,128]{2,1,0:T(8,128)(2,1)}, bf16[2,512,128]{2,1,0:T(8,128)(2,1)S(1)}, u32[]{:S(2)}, u32[]{:S(2)}) collective-permute-start(bf16[2,512,128]{2,1,0:T(8,128)(2,1)} %get-tuple-element.60), channel_id=1, source_target_pairs={{0,1},{1,0},{2,3},{3,2},{4,5},{5,4},{6,7},{7,6},{8,9},{9,8},{10,11... | collective-permute-start | bytes 786440 | tf_op jit(solution)/shard_map/ppermute | solution.py:324
  83.2 16.5 %copy-start = (bf16[2,512,128]{2,1,0:T(8,128)(2,1)}, bf16[2,512,128]{2,1,0:T(8,128)(2,1)S(1)}, u32[]{:S(2)}) copy-start(bf16[2,512,128]{2,1,0:T(8,128)(2,1)S(1)} %collective-permute-done.8.refs_2_) | copy-start | bytes 786436
  84.8 14.9 %copy-start.2 = (bf16[2,512,128]{2,1,0:T(8,128)(2,1)}, bf16[2,512,128]{2,1,0:T(8,128)(2,1)S(1)}, u32[]{:S(2)}) copy-start(bf16[2,512,128]{2,1,0:T(8,128)(2,1)S(1)} %collective-permute-done.7.refs_1_) | copy-start | bytes 786436
  99.7 6.0 %collective-permute-start.9 = (bf16[128,256]{1,0:T(8,128)(2,1)S(1)}, bf16[128,256]{1,0:T(8,128)(2,1)S(1)}, u32[]{:S(2)}, u32[]{:S(2)}) collective-permute-start(bf16[128,256]{1,0:T(8,128)(2,1)S(1)} %get-tuple-element.45), channel_id=1, source_target_pairs={{0,64},{64,0},{1,65},{65,1},{2,66},{66,2},{3,67},{67,3},{4,68},{68... | collective-permute-start | bytes 196616 | tf_op jit(solution)/shard_map/ppermute | solution.py:324
  106.5 15.9 %copy-start.1 = (bf16[2,512,128]{2,1,0:T(8,128)(2,1)S(1)}, bf16[2,512,128]{2,1,0:T(8,128)(2,1)}, u32[]{:S(2)}) copy-start(bf16[2,512,128]{2,1,0:T(8,128)(2,1)} %copy-done) | copy-start | bytes 786436
  106.5 15.9 %copy-start.3 = (bf16[2,512,128]{2,1,0:T(8,128)(2,1)S(1)}, bf16[2,512,128]{2,1,0:T(8,128)(2,1)}, u32[]{:S(2)}) copy-start(bf16[2,512,128]{2,1,0:T(8,128)(2,1)} %copy-done.2) | copy-start | bytes 786436
  106.5 15.8 %all-to-all-start.2 = ((bf16[8,128,256]{2,1,0:T(8,128)(2,1)}), bf16[8,128,256]{2,1,0:T(8,128)(2,1)S(1)}, u32[]{:S(2)}, u32[]{:S(2)}) async-start(bf16[8,128,256]{2,1,0:T(8,128)(2,1)} %get-tuple-element.52), calls=%async_computation.2 | async-start | bytes 1048576 | tf_op jit(solution)/shard_map/all_to_all | solution.py:421
  114.8 6.0 %collective-permute-start.11 = (bf16[4,512,128]{2,1,0:T(8,128)(2,1)S(1)}, bf16[4,512,128]{2,1,0:T(8,128)(2,1)S(1)}, u32[]{:S(2)}, u32[]{:S(2)}) collective-permute-start(bf16[4,512,128]{2,1,0:T(8,128)(2,1)S(1)} %collective-permute-done.10.refs_3_), channel_id=1, source_target_pairs={{0,1},{1,0},{2,3},{3,2},{4,5},{5,4},{6,7},{7,6},{8,9},{9,8},{10,11... | collective-permute-start | bytes 1572872 | tf_op jit(solution)/shard_map/ppermute | solution.py:324
  124.5 20.6 %all-to-all-start.3 = ((bf16[16,64,256]{2,1,0:T(8,128)(2,1)}), bf16[16,64,256]{2,1,0:T(8,128)(2,1)S(1)}, u32[]{:S(2)}, u32[]{:S(2)}) async-start(bf16[16,64,256]{2,1,0:T(8,128)(2,1)} %weights.1), calls=%async_computation.3 | async-start | bytes 1048576 | tf_op jit(solution)/shard_map/all_to_all | solution.py:423
  128.4 20.9 %collective-permute-start.6 = (bf16[128,1024]{1,0:T(8,128)(2,1)S(1)}, bf16[128,1024]{1,0:T(8,128)(2,1)S(1)}, u32[]{:S(2)}, u32[]{:S(2)}) collective-permute-start(bf16[128,1024]{1,0:T(8,128)(2,1)S(1)} %get-tuple-element.38), channel_id=1, source_target_pairs={{0,32},{32,0},{1,33},{33,1},{2,34},{34,2},{3,35},{35,3},{4,36},{36... | collective-permute-start | bytes 786440 | tf_op jit(solution)/shard_map/ppermute | solution.py:324
  145.9 8.9 %all-to-all-start.4 = ((f32[4,64,256]{2,1,0:T(8,128)}), f32[4,64,256]{2,1,0:T(8,128)S(1)}, u32[]{:S(2)}, u32[]{:S(2)}) async-start(f32[4,64,256]{2,1,0:T(8,128)} %sum_rows.1), calls=%async_computation.4 | async-start | bytes 524288 | tf_op jit(solution)/shard_map/all_to_all | solution.py:425
